TPU v7x, 32 devices: a whole 2x2x4 slice. The times are simulated.
32 devices in a mesh: ctx: 16 (over z, y, core), tp: 2 (over x).
Axes of the slice: x: 2, y: 2, z: 4, core: 2. Of those that a mesh axis runs over, the one named last changes fastest.
Arguments:
- queries: bfloat16 [4096, 2048], P('ctx', 'tp'), may hold values from -5 to 5
- keys: bfloat16 [4096, 256], P('ctx', 'tp'), may hold values from -5 to 5
- values: bfloat16 [4096, 256], P('ctx', 'tp'), may hold values from -6 to 6
- out_weight: bfloat16 [2048, 4096], P('tp'), may hold values from -0.125 to 0.125
- cotangent: bfloat16 [4096, 4096], P('ctx', 'tp'), may hold values from -6 to 6
- doc_lengths: int32 [8], replicated, may hold values from 1 to 2048, 4096 in all
Outputs:
- mixed_out: bfloat16 [4096, 4096], P('ctx', 'tp')
- query_grad: bfloat16 [4096, 2048], P('ctx', 'tp')
- keys_gradient: bfloat16 [4096, 256], P('ctx', 'tp')
- values_gradient: bfloat16 [4096, 256], P('ctx', 'tp')
Inputs may be any that keep to these rules, and one draw needn't show every extreme that they name: `doc_lengths`: document lengths in order along the packed sequence; they sum to 4096 and the longest is exactly 2048.
All inputs are finite; a program needn't handle non-finite values.
Results may differ from a plain program's by a relative error of at most 0.022.
Values may be sent and summed in bfloat16 or wider, within the bound.
No kernel may reach another device: no remote copies, remote signals or barrier semaphores. Data moves between devices by JAX's collectives and lax.ppermute only.
A program may use at most 192 MiB of HBM per device.

v0:
```python
from functools import partial
import math

import jax
import jax.numpy as jnp
from jax import lax
from jax.experimental import pallas as pl
from jax.experimental.pallas import tpu as pltpu
from jax.sharding import PartitionSpec as P

HEAD_WIDTH = 128
REACH = 8
GROUP = 4
BACK = REACH // GROUP
PLANES = BACK + 1
WINDOW = PLANES * GROUP
LOG2_E = math.log2(math.e)
MASKED = -1e30
NT = (((1,), (1,)), ((), ()))


def shifted(block, distance):
    size = lax.axis_size("ctx")
    route = [(i, i + distance) for i in range(size) if 0 <= i + distance < size]
    return lax.ppermute(block, "ctx", route)


def swapped(block, bit):
    return lax.ppermute(block, "ctx", [(i, i ^ bit) for i in range(lax.axis_size("ctx"))])


def tp_swapped(block):
    return lax.ppermute(block, "tp", [(0, 1), (1, 0)])


def params(mebibytes):
    return pltpu.CompilerParams(vmem_limit_bytes=mebibytes * 2**20)


def window_slot(block, place):
    plane = BACK - block // GROUP
    half = (block // 2 + place // 2) % 2
    core = (block + place) % 2
    return core, half * PLANES + plane


def doc_rows(lens_ref, first, rows):
    positions = first + lax.broadcasted_iota(jnp.int32, (1, rows), 1)

    def add_doc(doc, carry):
        end, starts, start = carry
        length = lens_ref[doc]
        end = end + length
        return (
            end,
            starts + jnp.where(positions >= end, length, 0),
            start + jnp.where(first >= end, length, 0),
        )

    zero = jnp.int32(0)
    _, starts, start = lax.fori_loop(
        0, lens_ref.shape[0], add_doc, (zero, jnp.zeros((1, rows), jnp.int32), zero)
    )
    return positions, starts, start


def block_bias(block, base, rows, positions, starts):
    key_pos = base + block * rows + lax.broadcasted_iota(jnp.int32, (rows, rows), 0)
    return jnp.where((key_pos >= starts) & (key_pos <= positions), 0.0, MASKED).astype(jnp.float32)


def head(h):
    return slice(h * HEAD_WIDTH, (h + 1) * HEAD_WIDTH)


def window_place(rows):
    device = lax.axis_index("ctx")
    place = device % GROUP
    first = device * rows
    base = first - (BACK * GROUP + place) * rows
    return place, first, base


def forward_kernel(heads, planes, last, lens_ref, qt_ref, *rest):
    count = len(planes) * GROUP
    parts, rest = rest[:count], rest[count:]
    if last:
        acc_in, max_in, sum_in, win_in = rest[:4]
        out_ref, mass_ref, win_ref, acc_ref, max_ref, sum_ref, score_ref, prob_ref = rest[4:]
    else:
        acc_ref, max_ref, sum_ref, win_ref, score_ref, prob_ref = rest
    rows = qt_ref.shape[2]
    scale = LOG2_E / math.sqrt(HEAD_WIDTH)
    place, first, base = window_place(rows)
    positions, starts, start = doc_rows(lens_ref, first, rows)
    for at, plane in enumerate(planes):
        for way in range(GROUP):
            where = (BACK - plane) * GROUP + (place ^ way)
            win_ref[where] = parts[at * GROUP + way][...]
    if last:
        acc_ref[...] = acc_in[...]
        max_ref[...] = max_in[...]
        sum_ref[...] = sum_in[...]
        kept = (BACK + 1 - planes[0]) * GROUP
        win_ref[kept:] = win_in[kept:]
    else:
        acc_ref[...] = jnp.zeros_like(acc_ref)
        max_ref[...] = jnp.full_like(max_ref, MASKED)
        sum_ref[...] = jnp.zeros_like(sum_ref)

    def visit(block, carry):
        keys = win_ref[block, 0]
        values_t = win_ref[block, 1].T
        bias = block_bias(block, base, rows, positions, starts)
        for h in range(heads):
            score_ref[h] = jnp.dot(keys, qt_ref[h], preferred_element_type=jnp.float32)
        for h in range(heads):
            scores = score_ref[h] * scale + bias
            old_max = max_ref[h : h + 1, :]
            new_max = jnp.maximum(old_max, jnp.max(scores, axis=0, keepdims=True))
            prob = jnp.exp2(scores - new_max)
            alpha = jnp.exp2(old_max - new_max)
            max_ref[h : h + 1, :] = new_max
            sum_ref[h : h + 1, :] = sum_ref[h : h + 1, :] * alpha + jnp.sum(
                prob, axis=0, keepdims=True
            )
            prob_ref[h] = prob.astype(jnp.bfloat16)
            acc_ref[h] = acc_ref[h] * alpha
        for h in range(heads):
            acc_ref[h] += jnp.dot(values_t, prob_ref[h], preferred_element_type=jnp.float32)
        return carry

    lowest = (BACK - planes[-1]) * GROUP
    highest = (BACK - planes[0] + 1) * GROUP
    lax.fori_loop(
        jnp.maximum((start - base) // rows, lowest),
        jnp.minimum(BACK * GROUP + place + 1, highest),
        visit,
        0,
    )
    if last:
        for h in range(heads):
            out_ref[:, head(h)] = (acc_ref[h] / sum_ref[h : h + 1, :]).T.astype(jnp.bfloat16)
        mass_ref[...] = max_ref[...] + jnp.log2(sum_ref[...])


def backward_kernel(
    heads,
    lens_ref,
    q_ref,
    qt_ref,
    win_ref,
    att_ref,
    grad_ref,
    grad_t_ref,
    mass_ref,
    dq_ref,
    keep_ref,
    send_ref,
    acc_ref,
    delta_ref,
    wide_mass_ref,
    prob_ref,
    grad_score_ref,
    bias_ref,
):
    rows = q_ref.shape[0]
    score_scale = 1.0 / math.sqrt(HEAD_WIDTH)
    scale = LOG2_E * score_scale
    place, first, base = window_place(rows)
    positions, starts, start = doc_rows(lens_ref, first, rows)
    acc_ref[...] = jnp.zeros_like(acc_ref)
    keep_ref[...] = jnp.zeros_like(keep_ref)
    send_ref[...] = jnp.zeros_like(send_ref)
    mass_t = mass_ref[...].T
    for h in range(heads):
        product = grad_ref[:, head(h)].astype(jnp.float32) * att_ref[:, head(h)].astype(jnp.float32)
        delta_ref[h] = jnp.broadcast_to(
            jnp.sum(product, axis=1, keepdims=True), (rows, HEAD_WIDTH)
        )
        wide_mass_ref[h] = jnp.broadcast_to(mass_t[:, h : h + 1], (rows, HEAD_WIDTH))
    chunk = HEAD_WIDTH

    def across(ref, h, piece):
        return jnp.concatenate([ref[h, piece]] * (rows // HEAD_WIDTH), axis=1)

    def visit(block, carry):
        keys = win_ref[block, 0]
        keys_t = keys.T
        values_t = win_ref[block, 1].T
        bias_ref[...] = block_bias(block, base, rows, positions, starts).T
        for h in range(heads):
            for at in range(0, rows, chunk):
                piece = slice(at, at + chunk)
                scores = (
                    jnp.dot(q_ref[piece, head(h)], keys_t, preferred_element_type=jnp.float32) * scale
                    + bias_ref[piece]
                )
                prob = jnp.exp2(scores - across(wide_mass_ref, h, piece))
                prob_ref[h, piece] = prob.astype(jnp.bfloat16)
                grad_prob = jnp.dot(
                    grad_ref[piece, head(h)], values_t, preferred_element_type=jnp.float32
                )
                grad_score_ref[h, piece] = (
                    prob * (grad_prob - across(delta_ref, h, piece))
                ).astype(jnp.bfloat16)
        key_grad = jnp.zeros((HEAD_WIDTH, rows), jnp.float32)
        value_grad = jnp.zeros((HEAD_WIDTH, rows), jnp.float32)
        for h in range(heads):
            value_grad = value_grad + jnp.dot(
                grad_t_ref[h], prob_ref[h], preferred_element_type=jnp.float32
            )
        for h in range(heads):
            key_grad = key_grad + jnp.dot(
                qt_ref[h], grad_score_ref[h], preferred_element_type=jnp.float32
            )
        for h in range(heads):
            acc_ref[h] += jnp.dot(grad_score_ref[h], keys, preferred_element_type=jnp.float32)
        key_grad = key_grad.T * score_scale
        value_grad = value_grad.T
        core, slot = window_slot(block, place)

        @pl.when(core == 0)
        def _():
            keep_ref[slot, 0] = key_grad
            keep_ref[slot, 1] = value_grad

        @pl.when(core == 1)
        def _():
            send_ref[slot, 0] = key_grad.astype(jnp.bfloat16)
            send_ref[slot, 1] = value_grad.astype(jnp.bfloat16)

        return carry

    lax.fori_loop((start - base) // rows, BACK * GROUP + place + 1, visit, 0)
    for h in range(heads):
        dq_ref[:, head(h)] = (acc_ref[h] * score_scale).astype(jnp.bfloat16)


def whole(shape=None):
    return pl.BlockSpec(memory_space=pltpu.VMEM)


SCALARS = pl.BlockSpec(memory_space=pltpu.SMEM)


def attend(doc_lengths, queries_t, planes, parts, before=()):
    heads, _, rows = queries_t.shape
    last = len(before) > 0
    visits = len(planes) * GROUP * heads * rows * rows
    sums = [(heads, HEAD_WIDTH, rows), (heads, rows), (heads, rows)]
    window = jax.ShapeDtypeStruct((WINDOW, 2, rows, HEAD_WIDTH), jnp.bfloat16)
    working = [
        pltpu.VMEM((heads, rows, rows), jnp.float32),
        pltpu.VMEM((heads, rows, rows), jnp.bfloat16),
    ]
    if last:
        out_shape = (
            jax.ShapeDtypeStruct((rows, heads * HEAD_WIDTH), jnp.bfloat16),
            jax.ShapeDtypeStruct((heads, rows), jnp.float32),
            window,
        )
        working = [pltpu.VMEM(shape, jnp.float32) for shape in sums] + working
    else:
        out_shape = tuple(jax.ShapeDtypeStruct(shape, jnp.float32) for shape in sums) + (window,)
    return pl.pallas_call(
        partial(forward_kernel, heads, planes, last),
        out_shape=out_shape,
        in_specs=[SCALARS] + [whole()] * (1 + len(parts) + len(before)),
        out_specs=(whole(),) * len(out_shape),
        scratch_shapes=working,
        compiler_params=params(12),
        cost_estimate=pl.CostEstimate(
            flops=4 * visits * HEAD_WIDTH, bytes_accessed=4 * 2**20, transcendentals=visits
        ),
        name="attend",
    )(doc_lengths, queries_t, *parts, *before)


def turn_kernel(wide_ref, out_ref):
    transpose_heads(wide_ref, out_ref)


def turned(wide):
    rows, width = wide.shape
    return pl.pallas_call(
        turn_kernel,
        out_shape=jax.ShapeDtypeStruct((width // HEAD_WIDTH, HEAD_WIDTH, rows), wide.dtype),
        in_specs=[whole()],
        out_specs=whole(),
        compiler_params=params(4),
        name="turned",
    )(wide)


def attend_back(doc_lengths, queries, queries_t, window, attention, grad, grad_t, mass):
    rows, width = queries.shape
    heads = width // HEAD_WIDTH
    visits = (REACH + 1) * heads * rows * rows
    parts_shape = (2 * PLANES, 2, rows, HEAD_WIDTH)
    return pl.pallas_call(
        partial(backward_kernel, heads),
        out_shape=(
            jax.ShapeDtypeStruct((rows, width), jnp.bfloat16),
            jax.ShapeDtypeStruct(parts_shape, jnp.float32),
            jax.ShapeDtypeStruct(parts_shape, jnp.bfloat16),
        ),
        in_specs=[SCALARS] + [whole()] * 7,
        out_specs=(whole(), whole(), whole()),
        scratch_shapes=[
            pltpu.VMEM((heads, rows, HEAD_WIDTH), jnp.float32),
            pltpu.VMEM((heads, rows, HEAD_WIDTH), jnp.float32),
            pltpu.VMEM((heads, rows, HEAD_WIDTH), jnp.float32),
            pltpu.VMEM((heads, rows, rows), jnp.bfloat16),
            pltpu.VMEM((heads, rows, rows), jnp.bfloat16),
            pltpu.VMEM((rows, rows), jnp.float32),
        ],
        compiler_params=params(16),
        cost_estimate=pl.CostEstimate(
            flops=10 * visits * HEAD_WIDTH, bytes_accessed=8 * 2**20, transcendentals=visits
        ),
        name="attend_back",
    )(doc_lengths, queries, queries_t, window, attention, grad, grad_t, mass)


def pair_kernel(keys_ref, values_ref, out_ref, sems):
    copies = [
        pltpu.make_async_copy(ref, out_ref.at[kind], sems.at[kind])
        for kind, ref in enumerate((keys_ref, values_ref))
    ]
    for copy in copies:
        copy.start()
    for copy in copies:
        copy.wait()


def pair_up(keys, values):
    return pl.pallas_call(
        pair_kernel,
        out_shape=jax.ShapeDtypeStruct((2,) + keys.shape, keys.dtype),
        in_specs=[pl.BlockSpec(memory_space=pl.ANY)] * 2,
        out_specs=whole(),
        scratch_shapes=[pltpu.SemaphoreType.DMA((2,))],
        compiler_params=params(4),
        name="pair_up",
    )(keys, values)


def project_kernel(tile, pieces, half_ref, att_ref, weight_ref, *rest):
    others, outs = rest[: len(rest) - pieces], rest[len(rest) - pieces :]
    columns = weight_ref.shape[1] // 2
    first = half_ref[0] * columns
    part = columns // max(len(others), pieces)
    for at in range(0, columns, tile):
        piece = pl.ds(pl.multiple_of(first + at, tile), tile)
        total = jnp.dot(
            att_ref[...], weight_ref[:, piece], preferred_element_type=jnp.float32
        ).astype(jnp.bfloat16)
        if others:
            other = others[at // part][:, at % part : at % part + tile].astype(jnp.float32)
            total = (total.astype(jnp.float32) + other).astype(jnp.bfloat16)
            outs[0][:, at : at + tile] = total
        else:
            outs[at // part][:, at % part : at % part + tile] = total


def project(half, attention, weight, *other, pieces=1, tile=512):
    rows, depth = attention.shape
    columns = weight.shape[1] // 2
    piece = jax.ShapeDtypeStruct((rows, columns // pieces), jnp.bfloat16)
    return pl.pallas_call(
        partial(project_kernel, tile, pieces),
        out_shape=(piece,) * pieces,
        in_specs=[SCALARS] + [whole()] * (2 + len(other)),
        out_specs=(whole(),) * pieces,
        compiler_params=params(8),
        cost_estimate=pl.CostEstimate(
            flops=2 * rows * depth * columns, bytes_accessed=2 * depth * columns, transcendentals=0
        ),
        name="project",
    )(half, attention, weight, *other)


def transpose_heads(wide_ref, out_ref):
    for h in range(out_ref.shape[0]):
        out_ref[h] = wide_ref[:, head(h)].T


def grad_kernel(tile, order_ref, *refs):
    halves, (weight_ref, out_ref, out_t_ref) = refs[:2], refs[2:]
    columns = halves[0].shape[1]
    for at in range(0, weight_ref.shape[0], tile):
        total = 0.0
        for side, cot_ref in enumerate(halves):
            piece = pl.ds(pl.multiple_of(order_ref[side] * columns, columns), columns)
            total += lax.dot_general(
                cot_ref[...], weight_ref[at : at + tile, piece], NT, preferred_element_type=jnp.float32
            )
        out_ref[:, at : at + tile] = total.astype(jnp.bfloat16)
    transpose_heads(out_ref, out_t_ref)


def attention_grad(order, halves, weight, tile=256):
    rows, columns = halves[0].shape
    depth = weight.shape[0]
    return pl.pallas_call(
        partial(grad_kernel, tile),
        out_shape=(
            jax.ShapeDtypeStruct((rows, depth), jnp.bfloat16),
            jax.ShapeDtypeStruct((depth // HEAD_WIDTH, HEAD_WIDTH, rows), jnp.bfloat16),
        ),
        in_specs=[SCALARS] + [whole()] * 3,
        out_specs=(whole(), whole()),
        compiler_params=params(8),
        cost_estimate=pl.CostEstimate(
            flops=4 * rows * depth * columns, bytes_accessed=4 * depth * columns, transcendentals=0
        ),
        name="attention_grad",
    )(order, *halves, weight)


def body(queries, keys, values, out_weight, cotangent, doc_lengths):
    mine = lax.axis_index("tp").astype(jnp.int32).reshape(1)
    theirs = 1 - mine
    order = jnp.concatenate([mine, theirs])
    pair = pair_up(keys, values)
    other_cot = tp_swapped(cotangent)
    planes = [pair] + [shifted(pair, plane * GROUP) for plane in range(1, PLANES)]
    queries_t = turned(queries)

    def group_of(block):
        pairs = [block, swapped(block, 2)]
        return [pairs[0], swapped(pairs[0], 1), pairs[1], swapped(pairs[1], 1)]

    groups = [group_of(block) for block in planes]
    early = tuple(range(BACK))
    sums = attend(doc_lengths, queries_t, early, sum((groups[plane] for plane in early), []))
    attention, mass, window = attend(doc_lengths, queries_t, (BACK,), groups[BACK], sums)
    other_terms = project(theirs, attention, out_weight, pieces=2)
    early_mixed = tp_swapped(other_terms[0])
    other_cot, other_terms = lax.optimization_barrier((other_cot, other_terms))
    grad, grad_t = attention_grad(order, (cotangent, other_cot), out_weight)
    query_grad, keep, send = attend_back(
        doc_lengths, queries, queries_t, window, attention, grad, grad_t, mass
    )
    send, early_mixed = lax.optimization_barrier((send, early_mixed))
    late_mixed = tp_swapped(other_terms[1])
    received = swapped(send, 1)

    def core_sum(slot):
        return keep[slot] + received[slot].astype(jnp.float32)

    crossed = [
        swapped(core_sum(PLANES + plane).astype(jnp.bfloat16), 2) for plane in reversed(range(PLANES))
    ][::-1]
    half_sum = [core_sum(plane) + crossed[plane].astype(jnp.float32) for plane in range(PLANES)]
    totals = half_sum[0]
    for plane in reversed(range(1, PLANES)):
        totals = totals + shifted(
            half_sum[plane].astype(jnp.bfloat16), -plane * GROUP
        ).astype(jnp.float32)
    (mixed_out,) = project(mine, attention, out_weight, early_mixed, late_mixed)
    keys_gradient = totals[0].astype(jnp.bfloat16)
    values_gradient = totals[1].astype(jnp.bfloat16)
    return (mixed_out, query_grad, keys_gradient, values_gradient)


def solution(mesh):
    in_specs = (P("ctx", "tp"), P("ctx", "tp"), P("ctx", "tp"), P("tp", None), P("ctx", "tp"), P())
    out_specs = (P("ctx", "tp"), P("ctx", "tp"), P("ctx", "tp"), P("ctx", "tp"))
    return jax.shard_map(body, mesh=mesh, in_specs=in_specs, out_specs=out_specs, check_vma=False)
```

profile of v0, /device:TPU:16, one launch (start us, length us, event | category | flops | bytes accessed | tf_op | source)
XLA Modules:
  0.0 75.0 jit_solution(16862515162620306217)
XLA Ops:
  0.6 1.6 %collective-permute-start.11 = (bf16[256,2048]{1,0:T(8,128)(2,1)}, bf16[256,2048]{1,0:T(8,128)(2,1)S(1)}, u32[]{:S(2)}, u32[]{:S(2)}) collective-permute-start(bf16[256,2048]{1,0:T(8,128)(2,1)} %refs_0_.1), channel_id=1, source_target_pairs={{0,1},{1,0},{2,3},{3,2},{4,5},{5,4},{6,7},{7,6},{8,9},{9,8},{10,11... | collective-permute-start | bytes 3145736 | tf_op jit(solution)/shard_map/ppermute | solution.py:33
  2.2 0.8 %copy-done.4 = bf16[256,128]{1,0:T(8,128)(2,1)S(1)} copy-done((bf16[256,128]{1,0:T(8,128)(2,1)S(1)}, bf16[256,128]{1,0:T(8,128)(2,1)}, u32[]{:S(2)}) %copy-start.4) | copy-done | bytes 65560
  3.0 0.8 %copy-done.5 = bf16[256,128]{1,0:T(8,128)(2,1)S(1)} copy-done((bf16[256,128]{1,0:T(8,128)(2,1)S(1)}, bf16[256,128]{1,0:T(8,128)(2,1)}, u32[]{:S(2)}) %copy-start.5) | copy-done | bytes 65560
  4.0 3.5 %collective-permute-start.7 = (bf16[2,256,128]{2,1,0:T(8,128)(2,1)S(1)}, bf16[2,256,128]{2,1,0:T(8,128)(2,1)S(1)}, u32[]{:S(2)}, u32[]{:S(2)}) collective-permute-start(bf16[2,256,128]{2,1,0:T(8,128)(2,1)S(1)} %pair_up.1.rest_0_), channel_id=1, source_target_pairs={{0,8},{2,10},{4,12},{6,14},{8,16},{10,18},{12,20},{14,22},{16,24},... | collective-permute-start | bytes 393224 | tf_op jit(solution)/shard_map/ppermute | solution.py:25
  7.5 1.6 %collective-permute-start.5 = (bf16[2,256,128]{2,1,0:T(8,128)(2,1)S(1)}, bf16[2,256,128]{2,1,0:T(8,128)(2,1)S(1)}, u32[]{:S(2)}, u32[]{:S(2)}) collective-permute-start(bf16[2,256,128]{2,1,0:T(8,128)(2,1)S(1)} %pair_up.1.rest_0_), channel_id=1, source_target_pairs={{0,4},{2,6},{4,0},{6,2},{8,12},{10,14},{12,8},{14,10},{16,20},{18,... | collective-permute-start | bytes 393224 | tf_op jit(solution)/shard_map/ppermute | solution.py:29
  9.1 1.3 %collective-permute-start = (bf16[2,256,128]{2,1,0:T(8,128)(2,1)S(1)}, bf16[2,256,128]{2,1,0:T(8,128)(2,1)S(1)}, u32[]{:S(2)}, u32[]{:S(2)}) collective-permute-start(bf16[2,256,128]{2,1,0:T(8,128)(2,1)S(1)} %pair_up.1.rest_0_), channel_id=1, source_target_pairs={{0,16},{2,18},{4,20},{6,22},{8,24},{10,26},{12,28},{14,30},{1,17},... | collective-permute-start | bytes 393224 | tf_op jit(solution)/shard_map/ppermute | solution.py:25
  10.5 0.4 collective-permute-done.7.rest_4_
  10.9 1.7 %collective-permute-start.9 = (bf16[2,256,128]{2,1,0:T(8,128)(2,1)S(1)}, bf16[2,256,128]{2,1,0:T(8,128)(2,1)S(1)}, u32[]{:S(2)}, u32[]{:S(2)}) collective-permute-start(bf16[2,256,128]{2,1,0:T(8,128)(2,1)S(1)} %collective-permute-done.7.rest_4_), channel_id=1, source_target_pairs={{0,4},{2,6},{4,0},{6,2},{8,12},{10,14},{12,8},{14,10},{16,20},{18,... | collective-permute-start | bytes 393224 | tf_op jit(solution)/shard_map/ppermute | solution.py:29
  12.6 4.3 %collective-permute-done.rest_0_ = bf16[2,256,128]{2,1,0:T(8,128)(2,1)S(1)} collective-permute-done((bf16[2,256,128]{2,1,0:T(8,128)(2,1)S(1)}, bf16[2,256,128]{2,1,0:T(8,128)(2,1)S(1)}, u32[]{:S(2)}, u32[]{:S(2)}) %collective-permute-start) | collective-permute-done | bytes 131104 | tf_op jit(solution)/shard_map/ppermute | solution.py:25
  17.0 0.5 collective-permute-start.2
  17.5 0.5 collective-permute-start.10
  18.0 1.0 %copy-done.2 = bf16[256,1024]{1,0:T(8,128)(2,1)S(1)} copy-done((bf16[256,1024]{1,0:T(8,128)(2,1)S(1)}, bf16[256,1024]{1,0:T(8,128)(2,1)}, u32[]{:S(2)}) %copy-start.2) | copy-done | bytes 524312
  19.4 2.5 %collective-permute-done.2.rest_2_ = bf16[2,256,128]{2,1,0:T(8,128)(2,1)S(1)} collective-permute-done((bf16[2,256,128]{2,1,0:T(8,128)(2,1)S(1)}, bf16[2,256,128]{2,1,0:T(8,128)(2,1)S(1)}, u32[]{:S(2)}, u32[]{:S(2)}) %collective-permute-start.2) | collective-permute-done | bytes 131104 | tf_op jit(solution)/shard_map/ppermute | solution.py:29
  21.9 0.6 copy-done.6
  22.6 4.8 %attend.2 = (f32[8,128,256]{2,1,0:T(8,128)S(1)}, f32[8,256]{1,0:T(8,128)S(1)}, f32[8,256]{1,0:T(8,128)S(1)}, bf16[12,2,256,128]{3,2,1,0:T(8,128)(2,1)S(1)}) custom-call(s32[8]{0:T(128)S(1)} %copy-done.6, bf16[8,128,256]{2,1,0:T(8,128)(2,1)S(1)} %turned.1.qt_ref, bf16[2,256,128]{2,1,0:T(8,128)(2,1)S(1)} %pair_up.1.rest_0_, ...), custom_call_target="tpu_custom_call" | custom-call | flops 2147483648 | bytes 4194304 | tf_op jit(solution)/shard_map/attend/pallas_call | solution.py:266
  27.5 1.0 %attend.3 = (bf16[256,1024]{1,0:T(8,128)(2,1)S(1)}, f32[8,256]{1,0:T(8,128)S(1)}, bf16[12,2,256,128]{3,2,1,0:T(8,128)(2,1)S(1)}) custom-call(s32[8]{0:T(128)S(1)} %copy-done.7, bf16[8,128,256]{2,1,0:T(8,128)(2,1)S(1)} %turned.1.qt_ref, bf16[2,256,128]{2,1,0:T(8,128)(2,1)S(1)} %collective-permute-done.rest_0_, ...), custom_call_target="tpu_custom_call" | custom-call | flops 1073741824 | bytes 4194304 | tf_op jit(solution)/shard_map/attend/pallas_call | solution.py:266
  28.5 1.3 %project.2 = (bf16[256,1024]{1,0:T(8,128)(2,1)S(1)}, bf16[256,1024]{1,0:T(8,128)(2,1)S(1)}) custom-call(s32[1]{0:T(128)S(6)} %sub.3.half_ref, bf16[256,1024]{1,0:T(8,128)(2,1)S(1)} %get-tuple-element.26.att_ref, bf16[1024,4096]{1,0:T(8,128)(2,1)S(1)} %copy-done), custom_call_target="tpu_custom_call" | custom-call | flops 1073741824 | bytes 4194304 | tf_op jit(solution)/shard_map/project/pallas_call | solution.py:371
  29.8 0.6 collective-permute-start.12
  30.4 3.1 %attention_grad.1 = (bf16[256,1024]{1,0:T(8,128)(2,1)S(1)}, bf16[8,128,256]{2,1,0:T(8,128)(2,1)S(1)}) custom-call(s32[2]{0:T(128)S(1)} %pad_add_fusion.order_ref, bf16[256,2048]{1,0:T(8,128)(2,1)S(1)} %copy-done.1, bf16[256,2048]{1,0:T(8,128)(2,1)S(1)} %collective-permute-done.11.refs_1_, bf16[1024,4096]{1,0:T(8,128)(2,1)S(1)} %copy-done), custom_call_target="tpu_custom_call" | custom-call | flops 2147483648 | bytes 8388608 | tf_op jit(solution)/shard_map/attention_grad/pallas_call | solution.py:406
  33.5 8.2 %attend_back.1 = (bf16[256,1024]{1,0:T(8,128)(2,1)}, f32[6,2,256,128]{3,2,1,0:T(8,128)S(1)}, bf16[6,2,256,128]{3,2,1,0:T(8,128)(2,1)S(1)}) custom-call(s32[8]{0:T(128)S(1)} %copy-done.7, bf16[256,1024]{1,0:T(8,128)(2,1)S(1)} %copy-done.3, bf16[8,128,256]{2,1,0:T(8,128)(2,1)S(1)} %turned.1.qt_ref, bf16[12,2,256,128]{3,2,1,0:T(8,128)(2,1)S(1)} %get-tuple-element.27.win_ref, ...), custom_call_target="tpu_custom_call" | custom-call | flops 6039797760 | bytes 8388608 | tf_op jit(solution)/shard_map/attend_back/pallas_call | solution.py:301
  41.7 2.4 %collective-permute-done.12.rest_0_ = bf16[256,1024]{1,0:T(8,128)(2,1)S(1)} collective-permute-done((bf16[256,1024]{1,0:T(8,128)(2,1)S(1)}, bf16[256,1024]{1,0:T(8,128)(2,1)S(1)}, u32[]{:S(2)}, u32[]{:S(2)}) %collective-permute-start.12) | collective-permute-done | bytes 524320 | tf_op jit(solution)/shard_map/ppermute | solution.py:33
  44.4 1.4 %collective-permute-start.13 = (bf16[256,1024]{1,0:T(8,128)(2,1)S(1)}, bf16[256,1024]{1,0:T(8,128)(2,1)S(1)}, u32[]{:S(2)}, u32[]{:S(2)}) collective-permute-start(bf16[256,1024]{1,0:T(8,128)(2,1)S(1)} %get-tuple-element.36), channel_id=1, source_target_pairs={{0,1},{1,0},{2,3},{3,2},{4,5},{5,4},{6,7},{7,6},{8,9},{9,8},{10,11... | collective-permute-start | bytes 1572872 | tf_op jit(solution)/shard_map/ppermute | solution.py:33
  45.9 0.6 collective-permute-done.14
  46.5 5.3 %collective-permute-start.18 = (bf16[2,256,128]{2,1,0:T(8,128)(2,1)S(1)}, bf16[2,256,128]{2,1,0:T(8,128)(2,1)S(1)}, u32[]{:S(2)}, u32[]{:S(2)}) collective-permute-start(bf16[2,256,128]{2,1,0:T(8,128)(2,1)S(1)} %get-tuple-element.41), channel_id=1, source_target_pairs={{0,4},{2,6},{4,0},{6,2},{8,12},{10,14},{12,8},{14,10},{16,20},{18,... | collective-permute-start | bytes 393224 | tf_op jit(solution)/shard_map/ppermute | solution.py:29
  51.9 1.9 %collective-permute-start.15 = (bf16[2,256,128]{2,1,0:T(8,128)(2,1)S(1)}, bf16[2,256,128]{2,1,0:T(8,128)(2,1)S(1)}, u32[]{:S(2)}, u32[]{:S(2)}) collective-permute-start(bf16[2,256,128]{2,1,0:T(8,128)(2,1)S(1)} %get-tuple-element.40), channel_id=1, source_target_pairs={{0,4},{2,6},{4,0},{6,2},{8,12},{10,14},{12,8},{14,10},{16,20},{18,... | collective-permute-start | bytes 393224 | tf_op jit(solution)/shard_map/ppermute | solution.py:29
  53.9 2.3 %collective-permute-done.18 = bf16[2,256,128]{2,1,0:T(8,128)(2,1)S(1)} collective-permute-done((bf16[2,256,128]{2,1,0:T(8,128)(2,1)S(1)}, bf16[2,256,128]{2,1,0:T(8,128)(2,1)S(1)}, u32[]{:S(2)}, u32[]{:S(2)}) %collective-permute-start.18) | collective-permute-done | bytes 131104 | tf_op jit(solution)/shard_map/ppermute | solution.py:29
  56.2 2.8 %collective-permute-done.16 = bf16[2,256,128]{2,1,0:T(8,128)(2,1)S(1)} collective-permute-done((bf16[2,256,128]{2,1,0:T(8,128)(2,1)S(1)}, bf16[2,256,128]{2,1,0:T(8,128)(2,1)S(1)}, u32[]{:S(2)}, u32[]{:S(2)}) %collective-permute-start.16) | collective-permute-done | bytes 131104 | tf_op jit(solution)/shard_map/ppermute | solution.py:29
  59.1 1.3 %collective-permute-start.17 = (bf16[2,256,128]{2,1,0:T(8,128)(2,1)S(1)}, bf16[2,256,128]{2,1,0:T(8,128)(2,1)S(1)}, u32[]{:S(2)}, u32[]{:S(2)}) collective-permute-start(bf16[2,256,128]{2,1,0:T(8,128)(2,1)S(1)} %get-tuple-element.43), channel_id=1, source_target_pairs={{16,0},{18,2},{20,4},{22,6},{24,8},{26,10},{28,12},{30,14},{17,1},... | collective-permute-start | bytes 393224 | tf_op jit(solution)/shard_map/ppermute | solution.py:25
  60.4 1.9 %collective-permute-start.19 = (bf16[2,256,128]{2,1,0:T(8,128)(2,1)S(1)}, bf16[2,256,128]{2,1,0:T(8,128)(2,1)S(1)}, u32[]{:S(2)}, u32[]{:S(2)}) collective-permute-start(bf16[2,256,128]{2,1,0:T(8,128)(2,1)S(1)} %get-tuple-element.44), channel_id=1, source_target_pairs={{8,0},{10,2},{12,4},{14,6},{16,8},{18,10},{20,12},{22,14},{24,16},... | collective-permute-start | bytes 393224 | tf_op jit(solution)/shard_map/ppermute | solution.py:25
  62.3 2.3 %project.3 = bf16[256,2048]{1,0:T(8,128)(2,1)} custom-call(s32[1]{0:T(128)} %bitcast.half_ref, bf16[256,1024]{1,0:T(8,128)(2,1)S(1)} %get-tuple-element.26.att_ref, bf16[1024,4096]{1,0:T(8,128)(2,1)S(1)} %copy-done, bf16[256,1024]{1,0:T(8,128)(2,1)S(1)} %collective-permute-done.12.rest_0_, bf16[256,1024]{1,0:T(8,128)(2,1)S(1)} %collective-permute-done.13.rest_1_), custom_call_target="tpu_custom_call" | custom-call | flops 1073741824 | bytes 4194304 | tf_op jit(solution)/shard_map/project/pallas_call | solution.py:371
  64.7 9.6 %collective-permute-done.19 = bf16[2,256,128]{2,1,0:T(8,128)(2,1)S(1)} collective-permute-done((bf16[2,256,128]{2,1,0:T(8,128)(2,1)S(1)}, bf16[2,256,128]{2,1,0:T(8,128)(2,1)S(1)}, u32[]{:S(2)}, u32[]{:S(2)}) %collective-permute-start.19) | collective-permute-done | bytes 131104 | tf_op jit(solution)/shard_map/ppermute | solution.py:25
  74.4 0.7 slice_bitcast_fusion
  (37 shorter events, 1.3 us)
Async XLA Ops:
  0.6 29.7 %collective-permute-start.11 = (bf16[256,2048]{1,0:T(8,128)(2,1)}, bf16[256,2048]{1,0:T(8,128)(2,1)S(1)}, u32[]{:S(2)}, u32[]{:S(2)}) collective-permute-start(bf16[256,2048]{1,0:T(8,128)(2,1)} %refs_0_.1), channel_id=1, source_target_pairs={{0,1},{1,0},{2,3},{3,2},{4,5},{5,4},{6,7},{7,6},{8,9},{9,8},{10,11... | collective-permute-start | bytes 3145736 | tf_op jit(solution)/shard_map/ppermute | solution.py:33
  2.2 0.8 %copy-start.4 = (bf16[256,128]{1,0:T(8,128)(2,1)S(1)}, bf16[256,128]{1,0:T(8,128)(2,1)}, u32[]{:S(2)}) copy-start(bf16[256,128]{1,0:T(8,128)(2,1)} %keys_ref.1) | copy-start | bytes 196612
  3.0 0.8 %copy-start.5 = (bf16[256,128]{1,0:T(8,128)(2,1)S(1)}, bf16[256,128]{1,0:T(8,128)(2,1)}, u32[]{:S(2)}) copy-start(bf16[256,128]{1,0:T(8,128)(2,1)} %values_ref.1) | copy-start | bytes 196612
  4.0 6.9 %collective-permute-start.7 = (bf16[2,256,128]{2,1,0:T(8,128)(2,1)S(1)}, bf16[2,256,128]{2,1,0:T(8,128)(2,1)S(1)}, u32[]{:S(2)}, u32[]{:S(2)}) collective-permute-start(bf16[2,256,128]{2,1,0:T(8,128)(2,1)S(1)} %pair_up.1.rest_0_), channel_id=1, source_target_pairs={{0,8},{2,10},{4,12},{6,14},{8,16},{10,18},{12,20},{14,22},{16,24},... | collective-permute-start | bytes 393224 | tf_op jit(solution)/shard_map/ppermute | solution.py:25
  7.5 5.1 %collective-permute-start.5 = (bf16[2,256,128]{2,1,0:T(8,128)(2,1)S(1)}, bf16[2,256,128]{2,1,0:T(8,128)(2,1)S(1)}, u32[]{:S(2)}, u32[]{:S(2)}) collective-permute-start(bf16[2,256,128]{2,1,0:T(8,128)(2,1)S(1)} %pair_up.1.rest_0_), channel_id=1, source_target_pairs={{0,4},{2,6},{4,0},{6,2},{8,12},{10,14},{12,8},{14,10},{16,20},{18,... | collective-permute-start | bytes 393224 | tf_op jit(solution)/shard_map/ppermute | solution.py:29
  9.1 7.8 %collective-permute-start = (bf16[2,256,128]{2,1,0:T(8,128)(2,1)S(1)}, bf16[2,256,128]{2,1,0:T(8,128)(2,1)S(1)}, u32[]{:S(2)}, u32[]{:S(2)}) collective-permute-start(bf16[2,256,128]{2,1,0:T(8,128)(2,1)S(1)} %pair_up.1.rest_0_), channel_id=1, source_target_pairs={{0,16},{2,18},{4,20},{6,22},{8,24},{10,26},{12,28},{14,30},{1,17},... | collective-permute-start | bytes 393224 | tf_op jit(solution)/shard_map/ppermute | solution.py:25
  10.4 7.1 %collective-permute-start.4 = (bf16[2,256,128]{2,1,0:T(8,128)(2,1)S(1)}, bf16[2,256,128]{2,1,0:T(8,128)(2,1)S(1)}, u32[]{:S(2)}, u32[]{:S(2)}) collective-permute-start(bf16[2,256,128]{2,1,0:T(8,128)(2,1)S(1)} %pair_up.1.rest_0_), channel_id=1, source_target_pairs={{0,2},{2,0},{4,6},{6,4},{8,10},{10,8},{12,14},{14,12},{16,18},{18,... | collective-permute-start | bytes 393224 | tf_op jit(solution)/shard_map/ppermute | solution.py:29
  10.9 6.6 %collective-permute-start.9 = (bf16[2,256,128]{2,1,0:T(8,128)(2,1)S(1)}, bf16[2,256,128]{2,1,0:T(8,128)(2,1)S(1)}, u32[]{:S(2)}, u32[]{:S(2)}) collective-permute-start(bf16[2,256,128]{2,1,0:T(8,128)(2,1)S(1)} %collective-permute-done.7.rest_4_), channel_id=1, source_target_pairs={{0,4},{2,6},{4,0},{6,2},{8,12},{10,14},{12,8},{14,10},{16,20},{18,... | collective-permute-start | bytes 393224 | tf_op jit(solution)/shard_map/ppermute | solution.py:29
  12.6 6.7 %collective-permute-start.8 = (bf16[2,256,128]{2,1,0:T(8,128)(2,1)S(1)}, bf16[2,256,128]{2,1,0:T(8,128)(2,1)S(1)}, u32[]{:S(2)}, u32[]{:S(2)}) collective-permute-start(bf16[2,256,128]{2,1,0:T(8,128)(2,1)S(1)} %collective-permute-done.7.rest_4_), channel_id=1, source_target_pairs={{0,2},{2,0},{4,6},{6,4},{8,10},{10,8},{12,14},{14,12},{16,18},{18,... | collective-permute-start | bytes 393224 | tf_op jit(solution)/shard_map/ppermute | solution.py:29
  17.0 5.0 %collective-permute-start.2 = (bf16[2,256,128]{2,1,0:T(8,128)(2,1)S(1)}, bf16[2,256,128]{2,1,0:T(8,128)(2,1)S(1)}, u32[]{:S(2)}, u32[]{:S(2)}) collective-permute-start(bf16[2,256,128]{2,1,0:T(8,128)(2,1)S(1)} %collective-permute-done.rest_0_), channel_id=1, source_target_pairs={{0,4},{2,6},{4,0},{6,2},{8,12},{10,14},{12,8},{14,10},{16,20},{18,... | collective-permute-start | bytes 393224 | tf_op jit(solution)/shard_map/ppermute | solution.py:29
  17.5 4.5 %collective-permute-start.6 = (bf16[2,256,128]{2,1,0:T(8,128)(2,1)S(1)}, bf16[2,256,128]{2,1,0:T(8,128)(2,1)S(1)}, u32[]{:S(2)}, u32[]{:S(2)}) collective-permute-start(bf16[2,256,128]{2,1,0:T(8,128)(2,1)S(1)} %collective-permute-done.5.rest_2_), channel_id=1, source_target_pairs={{0,2},{2,0},{4,6},{6,4},{8,10},{10,8},{12,14},{14,12},{16,18},{18,... | collective-permute-start | bytes 393224 | tf_op jit(solution)/shard_map/ppermute | solution.py:29
  17.5 4.5 %collective-permute-start.10 = (bf16[2,256,128]{2,1,0:T(8,128)(2,1)S(1)}, bf16[2,256,128]{2,1,0:T(8,128)(2,1)S(1)}, u32[]{:S(2)}, u32[]{:S(2)}) collective-permute-start(bf16[2,256,128]{2,1,0:T(8,128)(2,1)S(1)} %collective-permute-done.9.rest_6_), channel_id=1, source_target_pairs={{0,2},{2,0},{4,6},{6,4},{8,10},{10,8},{12,14},{14,12},{16,18},{18,... | collective-permute-start | bytes 393224 | tf_op jit(solution)/shard_map/ppermute | solution.py:29
  18.0 1.0 %copy-start.2 = (bf16[256,1024]{1,0:T(8,128)(2,1)S(1)}, bf16[256,1024]{1,0:T(8,128)(2,1)}, u32[]{:S(2)}) copy-start(bf16[256,1024]{1,0:T(8,128)(2,1)} %q_ref.1) | copy-start | bytes 1572868
  19.2 8.2 %copy-start.7 = (s32[8]{0:T(128)S(1)}, s32[8]{0:T(128)}, u32[]{:S(2)}) copy-start(s32[8]{0:T(128)} %lens_ref.5) | copy-start | bytes 100
  19.3 8.1 %collective-permute-start.1 = (bf16[2,256,128]{2,1,0:T(8,128)(2,1)S(1)}, bf16[2,256,128]{2,1,0:T(8,128)(2,1)S(1)}, u32[]{:S(2)}, u32[]{:S(2)}) collective-permute-start(bf16[2,256,128]{2,1,0:T(8,128)(2,1)S(1)} %collective-permute-done.rest_0_), channel_id=1, source_target_pairs={{0,2},{2,0},{4,6},{6,4},{8,10},{10,8},{12,14},{14,12},{16,18},{18,... | collective-permute-start | bytes 393224 | tf_op jit(solution)/shard_map/ppermute | solution.py:29
  21.9 5.5 %collective-permute-start.3 = (bf16[2,256,128]{2,1,0:T(8,128)(2,1)S(1)}, bf16[2,256,128]{2,1,0:T(8,128)(2,1)S(1)}, u32[]{:S(2)}, u32[]{:S(2)}) collective-permute-start(bf16[2,256,128]{2,1,0:T(8,128)(2,1)S(1)} %collective-permute-done.2.rest_2_), channel_id=1, source_target_pairs={{0,2},{2,0},{4,6},{6,4},{8,10},{10,8},{12,14},{14,12},{16,18},{18,... | collective-permute-start | bytes 393224 | tf_op jit(solution)/shard_map/ppermute | solution.py:29
  21.9 0.7 copy-start.6
  22.6 5.9 %copy-start = (bf16[1024,4096]{1,0:T(8,128)(2,1)S(1)}, bf16[1024,4096]{1,0:T(8,128)(2,1)}, u32[]{:S(2)}) copy-start(bf16[1024,4096]{1,0:T(8,128)(2,1)} %weight_ref.3) | copy-start | bytes 25165828
  28.5 1.9 %copy-start.1 = (bf16[256,2048]{1,0:T(8,128)(2,1)S(1)}, bf16[256,2048]{1,0:T(8,128)(2,1)}, u32[]{:S(2)}) copy-start(bf16[256,2048]{1,0:T(8,128)(2,1)} %refs_0_.1) | copy-start | bytes 3145732
  29.8 14.4 %collective-permute-start.12 = (bf16[256,1024]{1,0:T(8,128)(2,1)S(1)}, bf16[256,1024]{1,0:T(8,128)(2,1)S(1)}, u32[]{:S(2)}, u32[]{:S(2)}) collective-permute-start(bf16[256,1024]{1,0:T(8,128)(2,1)S(1)} %get-tuple-element.28), channel_id=1, source_target_pairs={{0,1},{1,0},{2,3},{3,2},{4,5},{5,4},{6,7},{7,6},{8,9},{9,8},{10,11... | collective-permute-start | bytes 1572872 | tf_op jit(solution)/shard_map/ppermute | solution.py:33
  30.4 3.1 %copy-start.3 = (bf16[256,1024]{1,0:T(8,128)(2,1)S(1)}, bf16[256,1024]{1,0:T(8,128)(2,1)}, u32[]{:S(2)}) copy-start(bf16[256,1024]{1,0:T(8,128)(2,1)} %q_ref.1) | copy-start | bytes 1572868
  44.1 2.3 %collective-permute-start.14 = (bf16[6,2,256,128]{3,2,1,0:T(8,128)(2,1)S(1)}, bf16[6,2,256,128]{3,2,1,0:T(8,128)(2,1)S(1)}, u32[]{:S(2)}, u32[]{:S(2)}) collective-permute-start(bf16[6,2,256,128]{3,2,1,0:T(8,128)(2,1)S(1)} %get-tuple-element.39), channel_id=1, source_target_pairs={{0,2},{2,0},{4,6},{6,4},{8,10},{10,8},{12,14},{14,12},{16,18},{18,... | collective-permute-start | bytes 2359304 | tf_op jit(solution)/shard_map/ppermute | solution.py:29
  44.4 17.9 %collective-permute-start.13 = (bf16[256,1024]{1,0:T(8,128)(2,1)S(1)}, bf16[256,1024]{1,0:T(8,128)(2,1)S(1)}, u32[]{:S(2)}, u32[]{:S(2)}) collective-permute-start(bf16[256,1024]{1,0:T(8,128)(2,1)S(1)} %get-tuple-element.36), channel_id=1, source_target_pairs={{0,1},{1,0},{2,3},{3,2},{4,5},{5,4},{6,7},{7,6},{8,9},{9,8},{10,11... | collective-permute-start | bytes 1572872 | tf_op jit(solution)/shard_map/ppermute | solution.py:33
  46.5 9.7 %collective-permute-start.18 = (bf16[2,256,128]{2,1,0:T(8,128)(2,1)S(1)}, bf16[2,256,128]{2,1,0:T(8,128)(2,1)S(1)}, u32[]{:S(2)}, u32[]{:S(2)}) collective-permute-start(bf16[2,256,128]{2,1,0:T(8,128)(2,1)S(1)} %get-tuple-element.41), channel_id=1, source_target_pairs={{0,4},{2,6},{4,0},{6,2},{8,12},{10,14},{12,8},{14,10},{16,20},{18,... | collective-permute-start | bytes 393224 | tf_op jit(solution)/shard_map/ppermute | solution.py:29
  51.9 7.1 %collective-permute-start.16 = (bf16[2,256,128]{2,1,0:T(8,128)(2,1)S(1)}, bf16[2,256,128]{2,1,0:T(8,128)(2,1)S(1)}, u32[]{:S(2)}, u32[]{:S(2)}) collective-permute-start(bf16[2,256,128]{2,1,0:T(8,128)(2,1)S(1)} %get-tuple-element.42), channel_id=1, source_target_pairs={{0,4},{2,6},{4,0},{6,2},{8,12},{10,14},{12,8},{14,10},{16,20},{18,... | collective-permute-start | bytes 393224 | tf_op jit(solution)/shard_map/ppermute | solution.py:29
  51.9 12.7 %collective-permute-start.15 = (bf16[2,256,128]{2,1,0:T(8,128)(2,1)S(1)}, bf16[2,256,128]{2,1,0:T(8,128)(2,1)S(1)}, u32[]{:S(2)}, u32[]{:S(2)}) collective-permute-start(bf16[2,256,128]{2,1,0:T(8,128)(2,1)S(1)} %get-tuple-element.40), channel_id=1, source_target_pairs={{0,4},{2,6},{4,0},{6,2},{8,12},{10,14},{12,8},{14,10},{16,20},{18,... | collective-permute-start | bytes 393224 | tf_op jit(solution)/shard_map/ppermute | solution.py:29
  59.1 5.6 %collective-permute-start.17 = (bf16[2,256,128]{2,1,0:T(8,128)(2,1)S(1)}, bf16[2,256,128]{2,1,0:T(8,128)(2,1)S(1)}, u32[]{:S(2)}, u32[]{:S(2)}) collective-permute-start(bf16[2,256,128]{2,1,0:T(8,128)(2,1)S(1)} %get-tuple-element.43), channel_id=1, source_target_pairs={{16,0},{18,2},{20,4},{22,6},{24,8},{26,10},{28,12},{30,14},{17,1},... | collective-permute-start | bytes 393224 | tf_op jit(solution)/shard_map/ppermute | solution.py:25
  60.4 13.9 %collective-permute-start.19 = (bf16[2,256,128]{2,1,0:T(8,128)(2,1)S(1)}, bf16[2,256,128]{2,1,0:T(8,128)(2,1)S(1)}, u32[]{:S(2)}, u32[]{:S(2)}) collective-permute-start(bf16[2,256,128]{2,1,0:T(8,128)(2,1)S(1)} %get-tuple-element.44), channel_id=1, source_target_pairs={{8,0},{10,2},{12,4},{14,6},{16,8},{18,10},{20,12},{22,14},{24,16},... | collective-permute-start | bytes 393224 | tf_op jit(solution)/shard_map/ppermute | solution.py:25
where the time goes:
time: 75.4 us; the launch traced here: 75 us
  waiting for transfers between devices  25 us (33%)
  starting transfers between devices  23.7 us (31%)
  Pallas kernels  21 us (28%)
  local copies, waits for them, and re-layouts  4.05 us (5%)
  between operations  0.82 us (1%)
    ppermute x4, waiting for transfers between devices, shifted(): return lax.ppermute(block, 'ctx', route)  14.4 us
    ppermute x13, starting transfers between devices, swapped(): lax.ppermute(block, 'ctx', [(i, i ^ bit) for i in range(lax.axis_size('ct...  12.2 us
    pallas_call x1, Pallas kernels, attend_back(): pl.pallas_call(partial(backward_kernel, heads), out_shape=(jax.ShapeDtype...  8.25 us
    ppermute x13, waiting for transfers between devices, swapped(): lax.ppermute(block, 'ctx', [(i, i ^ bit) for i in range(lax.axis_size('ct...  8.22 us
    ppermute x4, starting transfers between devices, shifted(): return lax.ppermute(block, 'ctx', route)  7.98 us
    pallas_call x2, Pallas kernels, attend(): pl.pallas_call(partial(forward_kernel, heads, planes, last), out_shape=ou...  5.81 us
    ppermute x3, starting transfers between devices, tp_swapped(): return lax.ppermute(block, 'tp', [(0, 1), (1, 0)])  3.58 us
    pallas_call x2, Pallas kernels, project(): pl.pallas_call(partial(project_kernel, tile, pieces), out_shape=(piece,)...  3.57 us
  transfers between devices with their start and end apart: 20, of which 8 were waited for; matrix products, arithmetic and copies ran while one was open for 0% of the time, Pallas kernels for 28%

commit v1 on v0

v1 whole, which is shorter than its diff:
```python
from functools import partial
import math

import jax
import jax.numpy as jnp
from jax import lax
from jax.experimental import pallas as pl
from jax.experimental.pallas import tpu as pltpu
from jax.sharding import PartitionSpec as P

HEAD_WIDTH = 128
REACH = 8
GROUP = 4
BACK = REACH // GROUP
PLANES = BACK + 1
WINDOW = PLANES * GROUP
LOG2_E = math.log2(math.e)
MASKED = -1e30
EXCESS = 64.0
SUM_ROWS = 16
NT = (((1,), (1,)), ((), ()))


def shifted(block, distance):
    size = lax.axis_size("ctx")
    route = [(i, i + distance) for i in range(size) if 0 <= i + distance < size]
    return lax.ppermute(block, "ctx", route)


def swapped(block, bit):
    return lax.ppermute(block, "ctx", [(i, i ^ bit) for i in range(lax.axis_size("ctx"))])


def tp_swapped(block):
    return lax.ppermute(block, "tp", [(0, 1), (1, 0)])


def params(mebibytes):
    return pltpu.CompilerParams(vmem_limit_bytes=mebibytes * 2**20)


def window_slot(block, place):
    plane = BACK - block // GROUP
    half = (block // 2 + place // 2) % 2
    core = (block + place) % 2
    return core, half * PLANES + plane


def doc_rows(lens_ref, first, rows):
    positions = first + lax.broadcasted_iota(jnp.int32, (1, rows), 1)

    def add_doc(doc, carry):
        end, starts, start = carry
        length = lens_ref[doc]
        end = end + length
        return (
            end,
            starts + jnp.where(positions >= end, length, 0),
            start + jnp.where(first >= end, length, 0),
        )

    zero = jnp.int32(0)
    _, starts, start = lax.fori_loop(
        0, lens_ref.shape[0], add_doc, (zero, jnp.zeros((1, rows), jnp.int32), zero)
    )
    return starts, start


def block_bias(block, base, first, starts):
    rows = starts.shape[1]
    key_pos = base + block * rows + lax.broadcasted_iota(jnp.int32, (rows, rows), 0)
    positions = first + lax.broadcasted_iota(jnp.int32, (1, rows), 1)
    return jnp.where((key_pos >= starts) & (key_pos <= positions), 0.0, MASKED).astype(jnp.float32)


def head(h):
    return slice(h * HEAD_WIDTH, (h + 1) * HEAD_WIDTH)


def window_place(rows):
    device = lax.axis_index("ctx")
    place = device % GROUP
    first = device * rows
    base = first - (BACK * GROUP + place) * rows
    return place, first, base


def forward_kernel(heads, planes, last, begin_ref, starts_ref, qt_ref, *rest):
    count = len(planes) * GROUP
    parts, rest = rest[:count], rest[count:]
    if last:
        acc_in, shift_in, win_in = rest[:3]
        out_ref, mass_ref, win_ref, acc_ref, shift_ref, score_ref, prob_ref, most_ref = rest[3:]
    else:
        acc_ref, shift_ref, win_ref, score_ref, prob_ref, most_ref = rest
    rows = qt_ref.shape[2]
    scale = LOG2_E / math.sqrt(HEAD_WIDTH)
    place, first, base = window_place(rows)
    begin = begin_ref[0]
    own = BACK * GROUP + place
    starts = starts_ref[0:1, :]
    in_first = starts <= jnp.min(starts, axis=1, keepdims=True)
    for at, plane in enumerate(planes):
        for way in range(GROUP):
            where = (BACK - plane) * GROUP + (place ^ way)
            win_ref[where] = parts[at * GROUP + way][...]
    if last:
        kept = (BACK + 1 - planes[0]) * GROUP
        win_ref[kept:] = win_in[kept:]

    def values_of(block):
        ones = jnp.ones((SUM_ROWS, rows), jnp.bfloat16)
        return jnp.concatenate([values_turned(win_ref, block), ones], axis=0)

    def weigh(values_t, h):
        return jnp.dot(values_t, prob_ref[h], preferred_element_type=jnp.float32)

    def visit_own():
        keys, values_t = win_ref[own, 0], values_of(own)
        bias = block_bias(own, base, first, starts)
        for h in range(heads):
            score_ref[h] = jnp.dot(keys, qt_ref[h], preferred_element_type=jnp.float32)
        for h in range(heads):
            scores = score_ref[h] * scale + bias
            shift = jnp.max(scores, axis=0, keepdims=True)
            shift_ref[h : h + 1, :] = shift
            prob_ref[h] = jnp.exp2(scores - shift).astype(jnp.bfloat16)
        for h in range(heads):
            acc_ref[h] = weigh(values_t, h)

    def visit(block, masked):
        keys, values_t = win_ref[block, 0], values_of(block)
        if masked:
            bias = block_bias(block, base, first, starts)
        for h in range(heads):
            shift = jnp.where(in_first, shift_ref[h : h + 1, :], -MASKED)
            scores = jnp.dot(keys, qt_ref[h], preferred_element_type=jnp.float32) * scale - shift
            if masked:
                scores = scores + bias
            most_ref[h : h + 1, :] = jnp.maximum(
                most_ref[h : h + 1, :], jnp.max(scores, axis=0, keepdims=True)
            )
            prob_ref[h] = jnp.exp2(scores).astype(jnp.bfloat16)
        for h in range(heads):
            acc_ref[h] += weigh(values_t, h)

    def visit_following(block):
        keys, values_t = win_ref[block, 0], values_of(block)
        bias = block_bias(block, base, first, starts)
        for h in range(heads):
            score_ref[h] = jnp.dot(keys, qt_ref[h], preferred_element_type=jnp.float32)
        for h in range(heads):
            scores = score_ref[h] * scale + bias
            old_shift = shift_ref[h : h + 1, :]
            shift = jnp.maximum(old_shift, jnp.max(scores, axis=0, keepdims=True))
            shift_ref[h : h + 1, :] = shift
            prob_ref[h] = jnp.exp2(scores - shift).astype(jnp.bfloat16)
            acc_ref[h] = acc_ref[h] * jnp.exp2(old_shift - shift)
        for h in range(heads):
            acc_ref[h] += weigh(values_t, h)

    lowest = (BACK - planes[-1]) * GROUP
    end = jnp.minimum(own, (BACK - planes[0] + 1) * GROUP)

    def begin_sums():
        if last:
            acc_ref[...] = acc_in[...]
            shift_ref[...] = shift_in[...]
        else:
            visit_own()

    begin_sums()
    most_ref[...] = jnp.full_like(most_ref, MASKED)

    @pl.when((begin >= lowest) & (begin < end))
    def _():
        visit(begin, True)

    pl.loop(jnp.maximum(begin + 1, lowest), end)(lambda block: visit(block, False))

    @pl.when(jnp.max(most_ref[...]) > EXCESS)
    def _():
        begin_sums()
        pl.loop(jnp.maximum(begin, lowest), end)(visit_following)

    if last:
        for h in range(heads):
            total = acc_ref[h, HEAD_WIDTH : HEAD_WIDTH + 1, :]
            mass_ref[h : h + 1, :] = shift_ref[h : h + 1, :] + jnp.log2(total)
            out_ref[:, head(h)] = (acc_ref[h, :HEAD_WIDTH] / total).T.astype(jnp.bfloat16)


def backward_kernel(
    heads,
    begin_ref,
    starts_ref,
    q_ref,
    qt_ref,
    win_ref,
    att_ref,
    grad_ref,
    grad_t_ref,
    mass_ref,
    dq_ref,
    keep_ref,
    send_ref,
    acc_ref,
    delta_ref,
    wide_mass_ref,
    prob_ref,
    grad_score_ref,
    bias_ref,
):
    rows = q_ref.shape[0]
    score_scale = 1.0 / math.sqrt(HEAD_WIDTH)
    scale = LOG2_E * score_scale
    place, first, base = window_place(rows)
    starts = starts_ref[0:1, :]
    mass_t = mass_ref[...].T
    for h in range(heads):
        product = grad_ref[:, head(h)].astype(jnp.float32) * att_ref[:, head(h)].astype(jnp.float32)
        delta_ref[h] = jnp.broadcast_to(
            jnp.sum(product, axis=1, keepdims=True), (rows, HEAD_WIDTH)
        )
        wide_mass_ref[h] = jnp.broadcast_to(mass_t[:, h : h + 1], (rows, HEAD_WIDTH))
    chunk = HEAD_WIDTH
    own = BACK * GROUP + place

    def across(ref, h, piece):
        return jnp.concatenate([ref[h, piece]] * (rows // HEAD_WIDTH), axis=1)

    def visit(block, own_block):
        keys = win_ref[block, 0]
        keys_t = keys.T
        values_t = values_turned(win_ref, block)
        bias_ref[...] = block_bias(block, base, first, starts).T
        for h in range(heads):
            for at in range(0, rows, chunk):
                piece = slice(at, at + chunk)
                scores = (
                    jnp.dot(q_ref[piece, head(h)], keys_t, preferred_element_type=jnp.float32) * scale
                    + bias_ref[piece]
                )
                prob = jnp.exp2(scores - across(wide_mass_ref, h, piece))
                prob_ref[h, piece] = prob.astype(jnp.bfloat16)
                grad_prob = jnp.dot(
                    grad_ref[piece, head(h)], values_t, preferred_element_type=jnp.float32
                )
                grad_score_ref[h, piece] = (
                    prob * (grad_prob - across(delta_ref, h, piece))
                ).astype(jnp.bfloat16)
        key_grad = jnp.zeros((HEAD_WIDTH, rows), jnp.float32)
        value_grad = jnp.zeros((HEAD_WIDTH, rows), jnp.float32)
        for h in range(heads):
            value_grad = value_grad + jnp.dot(
                grad_t_ref[h], prob_ref[h], preferred_element_type=jnp.float32
            )
        for h in range(heads):
            key_grad = key_grad + jnp.dot(
                qt_ref[h], grad_score_ref[h], preferred_element_type=jnp.float32
            )
        for h in range(heads):
            query_grad = jnp.dot(grad_score_ref[h], keys, preferred_element_type=jnp.float32)
            if own_block:
                acc_ref[h] = query_grad
            else:
                acc_ref[h] += query_grad
        give(block, key_grad * score_scale, value_grad)

    def give(block, key_grad, value_grad):
        core, slot = window_slot(block, place)

        @pl.when(core == 0)
        def _():
            keep_ref[slot, 0] = key_grad
            keep_ref[slot, 1] = value_grad

        @pl.when(core == 1)
        def _():
            send_ref[slot, 0] = key_grad.astype(jnp.bfloat16)
            send_ref[slot, 1] = value_grad.astype(jnp.bfloat16)

    def give_nothing(block):
        none = jnp.zeros((HEAD_WIDTH, rows), jnp.float32)
        give(block, none, none)

    visit(own, True)
    pl.loop(begin_ref[0], own)(lambda block: visit(block, False))
    pl.loop(0, begin_ref[0])(give_nothing)
    pl.loop(own + 1, WINDOW)(give_nothing)
    for h in range(heads):
        dq_ref[:, head(h)] = (acc_ref[h] * score_scale).astype(jnp.bfloat16)


def whole(shape=None):
    return pl.BlockSpec(memory_space=pltpu.VMEM)


SCALARS = pl.BlockSpec(memory_space=pltpu.SMEM)


def attend(prepared, planes, parts, before=()):
    queries_t, starts, begin = prepared
    heads, _, rows = queries_t.shape
    last = len(before) > 0
    visits = len(planes) * GROUP * heads * rows * rows
    sums = [(heads, HEAD_WIDTH + SUM_ROWS, rows), (heads, rows)]
    window = jax.ShapeDtypeStruct((WINDOW, 2, rows, HEAD_WIDTH), jnp.bfloat16)
    working = [
        pltpu.VMEM((heads, rows, rows), jnp.float32),
        pltpu.VMEM((heads, rows, rows), jnp.bfloat16),
        pltpu.VMEM((heads, rows), jnp.float32),
    ]
    if last:
        out_shape = (
            jax.ShapeDtypeStruct((rows, heads * HEAD_WIDTH), jnp.bfloat16),
            jax.ShapeDtypeStruct((heads, rows), jnp.float32),
            window,
        )
        working = [pltpu.VMEM(shape, jnp.float32) for shape in sums] + working
    else:
        out_shape = tuple(jax.ShapeDtypeStruct(shape, jnp.float32) for shape in sums) + (window,)
    return pl.pallas_call(
        partial(forward_kernel, heads, planes, last),
        out_shape=out_shape,
        in_specs=[SCALARS] + [whole()] * (2 + len(parts) + len(before)),
        out_specs=(whole(),) * len(out_shape),
        scratch_shapes=working,
        compiler_params=params(12),
        cost_estimate=pl.CostEstimate(
            flops=4 * visits * HEAD_WIDTH, bytes_accessed=4 * 2**20, transcendentals=visits
        ),
        name="attend",
    )(begin, starts, queries_t, *parts, *before)


def prepare_kernel(lens_ref, wide_ref, out_ref, starts_ref, begin_ref):
    rows = wide_ref.shape[0]
    _, first, base = window_place(rows)
    starts, start = doc_rows(lens_ref, first, rows)
    starts_ref[...] = jnp.broadcast_to(starts, starts_ref.shape)
    begin_ref[0] = (start - base) // rows
    transpose_heads(wide_ref, out_ref)


def prepare(doc_lengths, queries):
    rows, width = queries.shape
    return pl.pallas_call(
        prepare_kernel,
        out_shape=(
            jax.ShapeDtypeStruct((width // HEAD_WIDTH, HEAD_WIDTH, rows), queries.dtype),
            jax.ShapeDtypeStruct((8, rows), jnp.int32),
            jax.ShapeDtypeStruct((1,), jnp.int32),
        ),
        in_specs=[SCALARS, whole()],
        out_specs=(whole(), whole(), SCALARS),
        compiler_params=params(4),
        name="prepare",
    )(doc_lengths, queries)


def attend_back(prepared, queries, window, attention, grad, grad_t, mass):
    queries_t, starts, begin = prepared
    rows, width = queries.shape
    heads = width // HEAD_WIDTH
    visits = (REACH + 1) * heads * rows * rows
    parts_shape = (2 * PLANES, 2, HEAD_WIDTH, rows)
    return pl.pallas_call(
        partial(backward_kernel, heads),
        out_shape=(
            jax.ShapeDtypeStruct((rows, width), jnp.bfloat16),
            jax.ShapeDtypeStruct(parts_shape, jnp.float32),
            jax.ShapeDtypeStruct(parts_shape, jnp.bfloat16),
        ),
        in_specs=[SCALARS] + [whole()] * 8,
        out_specs=(whole(), whole(), whole()),
        scratch_shapes=[
            pltpu.VMEM((heads, rows, HEAD_WIDTH), jnp.float32),
            pltpu.VMEM((heads, rows, HEAD_WIDTH), jnp.float32),
            pltpu.VMEM((heads, rows, HEAD_WIDTH), jnp.float32),
            pltpu.VMEM((heads, rows, rows), jnp.bfloat16),
            pltpu.VMEM((heads, rows, rows), jnp.bfloat16),
            pltpu.VMEM((rows, rows), jnp.float32),
        ],
        compiler_params=params(16),
        cost_estimate=pl.CostEstimate(
            flops=10 * visits * HEAD_WIDTH, bytes_accessed=8 * 2**20, transcendentals=visits
        ),
        name="attend_back",
    )(begin, starts, queries, queries_t, window, attention, grad, grad_t, mass)


def pair_kernel(keys_ref, values_ref, out_ref):
    out_ref[0] = keys_ref[...]
    turned = values_ref[...].T
    for at in range(0, turned.shape[1], HEAD_WIDTH):
        out_ref[1, at : at + HEAD_WIDTH] = turned[:, at : at + HEAD_WIDTH]


def pair_up(keys, values):
    return pl.pallas_call(
        pair_kernel,
        out_shape=jax.ShapeDtypeStruct((2,) + keys.shape, keys.dtype),
        in_specs=[whole()] * 2,
        out_specs=whole(),
        compiler_params=params(4),
        name="pair_up",
    )(keys, values)


def values_turned(win_ref, block):
    rows = win_ref.shape[2]
    return jnp.concatenate(
        [win_ref[block, 1, at : at + HEAD_WIDTH] for at in range(0, rows, HEAD_WIDTH)], axis=1
    )


def finish_kernel(keep_ref, received_ref, *rest):
    others, outs = rest[:-2], rest[-2:]
    for kind, out_ref in enumerate(outs):
        total = keep_ref[0, kind] + received_ref[0, kind].astype(jnp.float32)
        for other in others:
            total = total + other[kind].astype(jnp.float32)
        out_ref[...] = total.T.astype(jnp.bfloat16)


def finish(keep, received, others):
    _, _, width, rows = keep.shape
    out = jax.ShapeDtypeStruct((rows, width), jnp.bfloat16)
    return pl.pallas_call(
        finish_kernel,
        out_shape=(out, out),
        in_specs=[whole()] * (2 + len(others)),
        out_specs=(whole(), whole()),
        compiler_params=params(4),
        name="finish",
    )(keep, received, *others)


def project_kernel(tile, pieces, half_ref, att_ref, weight_ref, *rest):
    others, outs = rest[: len(rest) - pieces], rest[len(rest) - pieces :]
    columns = weight_ref.shape[1] // 2
    at = 0
    for part in others or outs:
        for there in range(0, part.shape[1], tile):
            piece = pl.ds(pl.multiple_of(half_ref[0] * columns + at, tile), tile)
            total = jnp.dot(
                att_ref[...], weight_ref[:, piece], preferred_element_type=jnp.float32
            ).astype(jnp.bfloat16)
            if others:
                other = part[:, there : there + tile].astype(jnp.float32)
                total = (total.astype(jnp.float32) + other).astype(jnp.bfloat16)
                outs[0][:, at : at + tile] = total
            else:
                part[:, there : there + tile] = total
            at += tile


def project(half, attention, weight, *other, eighths=(8,)):
    rows, depth = attention.shape
    columns = weight.shape[1] // 2
    tile = columns // 8
    pieces = len(eighths)
    shapes = [(rows, columns * part // 8) for part in eighths]
    return pl.pallas_call(
        partial(project_kernel, tile, pieces),
        out_shape=tuple(jax.ShapeDtypeStruct(shape, jnp.bfloat16) for shape in shapes),
        in_specs=[SCALARS] + [whole()] * (2 + len(other)),
        out_specs=(whole(),) * pieces,
        compiler_params=params(8),
        cost_estimate=pl.CostEstimate(
            flops=2 * rows * depth * columns, bytes_accessed=2 * depth * columns, transcendentals=0
        ),
        name="project",
    )(half, attention, weight, *other)


def transpose_heads(wide_ref, out_ref):
    for h in range(out_ref.shape[0]):
        out_ref[h] = wide_ref[:, head(h)].T


def grad_kernel(tile, order_ref, *refs):
    halves, (weight_ref, out_ref, out_t_ref) = refs[:2], refs[2:]
    columns = halves[0].shape[1]
    for at in range(0, weight_ref.shape[0], tile):
        total = 0.0
        for side, cot_ref in enumerate(halves):
            piece = pl.ds(pl.multiple_of(order_ref[side] * columns, columns), columns)
            total += lax.dot_general(
                cot_ref[...], weight_ref[at : at + tile, piece], NT, preferred_element_type=jnp.float32
            )
        out_ref[:, at : at + tile] = total.astype(jnp.bfloat16)
    transpose_heads(out_ref, out_t_ref)


def attention_grad(order, halves, weight, tile=256):
    rows, columns = halves[0].shape
    depth = weight.shape[0]
    return pl.pallas_call(
        partial(grad_kernel, tile),
        out_shape=(
            jax.ShapeDtypeStruct((rows, depth), jnp.bfloat16),
            jax.ShapeDtypeStruct((depth // HEAD_WIDTH, HEAD_WIDTH, rows), jnp.bfloat16),
        ),
        in_specs=[SCALARS] + [whole()] * 3,
        out_specs=(whole(), whole()),
        compiler_params=params(8),
        cost_estimate=pl.CostEstimate(
            flops=4 * rows * depth * columns, bytes_accessed=4 * depth * columns, transcendentals=0
        ),
        name="attention_grad",
    )(order, *halves, weight)


def body(queries, keys, values, out_weight, cotangent, doc_lengths):
    mine = lax.axis_index("tp").astype(jnp.int32).reshape(1)
    theirs = 1 - mine
    order = jnp.concatenate([mine, theirs])
    pair = pair_up(keys, values)
    other_cot = tp_swapped(cotangent)
    planes = [pair] + [shifted(pair, plane * GROUP) for plane in range(1, PLANES)]
    prepared = prepare(doc_lengths, queries)
    planes[BACK], *prepared = lax.optimization_barrier((planes[BACK], *prepared))

    def group_of(block):
        half = swapped(block, 2)
        return [block, swapped(block, 1), half, swapped(half, 1)]

    def last_group_of(block):
        pairs = [block, swapped(block, 1)]
        return pairs + [swapped(each, 2) for each in pairs]

    groups = [group_of(block) for block in planes[:BACK]] + [last_group_of(planes[BACK])]
    early = tuple(range(BACK))
    sums = attend(prepared, early, sum((groups[plane] for plane in early), []))
    attention, mass, window = attend(prepared, (BACK,), groups[BACK], sums)
    other_terms = project(theirs, attention, out_weight, eighths=(5, 3))
    early_mixed = tp_swapped(other_terms[0])
    other_cot, other_terms = lax.optimization_barrier((other_cot, other_terms))
    grad, grad_t = attention_grad(order, (cotangent, other_cot), out_weight)
    query_grad, keep, send = attend_back(
        prepared, queries, window, attention, grad, grad_t, mass
    )
    send, early_mixed = lax.optimization_barrier((send, early_mixed))
    late_mixed = tp_swapped(other_terms[1])
    received = swapped(send, 1)

    def core_sum(slots):
        return keep[slots] + received[slots].astype(jnp.float32)

    crossed = {}
    for plane in reversed(range(PLANES)):
        crossed[plane] = swapped(core_sum(PLANES + plane).astype(jnp.bfloat16), 2)
    arrived = []
    for plane in range(1, PLANES):
        half_sum = core_sum(plane) + crossed[plane].astype(jnp.float32)
        arrived.append(shifted(half_sum.astype(jnp.bfloat16), -plane * GROUP))
    (mixed_out,) = project(mine, attention, out_weight, early_mixed, late_mixed)
    keys_gradient, values_gradient = finish(keep, received, [crossed[0]] + arrived)
    return (mixed_out, query_grad, keys_gradient, values_gradient)


def solution(mesh):
    in_specs = (P("ctx", "tp"), P("ctx", "tp"), P("ctx", "tp"), P("tp", None), P("ctx", "tp"), P())
    out_specs = (P("ctx", "tp"), P("ctx", "tp"), P("ctx", "tp"), P("ctx", "tp"))
    return jax.shard_map(body, mesh=mesh, in_specs=in_specs, out_specs=out_specs, check_vma=False)
```

time: 75.4 us -> 71.8 us (0.952)
  the two profiles are of different devices: /device:TPU:16 before, /device:TPU:0 now
where the time goes in v1:
time: 71.8 us; the launch traced here: 71.4 us
  waiting for transfers between devices  27.6 us (38%)
  starting transfers between devices  23.3 us (32%)
  Pallas kernels  16.1 us (22%)
  local copies, waits for them, and re-layouts  3.39 us (5%)
  between operations  0.77 us (1%)
    ppermute x13, waiting for transfers between devices, swapped(): lax.ppermute(block, 'ctx', [(i, i ^ bit) for i in range(lax.axis_size('ct...  14.1 us
    ppermute x4, starting transfers between devices, shifted(): return lax.ppermute(block, 'ctx', route)  10.6 us
    ppermute x3, waiting for transfers between devices, tp_swapped(): return lax.ppermute(block, 'tp', [(0, 1), (1, 0)])  9.41 us
    ppermute x13, starting transfers between devices, swapped(): lax.ppermute(block, 'ctx', [(i, i ^ bit) for i in range(lax.axis_size('ct...  8.56 us
    ppermute x3, starting transfers between devices, tp_swapped(): return lax.ppermute(block, 'tp', [(0, 1), (1, 0)])  4.14 us
    pallas_call x1, Pallas kernels, attend_back(): pl.pallas_call(partial(backward_kernel, heads), out_shape=(jax.ShapeDtype...  4.11 us
    ppermute x4, waiting for transfers between devices, shifted(): return lax.ppermute(block, 'ctx', route)  4.04 us
    pallas_call x2, Pallas kernels, project(): pl.pallas_call(partial(project_kernel, tile, pieces), out_shape=tuple((ja...  3.62 us
  transfers between devices with their start and end apart: 20, of which 11 were waited for; matrix products, arithmetic and copies ran while one was open for 0% of the time, Pallas kernels for 21%

profile of v1, /device:TPU:0, one launch (start us, length us, event | category | flops | bytes accessed | tf_op | source)
XLA Modules:
  0.0 71.4 jit_solution(15221657243137097266)
XLA Ops:
  0.6 3.0 %collective-permute-start.11 = (bf16[256,2048]{1,0:T(8,128)(2,1)}, bf16[256,2048]{1,0:T(8,128)(2,1)S(1)}, u32[]{:S(2)}, u32[]{:S(2)}) collective-permute-start(bf16[256,2048]{1,0:T(8,128)(2,1)} %refs_0_.1), channel_id=1, source_target_pairs={{0,1},{1,0},{2,3},{3,2},{4,5},{5,4},{6,7},{7,6},{8,9},{9,8},{10,11... | collective-permute-start | bytes 3145736 | tf_op jit(solution)/shard_map/ppermute | solution.py:35
  3.6 0.8 %copy-done.4 = bf16[256,128]{1,0:T(8,128)(2,1)S(1)} copy-done((bf16[256,128]{1,0:T(8,128)(2,1)S(1)}, bf16[256,128]{1,0:T(8,128)(2,1)}, u32[]{:S(2)}) %copy-start.4) | copy-done | bytes 65560
  4.5 0.8 %copy-done.5 = bf16[256,128]{1,0:T(8,128)(2,1)S(1)} copy-done((bf16[256,128]{1,0:T(8,128)(2,1)S(1)}, bf16[256,128]{1,0:T(8,128)(2,1)}, u32[]{:S(2)}) %copy-start.5) | copy-done | bytes 65560
  5.4 3.5 %collective-permute-start.7 = (bf16[2,256,128]{2,1,0:T(8,128)(2,1)S(1)}, bf16[2,256,128]{2,1,0:T(8,128)(2,1)S(1)}, u32[]{:S(2)}, u32[]{:S(2)}) collective-permute-start(bf16[2,256,128]{2,1,0:T(8,128)(2,1)S(1)} %pair_up.1.rest_0_), channel_id=1, source_target_pairs={{0,8},{2,10},{4,12},{6,14},{8,16},{10,18},{12,20},{14,22},{16,24},... | collective-permute-start | bytes 393224 | tf_op jit(solution)/shard_map/ppermute | solution.py:27
  8.9 4.5 %collective-permute-start = (bf16[2,256,128]{2,1,0:T(8,128)(2,1)S(1)}, bf16[2,256,128]{2,1,0:T(8,128)(2,1)S(1)}, u32[]{:S(2)}, u32[]{:S(2)}) collective-permute-start(bf16[2,256,128]{2,1,0:T(8,128)(2,1)S(1)} %pair_up.1.rest_0_), channel_id=1, source_target_pairs={{0,16},{2,18},{4,20},{6,22},{8,24},{10,26},{12,28},{14,30},{1,17},... | collective-permute-start | bytes 393224 | tf_op jit(solution)/shard_map/ppermute | solution.py:27
  13.4 1.6 %collective-permute-start.5 = (bf16[2,256,128]{2,1,0:T(8,128)(2,1)S(1)}, bf16[2,256,128]{2,1,0:T(8,128)(2,1)S(1)}, u32[]{:S(2)}, u32[]{:S(2)}) collective-permute-start(bf16[2,256,128]{2,1,0:T(8,128)(2,1)S(1)} %pair_up.1.rest_0_), channel_id=1, source_target_pairs={{0,4},{2,6},{4,0},{6,2},{8,12},{10,14},{12,8},{14,10},{16,20},{18,... | collective-permute-start | bytes 393224 | tf_op jit(solution)/shard_map/ppermute | solution.py:31
  15.5 1.0 %copy-done.2 = bf16[256,1024]{1,0:T(8,128)(2,1)S(1)} copy-done((bf16[256,1024]{1,0:T(8,128)(2,1)S(1)}, bf16[256,1024]{1,0:T(8,128)(2,1)}, u32[]{:S(2)}) %copy-start.2) | copy-done | bytes 524312
  16.5 0.7 copy-done.6
  17.2 1.1 %prepare.1 = (bf16[8,128,256]{2,1,0:T(8,128)(2,1)S(1)}, s32[8,256]{1,0:T(8,128)S(1)}, s32[1]{0:T(128)}) custom-call(s32[8]{0:T(128)S(1)} %copy-done.6, bf16[256,1024]{1,0:T(8,128)(2,1)S(1)} %copy-done.2), custom_call_target="tpu_custom_call" | custom-call | tf_op jit(solution)/shard_map/prepare/pallas_call | solution.py:348
  19.3 1.9 %collective-permute-done.9.rest_6_ = bf16[2,256,128]{2,1,0:T(8,128)(2,1)S(1)} collective-permute-done((bf16[2,256,128]{2,1,0:T(8,128)(2,1)S(1)}, bf16[2,256,128]{2,1,0:T(8,128)(2,1)S(1)}, u32[]{:S(2)}, u32[]{:S(2)}) %collective-permute-start.9) | collective-permute-done | bytes 131104 | tf_op jit(solution)/shard_map/ppermute | solution.py:31
  21.3 1.5 %collective-permute-start.2 = (bf16[2,256,128]{2,1,0:T(8,128)(2,1)S(1)}, bf16[2,256,128]{2,1,0:T(8,128)(2,1)S(1)}, u32[]{:S(2)}, u32[]{:S(2)}) collective-permute-start(bf16[2,256,128]{2,1,0:T(8,128)(2,1)S(1)} %collective-permute-done.rest_0_), channel_id=1, source_target_pairs={{0,4},{2,6},{4,0},{6,2},{8,12},{10,14},{12,8},{14,10},{16,20},{18,... | collective-permute-start | bytes 393224 | tf_op jit(solution)/shard_map/ppermute | solution.py:31
  23.4 1.9 %attend.2 = (f32[8,144,256]{2,1,0:T(8,128)S(1)}, f32[8,256]{1,0:T(8,128)S(1)}, bf16[12,2,256,128]{3,2,1,0:T(8,128)(2,1)S(1)}) custom-call(s32[1]{0:T(128)} %get-tuple-element.33.begin_ref, s32[8,256]{1,0:T(8,128)S(1)} %get-tuple-element.34.starts_ref, bf16[8,128,256]{2,1,0:T(8,128)(2,1)S(1)} %get-tuple-element.35.qt_ref, ...), custom_call_target="tpu_custom_call" | custom-call | flops 2147483648 | bytes 4194304 | tf_op jit(solution)/shard_map/attend/pallas_call | solution.py:323
  25.3 2.3 %collective-permute-done.2.rest_2_ = bf16[2,256,128]{2,1,0:T(8,128)(2,1)S(1)} collective-permute-done((bf16[2,256,128]{2,1,0:T(8,128)(2,1)S(1)}, bf16[2,256,128]{2,1,0:T(8,128)(2,1)S(1)}, u32[]{:S(2)}, u32[]{:S(2)}) %collective-permute-start.2) | collective-permute-done | bytes 131104 | tf_op jit(solution)/shard_map/ppermute | solution.py:31
  27.6 2.4 %collective-permute-done.3.rest_3_ = bf16[2,256,128]{2,1,0:T(8,128)(2,1)S(1)} collective-permute-done((bf16[2,256,128]{2,1,0:T(8,128)(2,1)S(1)}, bf16[2,256,128]{2,1,0:T(8,128)(2,1)S(1)}, u32[]{:S(2)}, u32[]{:S(2)}) %collective-permute-start.3) | collective-permute-done | bytes 131104 | tf_op jit(solution)/shard_map/ppermute | solution.py:31
  30.0 1.4 %attend.3 = (bf16[256,1024]{1,0:T(8,128)(2,1)S(1)}, f32[8,256]{1,0:T(8,128)S(1)}, bf16[12,2,256,128]{3,2,1,0:T(8,128)(2,1)S(1)}) custom-call(s32[1]{0:T(128)} %get-tuple-element.33.begin_ref, s32[8,256]{1,0:T(8,128)S(1)} %get-tuple-element.34.starts_ref, bf16[8,128,256]{2,1,0:T(8,128)(2,1)S(1)} %get-tuple-element.35.qt_ref, ...), custom_call_target="tpu_custom_call" | custom-call | flops 1073741824 | bytes 4194304 | tf_op jit(solution)/shard_map/attend/pallas_call | solution.py:323
  31.5 1.3 %project.2 = (bf16[256,1280]{1,0:T(8,128)(2,1)S(1)}, bf16[256,768]{1,0:T(8,128)(2,1)S(1)}) custom-call(s32[1]{0:T(128)S(6)} %sub.3.half_ref, bf16[256,1024]{1,0:T(8,128)(2,1)S(1)} %get-tuple-element.40.att_ref, bf16[1024,4096]{1,0:T(8,128)(2,1)S(1)} %copy-done), custom_call_target="tpu_custom_call" | custom-call | flops 1073741824 | bytes 4194304 | tf_op jit(solution)/shard_map/project/pallas_call | solution.py:465
  32.8 0.6 collective-permute-start.12
  33.4 3.1 %attention_grad.1 = (bf16[256,1024]{1,0:T(8,128)(2,1)S(1)}, bf16[8,128,256]{2,1,0:T(8,128)(2,1)S(1)}) custom-call(s32[2]{0:T(128)S(1)} %pad_add_fusion.order_ref, bf16[256,2048]{1,0:T(8,128)(2,1)S(1)} %copy-done.1, bf16[256,2048]{1,0:T(8,128)(2,1)S(1)} %collective-permute-done.11.refs_1_, bf16[1024,4096]{1,0:T(8,128)(2,1)S(1)} %copy-done), custom_call_target="tpu_custom_call" | custom-call | flops 2147483648 | bytes 8388608 | tf_op jit(solution)/shard_map/attention_grad/pallas_call | solution.py:500
  36.5 4.1 %attend_back.1 = (bf16[256,1024]{1,0:T(8,128)(2,1)}, f32[6,2,128,256]{3,2,1,0:T(8,128)S(1)}, bf16[6,2,128,256]{3,2,1,0:T(8,128)(2,1)S(1)}) custom-call(s32[1]{0:T(128)} %get-tuple-element.33.begin_ref, s32[8,256]{1,0:T(8,128)S(1)} %get-tuple-element.34.starts_ref, bf16[256,1024]{1,0:T(8,128)(2,1)S(1)} %copy-done.3, ...), custom_call_target="tpu_custom_call" | custom-call | flops 6039797760 | bytes 8388608 | tf_op jit(solution)/shard_map/attend_back/pallas_call | solution.py:368
  40.6 8.6 %collective-permute-done.12.rest_0_ = bf16[256,1280]{1,0:T(8,128)(2,1)S(1)} collective-permute-done((bf16[256,1280]{1,0:T(8,128)(2,1)S(1)}, bf16[256,1280]{1,0:T(8,128)(2,1)S(1)}, u32[]{:S(2)}, u32[]{:S(2)}) %collective-permute-start.12) | collective-permute-done | bytes 655392 | tf_op jit(solution)/shard_map/ppermute | solution.py:35
  49.2 2.3 %collective-permute-done.14.received_ref = bf16[6,2,128,256]{3,2,1,0:T(8,128)(2,1)S(1)} collective-permute-done((bf16[6,2,128,256]{3,2,1,0:T(8,128)(2,1)S(1)}, bf16[6,2,128,256]{3,2,1,0:T(8,128)(2,1)S(1)}, u32[]{:S(2)}, u32[]{:S(2)}) %collective-permute-start.14) | collective-permute-done | bytes 786464 | tf_op jit(solution)/shard_map/ppermute | solution.py:31
  51.6 1.6 %collective-permute-start.18 = (bf16[2,128,256]{2,1,0:T(8,128)(2,1)S(1)}, bf16[2,128,256]{2,1,0:T(8,128)(2,1)S(1)}, u32[]{:S(2)}, u32[]{:S(2)}) collective-permute-start(bf16[2,128,256]{2,1,0:T(8,128)(2,1)S(1)} %get-tuple-element.58), channel_id=1, source_target_pairs={{0,4},{2,6},{4,0},{6,2},{8,12},{10,14},{12,8},{14,10},{16,20},{18,... | collective-permute-start | bytes 393224 | tf_op jit(solution)/shard_map/ppermute | solution.py:31
  53.7 0.5 collective-permute-start.13
  54.2 1.5 %collective-permute-start.15 = (bf16[2,128,256]{2,1,0:T(8,128)(2,1)S(1)}, bf16[2,128,256]{2,1,0:T(8,128)(2,1)S(1)}, u32[]{:S(2)}, u32[]{:S(2)}) collective-permute-start(bf16[2,128,256]{2,1,0:T(8,128)(2,1)S(1)} %get-tuple-element.60), channel_id=1, source_target_pairs={{0,4},{2,6},{4,0},{6,2},{8,12},{10,14},{12,8},{14,10},{16,20},{18,... | collective-permute-start | bytes 393224 | tf_op jit(solution)/shard_map/ppermute | solution.py:31
  55.8 2.2 %collective-permute-done.18 = bf16[2,128,256]{2,1,0:T(8,128)(2,1)S(1)} collective-permute-done((bf16[2,128,256]{2,1,0:T(8,128)(2,1)S(1)}, bf16[2,128,256]{2,1,0:T(8,128)(2,1)S(1)}, u32[]{:S(2)}, u32[]{:S(2)}) %collective-permute-start.18) | collective-permute-done | bytes 131104 | tf_op jit(solution)/shard_map/ppermute | solution.py:31
  58.0 2.8 %collective-permute-done.16 = bf16[2,128,256]{2,1,0:T(8,128)(2,1)S(1)} collective-permute-done((bf16[2,128,256]{2,1,0:T(8,128)(2,1)S(1)}, bf16[2,128,256]{2,1,0:T(8,128)(2,1)S(1)}, u32[]{:S(2)}, u32[]{:S(2)}) %collective-permute-start.16) | collective-permute-done | bytes 131104 | tf_op jit(solution)/shard_map/ppermute | solution.py:31
  60.9 1.3 %collective-permute-start.19 = (bf16[2,128,256]{2,1,0:T(8,128)(2,1)S(1)}, bf16[2,128,256]{2,1,0:T(8,128)(2,1)S(1)}, u32[]{:S(2)}, u32[]{:S(2)}) collective-permute-start(bf16[2,128,256]{2,1,0:T(8,128)(2,1)S(1)} %get-tuple-element.56), channel_id=1, source_target_pairs={{16,0},{18,2},{20,4},{22,6},{24,8},{26,10},{28,12},{30,14},{17,1},... | collective-permute-start | bytes 393224 | tf_op jit(solution)/shard_map/ppermute | solution.py:27
  62.2 1.3 %collective-permute-start.17 = (bf16[2,128,256]{2,1,0:T(8,128)(2,1)S(1)}, bf16[2,128,256]{2,1,0:T(8,128)(2,1)S(1)}, u32[]{:S(2)}, u32[]{:S(2)}) collective-permute-start(bf16[2,128,256]{2,1,0:T(8,128)(2,1)S(1)} %get-tuple-element.57), channel_id=1, source_target_pairs={{8,0},{10,2},{12,4},{14,6},{16,8},{18,10},{20,12},{22,14},{24,16},... | collective-permute-start | bytes 393224 | tf_op jit(solution)/shard_map/ppermute | solution.py:27
  63.5 0.8 %collective-permute-done.13.rest_1_ = bf16[256,768]{1,0:T(8,128)(2,1)S(1)} collective-permute-done((bf16[256,768]{1,0:T(8,128)(2,1)S(1)}, bf16[256,768]{1,0:T(8,128)(2,1)S(1)}, u32[]{:S(2)}, u32[]{:S(2)}) %collective-permute-start.13) | collective-permute-done | bytes 393248 | tf_op jit(solution)/shard_map/ppermute | solution.py:35
  64.3 2.3 %project.3 = bf16[256,2048]{1,0:T(8,128)(2,1)} custom-call(s32[1]{0:T(128)} %bitcast.half_ref, bf16[256,1024]{1,0:T(8,128)(2,1)S(1)} %get-tuple-element.40.att_ref, bf16[1024,4096]{1,0:T(8,128)(2,1)S(1)} %copy-done, bf16[256,1280]{1,0:T(8,128)(2,1)S(1)} %collective-permute-done.12.rest_0_, bf16[256,768]{1,0:T(8,128)(2,1)S(1)} %collective-permute-done.13.rest_1_), custom_call_target="tpu_custom_call" | custom-call | flops 1073741824 | bytes 4194304 | tf_op jit(solution)/shard_map/project/pallas_call | solution.py:465
  66.6 3.9 %collective-permute-done.19.rest_2_ = bf16[2,128,256]{2,1,0:T(8,128)(2,1)S(1)} collective-permute-done((bf16[2,128,256]{2,1,0:T(8,128)(2,1)S(1)}, bf16[2,128,256]{2,1,0:T(8,128)(2,1)S(1)}, u32[]{:S(2)}, u32[]{:S(2)}) %collective-permute-start.19) | collective-permute-done | bytes 131104 | tf_op jit(solution)/shard_map/ppermute | solution.py:27
  70.6 0.8 %finish.1 = (bf16[256,128]{1,0:T(8,128)(2,1)}, bf16[256,128]{1,0:T(8,128)(2,1)}) custom-call(f32[6,2,128,256]{3,2,1,0:T(8,128)S(1)} %get-tuple-element.52.keep_ref, bf16[6,2,128,256]{3,2,1,0:T(8,128)(2,1)S(1)} %collective-permute-done.14.received_ref, bf16[2,128,256]{2,1,0:T(8,128)(2,1)S(1)} %collective-permute-done.15.rest_0_, ...), custom_call_target="tpu_custom_call" | custom-call | tf_op jit(solution)/shard_map/finish/pallas_call | solution.py:430
  (34 shorter events, 3.0 us)
Async XLA Ops:
  0.6 32.8 %collective-permute-start.11 = (bf16[256,2048]{1,0:T(8,128)(2,1)}, bf16[256,2048]{1,0:T(8,128)(2,1)S(1)}, u32[]{:S(2)}, u32[]{:S(2)}) collective-permute-start(bf16[256,2048]{1,0:T(8,128)(2,1)} %refs_0_.1), channel_id=1, source_target_pairs={{0,1},{1,0},{2,3},{3,2},{4,5},{5,4},{6,7},{7,6},{8,9},{9,8},{10,11... | collective-permute-start | bytes 3145736 | tf_op jit(solution)/shard_map/ppermute | solution.py:35
  3.6 0.8 %copy-start.4 = (bf16[256,128]{1,0:T(8,128)(2,1)S(1)}, bf16[256,128]{1,0:T(8,128)(2,1)}, u32[]{:S(2)}) copy-start(bf16[256,128]{1,0:T(8,128)(2,1)} %keys_ref.1) | copy-start | bytes 196612
  4.5 0.8 %copy-start.5 = (bf16[256,128]{1,0:T(8,128)(2,1)S(1)}, bf16[256,128]{1,0:T(8,128)(2,1)}, u32[]{:S(2)}) copy-start(bf16[256,128]{1,0:T(8,128)(2,1)} %values_ref.1) | copy-start | bytes 196612
  5.4 9.6 %collective-permute-start.7 = (bf16[2,256,128]{2,1,0:T(8,128)(2,1)S(1)}, bf16[2,256,128]{2,1,0:T(8,128)(2,1)S(1)}, u32[]{:S(2)}, u32[]{:S(2)}) collective-permute-start(bf16[2,256,128]{2,1,0:T(8,128)(2,1)S(1)} %pair_up.1.rest_0_), channel_id=1, source_target_pairs={{0,8},{2,10},{4,12},{6,14},{8,16},{10,18},{12,20},{14,22},{16,24},... | collective-permute-start | bytes 393224 | tf_op jit(solution)/shard_map/ppermute | solution.py:27
  8.9 9.5 %collective-permute-start = (bf16[2,256,128]{2,1,0:T(8,128)(2,1)S(1)}, bf16[2,256,128]{2,1,0:T(8,128)(2,1)S(1)}, u32[]{:S(2)}, u32[]{:S(2)}) collective-permute-start(bf16[2,256,128]{2,1,0:T(8,128)(2,1)S(1)} %pair_up.1.rest_0_), channel_id=1, source_target_pairs={{0,16},{2,18},{4,20},{6,22},{8,24},{10,26},{12,28},{14,30},{1,17},... | collective-permute-start | bytes 393224 | tf_op jit(solution)/shard_map/ppermute | solution.py:27
  13.4 5.4 %collective-permute-start.5 = (bf16[2,256,128]{2,1,0:T(8,128)(2,1)S(1)}, bf16[2,256,128]{2,1,0:T(8,128)(2,1)S(1)}, u32[]{:S(2)}, u32[]{:S(2)}) collective-permute-start(bf16[2,256,128]{2,1,0:T(8,128)(2,1)S(1)} %pair_up.1.rest_0_), channel_id=1, source_target_pairs={{0,4},{2,6},{4,0},{6,2},{8,12},{10,14},{12,8},{14,10},{16,20},{18,... | collective-permute-start | bytes 393224 | tf_op jit(solution)/shard_map/ppermute | solution.py:31
  15.0 4.0 %collective-permute-start.4 = (bf16[2,256,128]{2,1,0:T(8,128)(2,1)S(1)}, bf16[2,256,128]{2,1,0:T(8,128)(2,1)S(1)}, u32[]{:S(2)}, u32[]{:S(2)}) collective-permute-start(bf16[2,256,128]{2,1,0:T(8,128)(2,1)S(1)} %pair_up.1.rest_0_), channel_id=1, source_target_pairs={{0,2},{2,0},{4,6},{6,4},{8,10},{10,8},{12,14},{14,12},{16,18},{18,... | collective-permute-start | bytes 393224 | tf_op jit(solution)/shard_map/ppermute | solution.py:31
  15.0 6.3 %collective-permute-start.9 = (bf16[2,256,128]{2,1,0:T(8,128)(2,1)S(1)}, bf16[2,256,128]{2,1,0:T(8,128)(2,1)S(1)}, u32[]{:S(2)}, u32[]{:S(2)}) collective-permute-start(bf16[2,256,128]{2,1,0:T(8,128)(2,1)S(1)} %collective-permute-done.7.rest_4_), channel_id=1, source_target_pairs={{0,4},{2,6},{4,0},{6,2},{8,12},{10,14},{12,8},{14,10},{16,20},{18,... | collective-permute-start | bytes 393224 | tf_op jit(solution)/shard_map/ppermute | solution.py:31
  15.5 1.0 %copy-start.2 = (bf16[256,1024]{1,0:T(8,128)(2,1)S(1)}, bf16[256,1024]{1,0:T(8,128)(2,1)}, u32[]{:S(2)}) copy-start(bf16[256,1024]{1,0:T(8,128)(2,1)} %q_ref.1) | copy-start | bytes 1572868
  16.5 0.7 copy-start.6
  18.4 3.0 %collective-permute-start.8 = (bf16[2,256,128]{2,1,0:T(8,128)(2,1)S(1)}, bf16[2,256,128]{2,1,0:T(8,128)(2,1)S(1)}, u32[]{:S(2)}, u32[]{:S(2)}) collective-permute-start(bf16[2,256,128]{2,1,0:T(8,128)(2,1)S(1)} %collective-permute-done.7.rest_4_), channel_id=1, source_target_pairs={{0,2},{2,0},{4,6},{6,4},{8,10},{10,8},{12,14},{14,12},{16,18},{18,... | collective-permute-start | bytes 393224 | tf_op jit(solution)/shard_map/ppermute | solution.py:31
  18.8 4.0 %collective-permute-start.1 = (bf16[2,256,128]{2,1,0:T(8,128)(2,1)S(1)}, bf16[2,256,128]{2,1,0:T(8,128)(2,1)S(1)}, u32[]{:S(2)}, u32[]{:S(2)}) collective-permute-start(bf16[2,256,128]{2,1,0:T(8,128)(2,1)S(1)} %collective-permute-done.rest_0_), channel_id=1, source_target_pairs={{0,2},{2,0},{4,6},{6,4},{8,10},{10,8},{12,14},{14,12},{16,18},{18,... | collective-permute-start | bytes 393224 | tf_op jit(solution)/shard_map/ppermute | solution.py:31
  18.9 4.4 %collective-permute-start.6 = (bf16[2,256,128]{2,1,0:T(8,128)(2,1)S(1)}, bf16[2,256,128]{2,1,0:T(8,128)(2,1)S(1)}, u32[]{:S(2)}, u32[]{:S(2)}) collective-permute-start(bf16[2,256,128]{2,1,0:T(8,128)(2,1)S(1)} %collective-permute-done.5.rest_2_), channel_id=1, source_target_pairs={{0,2},{2,0},{4,6},{6,4},{8,10},{10,8},{12,14},{14,12},{16,18},{18,... | collective-permute-start | bytes 393224 | tf_op jit(solution)/shard_map/ppermute | solution.py:31
  21.2 2.1 %collective-permute-start.10 = (bf16[2,256,128]{2,1,0:T(8,128)(2,1)S(1)}, bf16[2,256,128]{2,1,0:T(8,128)(2,1)S(1)}, u32[]{:S(2)}, u32[]{:S(2)}) collective-permute-start(bf16[2,256,128]{2,1,0:T(8,128)(2,1)S(1)} %collective-permute-done.9.rest_6_), channel_id=1, source_target_pairs={{0,2},{2,0},{4,6},{6,4},{8,10},{10,8},{12,14},{14,12},{16,18},{18,... | collective-permute-start | bytes 393224 | tf_op jit(solution)/shard_map/ppermute | solution.py:31
  21.3 6.3 %collective-permute-start.2 = (bf16[2,256,128]{2,1,0:T(8,128)(2,1)S(1)}, bf16[2,256,128]{2,1,0:T(8,128)(2,1)S(1)}, u32[]{:S(2)}, u32[]{:S(2)}) collective-permute-start(bf16[2,256,128]{2,1,0:T(8,128)(2,1)S(1)} %collective-permute-done.rest_0_), channel_id=1, source_target_pairs={{0,4},{2,6},{4,0},{6,2},{8,12},{10,14},{12,8},{14,10},{16,20},{18,... | collective-permute-start | bytes 393224 | tf_op jit(solution)/shard_map/ppermute | solution.py:31
  22.8 7.2 %collective-permute-start.3 = (bf16[2,256,128]{2,1,0:T(8,128)(2,1)S(1)}, bf16[2,256,128]{2,1,0:T(8,128)(2,1)S(1)}, u32[]{:S(2)}, u32[]{:S(2)}) collective-permute-start(bf16[2,256,128]{2,1,0:T(8,128)(2,1)S(1)} %collective-permute-done.1.rest_1_), channel_id=1, source_target_pairs={{0,4},{2,6},{4,0},{6,2},{8,12},{10,14},{12,8},{14,10},{16,20},{18,... | collective-permute-start | bytes 393224 | tf_op jit(solution)/shard_map/ppermute | solution.py:31
  23.4 8.1 %copy-start = (bf16[1024,4096]{1,0:T(8,128)(2,1)S(1)}, bf16[1024,4096]{1,0:T(8,128)(2,1)}, u32[]{:S(2)}) copy-start(bf16[1024,4096]{1,0:T(8,128)(2,1)} %weight_ref.3) | copy-start | bytes 25165828
  31.5 1.9 %copy-start.1 = (bf16[256,2048]{1,0:T(8,128)(2,1)S(1)}, bf16[256,2048]{1,0:T(8,128)(2,1)}, u32[]{:S(2)}) copy-start(bf16[256,2048]{1,0:T(8,128)(2,1)} %refs_0_.1) | copy-start | bytes 3145732
  32.8 16.4 %collective-permute-start.12 = (bf16[256,1280]{1,0:T(8,128)(2,1)S(1)}, bf16[256,1280]{1,0:T(8,128)(2,1)S(1)}, u32[]{:S(2)}, u32[]{:S(2)}) collective-permute-start(bf16[256,1280]{1,0:T(8,128)(2,1)S(1)} %get-tuple-element.42), channel_id=1, source_target_pairs={{0,1},{1,0},{2,3},{3,2},{4,5},{5,4},{6,7},{7,6},{8,9},{9,8},{10,11... | collective-permute-start | bytes 1966088 | tf_op jit(solution)/shard_map/ppermute | solution.py:35
  33.4 3.1 %copy-start.3 = (bf16[256,1024]{1,0:T(8,128)(2,1)S(1)}, bf16[256,1024]{1,0:T(8,128)(2,1)}, u32[]{:S(2)}) copy-start(bf16[256,1024]{1,0:T(8,128)(2,1)} %q_ref.1) | copy-start | bytes 1572868
  49.2 2.3 %collective-permute-start.14 = (bf16[6,2,128,256]{3,2,1,0:T(8,128)(2,1)S(1)}, bf16[6,2,128,256]{3,2,1,0:T(8,128)(2,1)S(1)}, u32[]{:S(2)}, u32[]{:S(2)}) collective-permute-start(bf16[6,2,128,256]{3,2,1,0:T(8,128)(2,1)S(1)} %get-tuple-element.53), channel_id=1, source_target_pairs={{0,2},{2,0},{4,6},{6,4},{8,10},{10,8},{12,14},{14,12},{16,18},{18,... | collective-permute-start | bytes 2359304 | tf_op jit(solution)/shard_map/ppermute | solution.py:31
  51.6 6.4 %collective-permute-start.18 = (bf16[2,128,256]{2,1,0:T(8,128)(2,1)S(1)}, bf16[2,128,256]{2,1,0:T(8,128)(2,1)S(1)}, u32[]{:S(2)}, u32[]{:S(2)}) collective-permute-start(bf16[2,128,256]{2,1,0:T(8,128)(2,1)S(1)} %get-tuple-element.58), channel_id=1, source_target_pairs={{0,4},{2,6},{4,0},{6,2},{8,12},{10,14},{12,8},{14,10},{16,20},{18,... | collective-permute-start | bytes 393224 | tf_op jit(solution)/shard_map/ppermute | solution.py:31
  53.2 7.6 %collective-permute-start.16 = (bf16[2,128,256]{2,1,0:T(8,128)(2,1)S(1)}, bf16[2,128,256]{2,1,0:T(8,128)(2,1)S(1)}, u32[]{:S(2)}, u32[]{:S(2)}) collective-permute-start(bf16[2,128,256]{2,1,0:T(8,128)(2,1)S(1)} %get-tuple-element.59), channel_id=1, source_target_pairs={{0,4},{2,6},{4,0},{6,2},{8,12},{10,14},{12,8},{14,10},{16,20},{18,... | collective-permute-start | bytes 393224 | tf_op jit(solution)/shard_map/ppermute | solution.py:31
  53.7 10.6 %collective-permute-start.13 = (bf16[256,768]{1,0:T(8,128)(2,1)S(1)}, bf16[256,768]{1,0:T(8,128)(2,1)S(1)}, u32[]{:S(2)}, u32[]{:S(2)}) collective-permute-start(bf16[256,768]{1,0:T(8,128)(2,1)S(1)} %get-tuple-element.50), channel_id=1, source_target_pairs={{0,1},{1,0},{2,3},{3,2},{4,5},{5,4},{6,7},{7,6},{8,9},{9,8},{10,11... | collective-permute-start | bytes 1179656 | tf_op jit(solution)/shard_map/ppermute | solution.py:35
  54.2 12.4 %collective-permute-start.15 = (bf16[2,128,256]{2,1,0:T(8,128)(2,1)S(1)}, bf16[2,128,256]{2,1,0:T(8,128)(2,1)S(1)}, u32[]{:S(2)}, u32[]{:S(2)}) collective-permute-start(bf16[2,128,256]{2,1,0:T(8,128)(2,1)S(1)} %get-tuple-element.60), channel_id=1, source_target_pairs={{0,4},{2,6},{4,0},{6,2},{8,12},{10,14},{12,8},{14,10},{16,20},{18,... | collective-permute-start | bytes 393224 | tf_op jit(solution)/shard_map/ppermute | solution.py:31
  60.9 9.5 %collective-permute-start.19 = (bf16[2,128,256]{2,1,0:T(8,128)(2,1)S(1)}, bf16[2,128,256]{2,1,0:T(8,128)(2,1)S(1)}, u32[]{:S(2)}, u32[]{:S(2)}) collective-permute-start(bf16[2,128,256]{2,1,0:T(8,128)(2,1)S(1)} %get-tuple-element.56), channel_id=1, source_target_pairs={{16,0},{18,2},{20,4},{22,6},{24,8},{26,10},{28,12},{30,14},{17,1},... | collective-permute-start | bytes 393224 | tf_op jit(solution)/shard_map/ppermute | solution.py:27
  62.2 8.4 %collective-permute-start.17 = (bf16[2,128,256]{2,1,0:T(8,128)(2,1)S(1)}, bf16[2,128,256]{2,1,0:T(8,128)(2,1)S(1)}, u32[]{:S(2)}, u32[]{:S(2)}) collective-permute-start(bf16[2,128,256]{2,1,0:T(8,128)(2,1)S(1)} %get-tuple-element.57), channel_id=1, source_target_pairs={{8,0},{10,2},{12,4},{14,6},{16,8},{18,10},{20,12},{22,14},{24,16},... | collective-permute-start | bytes 393224 | tf_op jit(solution)/shard_map/ppermute | solution.py:27

commit v2 on v1

--- a/solution.py
+++ b/solution.py
@@ -21,10 +21,14 @@
 NT = (((1,), (1,)), ((), ()))
 
 
-def shifted(block, distance):
+def sent_on(block, distance):
     size = lax.axis_size("ctx")
-    route = [(i, i + distance) for i in range(size) if 0 <= i + distance < size]
-    return lax.ppermute(block, "ctx", route)
+    return lax.ppermute(block, "ctx", [(i, i + distance) for i in range(size - distance)])
+
+
+def sent_back(block, distance):
+    size = lax.axis_size("ctx")
+    return lax.ppermute(block, "ctx", [(i, (i - distance) % size) for i in range(size)])
 
 
 def swapped(block, bit):
@@ -519,7 +523,7 @@
     order = jnp.concatenate([mine, theirs])
     pair = pair_up(keys, values)
     other_cot = tp_swapped(cotangent)
-    planes = [pair] + [shifted(pair, plane * GROUP) for plane in range(1, PLANES)]
+    planes = [pair] + [sent_on(pair, plane * GROUP) for plane in range(1, PLANES)]
     prepared = prepare(doc_lengths, queries)
     planes[BACK], *prepared = lax.optimization_barrier((planes[BACK], *prepared))
 
@@ -555,7 +559,7 @@
     arrived = []
     for plane in range(1, PLANES):
         half_sum = core_sum(plane) + crossed[plane].astype(jnp.float32)
-        arrived.append(shifted(half_sum.astype(jnp.bfloat16), -plane * GROUP))
+        arrived.append(sent_back(half_sum.astype(jnp.bfloat16), plane * GROUP))
     (mixed_out,) = project(mine, attention, out_weight, early_mixed, late_mixed)
     keys_gradient, values_gradient = finish(keep, received, [crossed[0]] + arrived)
     return (mixed_out, query_grad, keys_gradient, values_gradient)

time: 71.8 us -> 70.3 us (0.979)
  waiting for transfers between devices: 27.6 us -> 26.5 us
    ppermute x4, waiting for transfers between devices: 4.04 us -> 2.78 us  [the longest x2 2.78 us: sent_back(): lax.ppermute(block, 'ctx', [(i, (i - distance) % size) for i in range(siz...]
  transfers between devices with their start and end apart: 20 -> 20, of which waited for: 11 -> 11; matrix products, arithmetic and copies ran while one was open for 0% -> 0% of each run, Pallas kernels for 21% -> 22%
where the time goes in v2:
time: 70.3 us; the launch traced here: 70.2 us
  waiting for transfers between devices  26.5 us (38%)
  starting transfers between devices  23.1 us (33%)
  Pallas kernels  16.1 us (23%)
  local copies, waits for them, and re-layouts  3.39 us (5%)
  between operations  0.76 us (1%)
    ppermute x13, waiting for transfers between devices, swapped(): lax.ppermute(block, 'ctx', [(i, i ^ bit) for i in range(lax.axis_size('ct...  14.1 us
    ppermute x3, waiting for transfers between devices, tp_swapped(): return lax.ppermute(block, 'tp', [(0, 1), (1, 0)])  9.55 us
    ppermute x13, starting transfers between devices, swapped(): lax.ppermute(block, 'ctx', [(i, i ^ bit) for i in range(lax.axis_size('ct...  8.56 us
    ppermute x2, starting transfers between devices, sent_on(): lax.ppermute(block, 'ctx', [(i, i + distance) for i in range(size - dista...  7.99 us
    ppermute x3, starting transfers between devices, tp_swapped(): return lax.ppermute(block, 'tp', [(0, 1), (1, 0)])  4.14 us
    pallas_call x1, Pallas kernels, attend_back(): pl.pallas_call(partial(backward_kernel, heads), out_shape=(jax.ShapeDtype...  4.11 us
    pallas_call x2, Pallas kernels, project(): pl.pallas_call(partial(project_kernel, tile, pieces), out_shape=tuple((ja...  3.62 us
    unnamed x14, local copies, waits for them, and re-layouts  3.39 us
  transfers between devices with their start and end apart: 20, of which 11 were waited for; matrix products, arithmetic and copies ran while one was open for 0% of the time, Pallas kernels for 22%

profile of v2, /device:TPU:0, one launch (start us, length us, event | category | flops | bytes accessed | tf_op | source)
XLA Modules:
  0.0 70.2 jit_solution(10850339179938514278)
XLA Ops:
  0.6 3.0 %collective-permute-start.11 = (bf16[256,2048]{1,0:T(8,128)(2,1)}, bf16[256,2048]{1,0:T(8,128)(2,1)S(1)}, u32[]{:S(2)}, u32[]{:S(2)}) collective-permute-start(bf16[256,2048]{1,0:T(8,128)(2,1)} %refs_0_.1), channel_id=1, source_target_pairs={{0,1},{1,0},{2,3},{3,2},{4,5},{5,4},{6,7},{7,6},{8,9},{9,8},{10,11... | collective-permute-start | bytes 3145736 | tf_op jit(solution)/shard_map/ppermute | solution.py:39
  3.6 0.8 %copy-done.4 = bf16[256,128]{1,0:T(8,128)(2,1)S(1)} copy-done((bf16[256,128]{1,0:T(8,128)(2,1)S(1)}, bf16[256,128]{1,0:T(8,128)(2,1)}, u32[]{:S(2)}) %copy-start.4) | copy-done | bytes 65560
  4.5 0.8 %copy-done.5 = bf16[256,128]{1,0:T(8,128)(2,1)S(1)} copy-done((bf16[256,128]{1,0:T(8,128)(2,1)S(1)}, bf16[256,128]{1,0:T(8,128)(2,1)}, u32[]{:S(2)}) %copy-start.5) | copy-done | bytes 65560
  5.4 3.5 %collective-permute-start.7 = (bf16[2,256,128]{2,1,0:T(8,128)(2,1)S(1)}, bf16[2,256,128]{2,1,0:T(8,128)(2,1)S(1)}, u32[]{:S(2)}, u32[]{:S(2)}) collective-permute-start(bf16[2,256,128]{2,1,0:T(8,128)(2,1)S(1)} %pair_up.1.rest_0_), channel_id=1, source_target_pairs={{0,8},{2,10},{4,12},{6,14},{8,16},{10,18},{12,20},{14,22},{16,24},... | collective-permute-start | bytes 393224 | tf_op jit(solution)/shard_map/ppermute | solution.py:26
  8.9 4.5 %collective-permute-start = (bf16[2,256,128]{2,1,0:T(8,128)(2,1)S(1)}, bf16[2,256,128]{2,1,0:T(8,128)(2,1)S(1)}, u32[]{:S(2)}, u32[]{:S(2)}) collective-permute-start(bf16[2,256,128]{2,1,0:T(8,128)(2,1)S(1)} %pair_up.1.rest_0_), channel_id=1, source_target_pairs={{0,16},{2,18},{4,20},{6,22},{8,24},{10,26},{12,28},{14,30},{1,17},... | collective-permute-start | bytes 393224 | tf_op jit(solution)/shard_map/ppermute | solution.py:26
  13.4 1.6 %collective-permute-start.5 = (bf16[2,256,128]{2,1,0:T(8,128)(2,1)S(1)}, bf16[2,256,128]{2,1,0:T(8,128)(2,1)S(1)}, u32[]{:S(2)}, u32[]{:S(2)}) collective-permute-start(bf16[2,256,128]{2,1,0:T(8,128)(2,1)S(1)} %pair_up.1.rest_0_), channel_id=1, source_target_pairs={{0,4},{2,6},{4,0},{6,2},{8,12},{10,14},{12,8},{14,10},{16,20},{18,... | collective-permute-start | bytes 393224 | tf_op jit(solution)/shard_map/ppermute | solution.py:35
  15.0 0.5 collective-permute-start.9
  15.5 1.0 %copy-done.2 = bf16[256,1024]{1,0:T(8,128)(2,1)S(1)} copy-done((bf16[256,1024]{1,0:T(8,128)(2,1)S(1)}, bf16[256,1024]{1,0:T(8,128)(2,1)}, u32[]{:S(2)}) %copy-start.2) | copy-done | bytes 524312
  16.5 0.7 copy-done.6
  17.2 1.1 %prepare.1 = (bf16[8,128,256]{2,1,0:T(8,128)(2,1)S(1)}, s32[8,256]{1,0:T(8,128)S(1)}, s32[1]{0:T(128)}) custom-call(s32[8]{0:T(128)S(1)} %copy-done.6, bf16[256,1024]{1,0:T(8,128)(2,1)S(1)} %copy-done.2), custom_call_target="tpu_custom_call" | custom-call | tf_op jit(solution)/shard_map/prepare/pallas_call | solution.py:352
  19.3 1.9 %collective-permute-done.9.rest_6_ = bf16[2,256,128]{2,1,0:T(8,128)(2,1)S(1)} collective-permute-done((bf16[2,256,128]{2,1,0:T(8,128)(2,1)S(1)}, bf16[2,256,128]{2,1,0:T(8,128)(2,1)S(1)}, u32[]{:S(2)}, u32[]{:S(2)}) %collective-permute-start.9) | collective-permute-done | bytes 131104 | tf_op jit(solution)/shard_map/ppermute | solution.py:35
  21.3 1.5 %collective-permute-start.2 = (bf16[2,256,128]{2,1,0:T(8,128)(2,1)S(1)}, bf16[2,256,128]{2,1,0:T(8,128)(2,1)S(1)}, u32[]{:S(2)}, u32[]{:S(2)}) collective-permute-start(bf16[2,256,128]{2,1,0:T(8,128)(2,1)S(1)} %collective-permute-done.rest_0_), channel_id=1, source_target_pairs={{0,4},{2,6},{4,0},{6,2},{8,12},{10,14},{12,8},{14,10},{16,20},{18,... | collective-permute-start | bytes 393224 | tf_op jit(solution)/shard_map/ppermute | solution.py:35
  23.4 1.9 %attend.2 = (f32[8,144,256]{2,1,0:T(8,128)S(1)}, f32[8,256]{1,0:T(8,128)S(1)}, bf16[12,2,256,128]{3,2,1,0:T(8,128)(2,1)S(1)}) custom-call(s32[1]{0:T(128)} %get-tuple-element.33.begin_ref, s32[8,256]{1,0:T(8,128)S(1)} %get-tuple-element.34.starts_ref, bf16[8,128,256]{2,1,0:T(8,128)(2,1)S(1)} %get-tuple-element.35.qt_ref, ...), custom_call_target="tpu_custom_call" | custom-call | flops 2147483648 | bytes 4194304 | tf_op jit(solution)/shard_map/attend/pallas_call | solution.py:327
  25.3 2.3 %collective-permute-done.2.rest_2_ = bf16[2,256,128]{2,1,0:T(8,128)(2,1)S(1)} collective-permute-done((bf16[2,256,128]{2,1,0:T(8,128)(2,1)S(1)}, bf16[2,256,128]{2,1,0:T(8,128)(2,1)S(1)}, u32[]{:S(2)}, u32[]{:S(2)}) %collective-permute-start.2) | collective-permute-done | bytes 131104 | tf_op jit(solution)/shard_map/ppermute | solution.py:35
  27.6 2.4 %collective-permute-done.3.rest_3_ = bf16[2,256,128]{2,1,0:T(8,128)(2,1)S(1)} collective-permute-done((bf16[2,256,128]{2,1,0:T(8,128)(2,1)S(1)}, bf16[2,256,128]{2,1,0:T(8,128)(2,1)S(1)}, u32[]{:S(2)}, u32[]{:S(2)}) %collective-permute-start.3) | collective-permute-done | bytes 131104 | tf_op jit(solution)/shard_map/ppermute | solution.py:35
  30.0 1.4 %attend.3 = (bf16[256,1024]{1,0:T(8,128)(2,1)S(1)}, f32[8,256]{1,0:T(8,128)S(1)}, bf16[12,2,256,128]{3,2,1,0:T(8,128)(2,1)S(1)}) custom-call(s32[1]{0:T(128)} %get-tuple-element.33.begin_ref, s32[8,256]{1,0:T(8,128)S(1)} %get-tuple-element.34.starts_ref, bf16[8,128,256]{2,1,0:T(8,128)(2,1)S(1)} %get-tuple-element.35.qt_ref, ...), custom_call_target="tpu_custom_call" | custom-call | flops 1073741824 | bytes 4194304 | tf_op jit(solution)/shard_map/attend/pallas_call | solution.py:327
  31.5 1.3 %project.2 = (bf16[256,1280]{1,0:T(8,128)(2,1)S(1)}, bf16[256,768]{1,0:T(8,128)(2,1)S(1)}) custom-call(s32[1]{0:T(128)S(6)} %sub.3.half_ref, bf16[256,1024]{1,0:T(8,128)(2,1)S(1)} %get-tuple-element.40.att_ref, bf16[1024,4096]{1,0:T(8,128)(2,1)S(1)} %copy-done), custom_call_target="tpu_custom_call" | custom-call | flops 1073741824 | bytes 4194304 | tf_op jit(solution)/shard_map/project/pallas_call | solution.py:469
  32.8 0.6 collective-permute-start.12
  33.4 3.1 %attention_grad.1 = (bf16[256,1024]{1,0:T(8,128)(2,1)S(1)}, bf16[8,128,256]{2,1,0:T(8,128)(2,1)S(1)}) custom-call(s32[2]{0:T(128)S(1)} %pad_add_fusion.order_ref, bf16[256,2048]{1,0:T(8,128)(2,1)S(1)} %copy-done.1, bf16[256,2048]{1,0:T(8,128)(2,1)S(1)} %collective-permute-done.11.refs_1_, bf16[1024,4096]{1,0:T(8,128)(2,1)S(1)} %copy-done), custom_call_target="tpu_custom_call" | custom-call | flops 2147483648 | bytes 8388608 | tf_op jit(solution)/shard_map/attention_grad/pallas_call | solution.py:504
  36.5 4.1 %attend_back.1 = (bf16[256,1024]{1,0:T(8,128)(2,1)}, f32[6,2,128,256]{3,2,1,0:T(8,128)S(1)}, bf16[6,2,128,256]{3,2,1,0:T(8,128)(2,1)S(1)}) custom-call(s32[1]{0:T(128)} %get-tuple-element.33.begin_ref, s32[8,256]{1,0:T(8,128)S(1)} %get-tuple-element.34.starts_ref, bf16[256,1024]{1,0:T(8,128)(2,1)S(1)} %copy-done.3, ...), custom_call_target="tpu_custom_call" | custom-call | flops 6039797760 | bytes 8388608 | tf_op jit(solution)/shard_map/attend_back/pallas_call | solution.py:372
  40.6 8.6 %collective-permute-done.12.rest_0_ = bf16[256,1280]{1,0:T(8,128)(2,1)S(1)} collective-permute-done((bf16[256,1280]{1,0:T(8,128)(2,1)S(1)}, bf16[256,1280]{1,0:T(8,128)(2,1)S(1)}, u32[]{:S(2)}, u32[]{:S(2)}) %collective-permute-start.12) | collective-permute-done | bytes 655392 | tf_op jit(solution)/shard_map/ppermute | solution.py:39
  49.2 2.3 %collective-permute-done.14.received_ref = bf16[6,2,128,256]{3,2,1,0:T(8,128)(2,1)S(1)} collective-permute-done((bf16[6,2,128,256]{3,2,1,0:T(8,128)(2,1)S(1)}, bf16[6,2,128,256]{3,2,1,0:T(8,128)(2,1)S(1)}, u32[]{:S(2)}, u32[]{:S(2)}) %collective-permute-start.14) | collective-permute-done | bytes 786464 | tf_op jit(solution)/shard_map/ppermute | solution.py:35
  51.6 1.6 %collective-permute-start.18 = (bf16[2,128,256]{2,1,0:T(8,128)(2,1)S(1)}, bf16[2,128,256]{2,1,0:T(8,128)(2,1)S(1)}, u32[]{:S(2)}, u32[]{:S(2)}) collective-permute-start(bf16[2,128,256]{2,1,0:T(8,128)(2,1)S(1)} %get-tuple-element.58), channel_id=1, source_target_pairs={{0,4},{2,6},{4,0},{6,2},{8,12},{10,14},{12,8},{14,10},{16,20},{18,... | collective-permute-start | bytes 393224 | tf_op jit(solution)/shard_map/ppermute | solution.py:35
  53.7 0.5 collective-permute-start.13
  54.2 1.5 %collective-permute-start.15 = (bf16[2,128,256]{2,1,0:T(8,128)(2,1)S(1)}, bf16[2,128,256]{2,1,0:T(8,128)(2,1)S(1)}, u32[]{:S(2)}, u32[]{:S(2)}) collective-permute-start(bf16[2,128,256]{2,1,0:T(8,128)(2,1)S(1)} %get-tuple-element.60), channel_id=1, source_target_pairs={{0,4},{2,6},{4,0},{6,2},{8,12},{10,14},{12,8},{14,10},{16,20},{18,... | collective-permute-start | bytes 393224 | tf_op jit(solution)/shard_map/ppermute | solution.py:35
  55.8 2.2 %collective-permute-done.18 = bf16[2,128,256]{2,1,0:T(8,128)(2,1)S(1)} collective-permute-done((bf16[2,128,256]{2,1,0:T(8,128)(2,1)S(1)}, bf16[2,128,256]{2,1,0:T(8,128)(2,1)S(1)}, u32[]{:S(2)}, u32[]{:S(2)}) %collective-permute-start.18) | collective-permute-done | bytes 131104 | tf_op jit(solution)/shard_map/ppermute | solution.py:35
  58.0 2.8 %collective-permute-done.16 = bf16[2,128,256]{2,1,0:T(8,128)(2,1)S(1)} collective-permute-done((bf16[2,128,256]{2,1,0:T(8,128)(2,1)S(1)}, bf16[2,128,256]{2,1,0:T(8,128)(2,1)S(1)}, u32[]{:S(2)}, u32[]{:S(2)}) %collective-permute-start.16) | collective-permute-done | bytes 131104 | tf_op jit(solution)/shard_map/ppermute | solution.py:35
  60.9 2.5 %collective-permute-start.19 = (bf16[2,128,256]{2,1,0:T(8,128)(2,1)S(1)}, bf16[2,128,256]{2,1,0:T(8,128)(2,1)S(1)}, u32[]{:S(2)}, u32[]{:S(2)}) collective-permute-start(bf16[2,128,256]{2,1,0:T(8,128)(2,1)S(1)} %get-tuple-element.56), channel_id=1, source_target_pairs={{0,16},{2,18},{4,20},{6,22},{8,24},{10,26},{12,28},{14,30},{16,0},... | collective-permute-start | bytes 393224 | tf_op jit(solution)/shard_map/ppermute | solution.py:31
  63.4 0.9 %collective-permute-done.13.rest_1_ = bf16[256,768]{1,0:T(8,128)(2,1)S(1)} collective-permute-done((bf16[256,768]{1,0:T(8,128)(2,1)S(1)}, bf16[256,768]{1,0:T(8,128)(2,1)S(1)}, u32[]{:S(2)}, u32[]{:S(2)}) %collective-permute-start.13) | collective-permute-done | bytes 393248 | tf_op jit(solution)/shard_map/ppermute | solution.py:39
  64.3 2.3 %project.3 = bf16[256,2048]{1,0:T(8,128)(2,1)} custom-call(s32[1]{0:T(128)} %bitcast.half_ref, bf16[256,1024]{1,0:T(8,128)(2,1)S(1)} %get-tuple-element.40.att_ref, bf16[1024,4096]{1,0:T(8,128)(2,1)S(1)} %copy-done, bf16[256,1280]{1,0:T(8,128)(2,1)S(1)} %collective-permute-done.12.rest_0_, bf16[256,768]{1,0:T(8,128)(2,1)S(1)} %collective-permute-done.13.rest_1_), custom_call_target="tpu_custom_call" | custom-call | flops 1073741824 | bytes 4194304 | tf_op jit(solution)/shard_map/project/pallas_call | solution.py:469
  66.6 2.3 %collective-permute-done.19.rest_2_ = bf16[2,128,256]{2,1,0:T(8,128)(2,1)S(1)} collective-permute-done((bf16[2,128,256]{2,1,0:T(8,128)(2,1)S(1)}, bf16[2,128,256]{2,1,0:T(8,128)(2,1)S(1)}, u32[]{:S(2)}, u32[]{:S(2)}) %collective-permute-start.19) | collective-permute-done | bytes 131104 | tf_op jit(solution)/shard_map/ppermute | solution.py:31
  69.4 0.8 %finish.1 = (bf16[256,128]{1,0:T(8,128)(2,1)}, bf16[256,128]{1,0:T(8,128)(2,1)}) custom-call(f32[6,2,128,256]{3,2,1,0:T(8,128)S(1)} %get-tuple-element.52.keep_ref, bf16[6,2,128,256]{3,2,1,0:T(8,128)(2,1)S(1)} %collective-permute-done.14.received_ref, bf16[2,128,256]{2,1,0:T(8,128)(2,1)S(1)} %collective-permute-done.15.rest_0_, ...), custom_call_target="tpu_custom_call" | custom-call | tf_op jit(solution)/shard_map/finish/pallas_call | solution.py:434
  (34 shorter events, 2.8 us)
Async XLA Ops:
  0.6 32.8 %collective-permute-start.11 = (bf16[256,2048]{1,0:T(8,128)(2,1)}, bf16[256,2048]{1,0:T(8,128)(2,1)S(1)}, u32[]{:S(2)}, u32[]{:S(2)}) collective-permute-start(bf16[256,2048]{1,0:T(8,128)(2,1)} %refs_0_.1), channel_id=1, source_target_pairs={{0,1},{1,0},{2,3},{3,2},{4,5},{5,4},{6,7},{7,6},{8,9},{9,8},{10,11... | collective-permute-start | bytes 3145736 | tf_op jit(solution)/shard_map/ppermute | solution.py:39
  3.6 0.8 %copy-start.4 = (bf16[256,128]{1,0:T(8,128)(2,1)S(1)}, bf16[256,128]{1,0:T(8,128)(2,1)}, u32[]{:S(2)}) copy-start(bf16[256,128]{1,0:T(8,128)(2,1)} %keys_ref.1) | copy-start | bytes 196612
  4.5 0.8 %copy-start.5 = (bf16[256,128]{1,0:T(8,128)(2,1)S(1)}, bf16[256,128]{1,0:T(8,128)(2,1)}, u32[]{:S(2)}) copy-start(bf16[256,128]{1,0:T(8,128)(2,1)} %values_ref.1) | copy-start | bytes 196612
  5.4 9.6 %collective-permute-start.7 = (bf16[2,256,128]{2,1,0:T(8,128)(2,1)S(1)}, bf16[2,256,128]{2,1,0:T(8,128)(2,1)S(1)}, u32[]{:S(2)}, u32[]{:S(2)}) collective-permute-start(bf16[2,256,128]{2,1,0:T(8,128)(2,1)S(1)} %pair_up.1.rest_0_), channel_id=1, source_target_pairs={{0,8},{2,10},{4,12},{6,14},{8,16},{10,18},{12,20},{14,22},{16,24},... | collective-permute-start | bytes 393224 | tf_op jit(solution)/shard_map/ppermute | solution.py:26
  8.9 9.5 %collective-permute-start = (bf16[2,256,128]{2,1,0:T(8,128)(2,1)S(1)}, bf16[2,256,128]{2,1,0:T(8,128)(2,1)S(1)}, u32[]{:S(2)}, u32[]{:S(2)}) collective-permute-start(bf16[2,256,128]{2,1,0:T(8,128)(2,1)S(1)} %pair_up.1.rest_0_), channel_id=1, source_target_pairs={{0,16},{2,18},{4,20},{6,22},{8,24},{10,26},{12,28},{14,30},{1,17},... | collective-permute-start | bytes 393224 | tf_op jit(solution)/shard_map/ppermute | solution.py:26
  13.4 5.4 %collective-permute-start.5 = (bf16[2,256,128]{2,1,0:T(8,128)(2,1)S(1)}, bf16[2,256,128]{2,1,0:T(8,128)(2,1)S(1)}, u32[]{:S(2)}, u32[]{:S(2)}) collective-permute-start(bf16[2,256,128]{2,1,0:T(8,128)(2,1)S(1)} %pair_up.1.rest_0_), channel_id=1, source_target_pairs={{0,4},{2,6},{4,0},{6,2},{8,12},{10,14},{12,8},{14,10},{16,20},{18,... | collective-permute-start | bytes 393224 | tf_op jit(solution)/shard_map/ppermute | solution.py:35
  15.0 4.0 %collective-permute-start.4 = (bf16[2,256,128]{2,1,0:T(8,128)(2,1)S(1)}, bf16[2,256,128]{2,1,0:T(8,128)(2,1)S(1)}, u32[]{:S(2)}, u32[]{:S(2)}) collective-permute-start(bf16[2,256,128]{2,1,0:T(8,128)(2,1)S(1)} %pair_up.1.rest_0_), channel_id=1, source_target_pairs={{0,2},{2,0},{4,6},{6,4},{8,10},{10,8},{12,14},{14,12},{16,18},{18,... | collective-permute-start | bytes 393224 | tf_op jit(solution)/shard_map/ppermute | solution.py:35
  15.0 6.3 %collective-permute-start.9 = (bf16[2,256,128]{2,1,0:T(8,128)(2,1)S(1)}, bf16[2,256,128]{2,1,0:T(8,128)(2,1)S(1)}, u32[]{:S(2)}, u32[]{:S(2)}) collective-permute-start(bf16[2,256,128]{2,1,0:T(8,128)(2,1)S(1)} %collective-permute-done.7.rest_4_), channel_id=1, source_target_pairs={{0,4},{2,6},{4,0},{6,2},{8,12},{10,14},{12,8},{14,10},{16,20},{18,... | collective-permute-start | bytes 393224 | tf_op jit(solution)/shard_map/ppermute | solution.py:35
  15.5 1.0 %copy-start.2 = (bf16[256,1024]{1,0:T(8,128)(2,1)S(1)}, bf16[256,1024]{1,0:T(8,128)(2,1)}, u32[]{:S(2)}) copy-start(bf16[256,1024]{1,0:T(8,128)(2,1)} %q_ref.1) | copy-start | bytes 1572868
  16.5 0.7 copy-start.6
  18.4 3.0 %collective-permute-start.8 = (bf16[2,256,128]{2,1,0:T(8,128)(2,1)S(1)}, bf16[2,256,128]{2,1,0:T(8,128)(2,1)S(1)}, u32[]{:S(2)}, u32[]{:S(2)}) collective-permute-start(bf16[2,256,128]{2,1,0:T(8,128)(2,1)S(1)} %collective-permute-done.7.rest_4_), channel_id=1, source_target_pairs={{0,2},{2,0},{4,6},{6,4},{8,10},{10,8},{12,14},{14,12},{16,18},{18,... | collective-permute-start | bytes 393224 | tf_op jit(solution)/shard_map/ppermute | solution.py:35
  18.8 4.0 %collective-permute-start.1 = (bf16[2,256,128]{2,1,0:T(8,128)(2,1)S(1)}, bf16[2,256,128]{2,1,0:T(8,128)(2,1)S(1)}, u32[]{:S(2)}, u32[]{:S(2)}) collective-permute-start(bf16[2,256,128]{2,1,0:T(8,128)(2,1)S(1)} %collective-permute-done.rest_0_), channel_id=1, source_target_pairs={{0,2},{2,0},{4,6},{6,4},{8,10},{10,8},{12,14},{14,12},{16,18},{18,... | collective-permute-start | bytes 393224 | tf_op jit(solution)/shard_map/ppermute | solution.py:35
  18.9 4.4 %collective-permute-start.6 = (bf16[2,256,128]{2,1,0:T(8,128)(2,1)S(1)}, bf16[2,256,128]{2,1,0:T(8,128)(2,1)S(1)}, u32[]{:S(2)}, u32[]{:S(2)}) collective-permute-start(bf16[2,256,128]{2,1,0:T(8,128)(2,1)S(1)} %collective-permute-done.5.rest_2_), channel_id=1, source_target_pairs={{0,2},{2,0},{4,6},{6,4},{8,10},{10,8},{12,14},{14,12},{16,18},{18,... | collective-permute-start | bytes 393224 | tf_op jit(solution)/shard_map/ppermute | solution.py:35
  21.2 2.1 %collective-permute-start.10 = (bf16[2,256,128]{2,1,0:T(8,128)(2,1)S(1)}, bf16[2,256,128]{2,1,0:T(8,128)(2,1)S(1)}, u32[]{:S(2)}, u32[]{:S(2)}) collective-permute-start(bf16[2,256,128]{2,1,0:T(8,128)(2,1)S(1)} %collective-permute-done.9.rest_6_), channel_id=1, source_target_pairs={{0,2},{2,0},{4,6},{6,4},{8,10},{10,8},{12,14},{14,12},{16,18},{18,... | collective-permute-start | bytes 393224 | tf_op jit(solution)/shard_map/ppermute | solution.py:35
  21.3 6.3 %collective-permute-start.2 = (bf16[2,256,128]{2,1,0:T(8,128)(2,1)S(1)}, bf16[2,256,128]{2,1,0:T(8,128)(2,1)S(1)}, u32[]{:S(2)}, u32[]{:S(2)}) collective-permute-start(bf16[2,256,128]{2,1,0:T(8,128)(2,1)S(1)} %collective-permute-done.rest_0_), channel_id=1, source_target_pairs={{0,4},{2,6},{4,0},{6,2},{8,12},{10,14},{12,8},{14,10},{16,20},{18,... | collective-permute-start | bytes 393224 | tf_op jit(solution)/shard_map/ppermute | solution.py:35
  22.8 7.2 %collective-permute-start.3 = (bf16[2,256,128]{2,1,0:T(8,128)(2,1)S(1)}, bf16[2,256,128]{2,1,0:T(8,128)(2,1)S(1)}, u32[]{:S(2)}, u32[]{:S(2)}) collective-permute-start(bf16[2,256,128]{2,1,0:T(8,128)(2,1)S(1)} %collective-permute-done.1.rest_1_), channel_id=1, source_target_pairs={{0,4},{2,6},{4,0},{6,2},{8,12},{10,14},{12,8},{14,10},{16,20},{18,... | collective-permute-start | bytes 393224 | tf_op jit(solution)/shard_map/ppermute | solution.py:35
  23.4 8.1 %copy-start = (bf16[1024,4096]{1,0:T(8,128)(2,1)S(1)}, bf16[1024,4096]{1,0:T(8,128)(2,1)}, u32[]{:S(2)}) copy-start(bf16[1024,4096]{1,0:T(8,128)(2,1)} %weight_ref.3) | copy-start | bytes 25165828
  31.5 1.9 %copy-start.1 = (bf16[256,2048]{1,0:T(8,128)(2,1)S(1)}, bf16[256,2048]{1,0:T(8,128)(2,1)}, u32[]{:S(2)}) copy-start(bf16[256,2048]{1,0:T(8,128)(2,1)} %refs_0_.1) | copy-start | bytes 3145732
  32.8 16.4 %collective-permute-start.12 = (bf16[256,1280]{1,0:T(8,128)(2,1)S(1)}, bf16[256,1280]{1,0:T(8,128)(2,1)S(1)}, u32[]{:S(2)}, u32[]{:S(2)}) collective-permute-start(bf16[256,1280]{1,0:T(8,128)(2,1)S(1)} %get-tuple-element.42), channel_id=1, source_target_pairs={{0,1},{1,0},{2,3},{3,2},{4,5},{5,4},{6,7},{7,6},{8,9},{9,8},{10,11... | collective-permute-start | bytes 1966088 | tf_op jit(solution)/shard_map/ppermute | solution.py:39
  33.4 3.1 %copy-start.3 = (bf16[256,1024]{1,0:T(8,128)(2,1)S(1)}, bf16[256,1024]{1,0:T(8,128)(2,1)}, u32[]{:S(2)}) copy-start(bf16[256,1024]{1,0:T(8,128)(2,1)} %q_ref.1) | copy-start | bytes 1572868
  49.2 2.3 %collective-permute-start.14 = (bf16[6,2,128,256]{3,2,1,0:T(8,128)(2,1)S(1)}, bf16[6,2,128,256]{3,2,1,0:T(8,128)(2,1)S(1)}, u32[]{:S(2)}, u32[]{:S(2)}) collective-permute-start(bf16[6,2,128,256]{3,2,1,0:T(8,128)(2,1)S(1)} %get-tuple-element.53), channel_id=1, source_target_pairs={{0,2},{2,0},{4,6},{6,4},{8,10},{10,8},{12,14},{14,12},{16,18},{18,... | collective-permute-start | bytes 2359304 | tf_op jit(solution)/shard_map/ppermute | solution.py:35
  51.6 6.4 %collective-permute-start.18 = (bf16[2,128,256]{2,1,0:T(8,128)(2,1)S(1)}, bf16[2,128,256]{2,1,0:T(8,128)(2,1)S(1)}, u32[]{:S(2)}, u32[]{:S(2)}) collective-permute-start(bf16[2,128,256]{2,1,0:T(8,128)(2,1)S(1)} %get-tuple-element.58), channel_id=1, source_target_pairs={{0,4},{2,6},{4,0},{6,2},{8,12},{10,14},{12,8},{14,10},{16,20},{18,... | collective-permute-start | bytes 393224 | tf_op jit(solution)/shard_map/ppermute | solution.py:35
  53.2 7.6 %collective-permute-start.16 = (bf16[2,128,256]{2,1,0:T(8,128)(2,1)S(1)}, bf16[2,128,256]{2,1,0:T(8,128)(2,1)S(1)}, u32[]{:S(2)}, u32[]{:S(2)}) collective-permute-start(bf16[2,128,256]{2,1,0:T(8,128)(2,1)S(1)} %get-tuple-element.59), channel_id=1, source_target_pairs={{0,4},{2,6},{4,0},{6,2},{8,12},{10,14},{12,8},{14,10},{16,20},{18,... | collective-permute-start | bytes 393224 | tf_op jit(solution)/shard_map/ppermute | solution.py:35
  53.7 10.6 %collective-permute-start.13 = (bf16[256,768]{1,0:T(8,128)(2,1)S(1)}, bf16[256,768]{1,0:T(8,128)(2,1)S(1)}, u32[]{:S(2)}, u32[]{:S(2)}) collective-permute-start(bf16[256,768]{1,0:T(8,128)(2,1)S(1)} %get-tuple-element.50), channel_id=1, source_target_pairs={{0,1},{1,0},{2,3},{3,2},{4,5},{5,4},{6,7},{7,6},{8,9},{9,8},{10,11... | collective-permute-start | bytes 1179656 | tf_op jit(solution)/shard_map/ppermute | solution.py:39
  54.2 12.4 %collective-permute-start.15 = (bf16[2,128,256]{2,1,0:T(8,128)(2,1)S(1)}, bf16[2,128,256]{2,1,0:T(8,128)(2,1)S(1)}, u32[]{:S(2)}, u32[]{:S(2)}) collective-permute-start(bf16[2,128,256]{2,1,0:T(8,128)(2,1)S(1)} %get-tuple-element.60), channel_id=1, source_target_pairs={{0,4},{2,6},{4,0},{6,2},{8,12},{10,14},{12,8},{14,10},{16,20},{18,... | collective-permute-start | bytes 393224 | tf_op jit(solution)/shard_map/ppermute | solution.py:35
  60.9 8.0 %collective-permute-start.19 = (bf16[2,128,256]{2,1,0:T(8,128)(2,1)S(1)}, bf16[2,128,256]{2,1,0:T(8,128)(2,1)S(1)}, u32[]{:S(2)}, u32[]{:S(2)}) collective-permute-start(bf16[2,128,256]{2,1,0:T(8,128)(2,1)S(1)} %get-tuple-element.56), channel_id=1, source_target_pairs={{0,16},{2,18},{4,20},{6,22},{8,24},{10,26},{12,28},{14,30},{16,0},... | collective-permute-start | bytes 393224 | tf_op jit(solution)/shard_map/ppermute | solution.py:31
  63.3 6.0 %collective-permute-start.17 = (bf16[2,128,256]{2,1,0:T(8,128)(2,1)S(1)}, bf16[2,128,256]{2,1,0:T(8,128)(2,1)S(1)}, u32[]{:S(2)}, u32[]{:S(2)}) collective-permute-start(bf16[2,128,256]{2,1,0:T(8,128)(2,1)S(1)} %get-tuple-element.57), channel_id=1, source_target_pairs={{0,24},{2,26},{4,28},{6,30},{8,0},{10,2},{12,4},{14,6},{16,8},{18,... | collective-permute-start | bytes 393224 | tf_op jit(solution)/shard_map/ppermute | solution.py:31

commit v3 on v2

--- a/solution.py
+++ b/solution.py
@@ -54,20 +54,21 @@
     positions = first + lax.broadcasted_iota(jnp.int32, (1, rows), 1)
 
     def add_doc(doc, carry):
-        end, starts, start = carry
+        end, starts, start, middle = carry
         length = lens_ref[doc]
         end = end + length
         return (
             end,
             starts + jnp.where(positions >= end, length, 0),
             start + jnp.where(first >= end, length, 0),
+            middle + jnp.where(first + rows // 2 >= end, length, 0),
         )
 
     zero = jnp.int32(0)
-    _, starts, start = lax.fori_loop(
-        0, lens_ref.shape[0], add_doc, (zero, jnp.zeros((1, rows), jnp.int32), zero)
+    _, starts, start, middle = lax.fori_loop(
+        0, lens_ref.shape[0], add_doc, (zero, jnp.zeros((1, rows), jnp.int32), zero, zero)
     )
-    return starts, start
+    return starts, start, middle
 
 
 def block_bias(block, base, first, starts):
@@ -229,22 +230,25 @@
         wide_mass_ref[h] = jnp.broadcast_to(mass_t[:, h : h + 1], (rows, HEAD_WIDTH))
     chunk = HEAD_WIDTH
     own = BACK * GROUP + place
+    begin = begin_ref[0]
 
     def across(ref, h, piece):
         return jnp.concatenate([ref[h, piece]] * (rows // HEAD_WIDTH), axis=1)
 
-    def visit(block, own_block):
+    def visit(block, masked, count=rows):
         keys = win_ref[block, 0]
         keys_t = keys.T
         values_t = values_turned(win_ref, block)
-        bias_ref[...] = block_bias(block, base, first, starts).T
-        for h in range(heads):
-            for at in range(0, rows, chunk):
+        if masked:
+            bias_ref[...] = block_bias(block, base, first, starts).T
+        for h in range(heads):
+            for at in range(0, count, chunk):
                 piece = slice(at, at + chunk)
                 scores = (
                     jnp.dot(q_ref[piece, head(h)], keys_t, preferred_element_type=jnp.float32) * scale
-                    + bias_ref[piece]
                 )
+                if masked:
+                    scores = scores + bias_ref[piece]
                 prob = jnp.exp2(scores - across(wide_mass_ref, h, piece))
                 prob_ref[h, piece] = prob.astype(jnp.bfloat16)
                 grad_prob = jnp.dot(
@@ -257,18 +261,16 @@
         value_grad = jnp.zeros((HEAD_WIDTH, rows), jnp.float32)
         for h in range(heads):
             value_grad = value_grad + jnp.dot(
-                grad_t_ref[h], prob_ref[h], preferred_element_type=jnp.float32
+                grad_t_ref[h, :, :count], prob_ref[h, :count], preferred_element_type=jnp.float32
             )
         for h in range(heads):
             key_grad = key_grad + jnp.dot(
-                qt_ref[h], grad_score_ref[h], preferred_element_type=jnp.float32
+                qt_ref[h, :, :count], grad_score_ref[h, :count], preferred_element_type=jnp.float32
             )
         for h in range(heads):
-            query_grad = jnp.dot(grad_score_ref[h], keys, preferred_element_type=jnp.float32)
-            if own_block:
-                acc_ref[h] = query_grad
-            else:
-                acc_ref[h] += query_grad
+            acc_ref[h, :count] += jnp.dot(
+                grad_score_ref[h, :count], keys, preferred_element_type=jnp.float32
+            )
         give(block, key_grad * score_scale, value_grad)
 
     def give(block, key_grad, value_grad):
@@ -288,9 +290,25 @@
         none = jnp.zeros((HEAD_WIDTH, rows), jnp.float32)
         give(block, none, none)
 
-    visit(own, True)
-    pl.loop(begin_ref[0], own)(lambda block: visit(block, False))
-    pl.loop(0, begin_ref[0])(give_nothing)
+    acc_ref[...] = jnp.zeros_like(acc_ref)
+    pl.loop(0, jnp.where(begin < own, 2, 1))(
+        lambda turn: visit(jnp.where(turn == 0, own, begin), True)
+    )
+    in_first = jnp.where(starts <= jnp.min(starts, axis=1, keepdims=True), 1.0, 0.0)
+    in_first = jnp.broadcast_to(in_first, (8, rows)).T[:, 0:1]
+    for h in range(heads):
+        wide_mass_ref[h] = jnp.where(in_first > 0.5, wide_mass_ref[h], -MASKED)
+    few = begin_ref[1] == 1
+
+    @pl.when(few)
+    def _():
+        pl.loop(begin + 1, own)(lambda block: visit(block, False, rows // 2))
+
+    @pl.when(jnp.logical_not(few))
+    def _():
+        pl.loop(begin + 1, own)(lambda block: visit(block, False))
+
+    pl.loop(0, begin)(give_nothing)
     pl.loop(own + 1, WINDOW)(give_nothing)
     for h in range(heads):
         dq_ref[:, head(h)] = (acc_ref[h] * score_scale).astype(jnp.bfloat16)
@@ -341,9 +359,10 @@
 def prepare_kernel(lens_ref, wide_ref, out_ref, starts_ref, begin_ref):
     rows = wide_ref.shape[0]
     _, first, base = window_place(rows)
-    starts, start = doc_rows(lens_ref, first, rows)
+    starts, start, middle = doc_rows(lens_ref, first, rows)
     starts_ref[...] = jnp.broadcast_to(starts, starts_ref.shape)
     begin_ref[0] = (start - base) // rows
+    begin_ref[1] = jnp.where(middle > start, 1, 0)
     transpose_heads(wide_ref, out_ref)
 
 
@@ -354,7 +373,7 @@
         out_shape=(
             jax.ShapeDtypeStruct((width // HEAD_WIDTH, HEAD_WIDTH, rows), queries.dtype),
             jax.ShapeDtypeStruct((8, rows), jnp.int32),
-            jax.ShapeDtypeStruct((1,), jnp.int32),
+            jax.ShapeDtypeStruct((2,), jnp.int32),
         ),
         in_specs=[SCALARS, whole()],
         out_specs=(whole(), whole(), SCALARS),

time: 70.3 us -> 70.2 us (level)
    ppermute x3, waiting for transfers between devices: 9.55 us -> 8.65 us  [tp_swapped(): return lax.ppermute(block, 'tp', [(0, 1), (1, 0)])]
where the time goes in v3:
time: 70.2 us; the launch traced here: 70.3 us
  waiting for transfers between devices  26 us (37%)
  starting transfers between devices  23.5 us (33%)
  Pallas kernels  16.4 us (23%)
  local copies, waits for them, and re-layouts  3.39 us (5%)
  between operations  0.76 us (1%)
    ppermute x13, waiting for transfers between devices, swapped(): lax.ppermute(block, 'ctx', [(i, i ^ bit) for i in range(lax.axis_size('ct...  14.3 us
    ppermute x3, waiting for transfers between devices, tp_swapped(): return lax.ppermute(block, 'tp', [(0, 1), (1, 0)])  8.65 us
    ppermute x13, starting transfers between devices, swapped(): lax.ppermute(block, 'ctx', [(i, i ^ bit) for i in range(lax.axis_size('ct...  8.56 us
    ppermute x2, starting transfers between devices, sent_on(): lax.ppermute(block, 'ctx', [(i, i + distance) for i in range(size - dista...  7.99 us
    pallas_call x1, Pallas kernels, attend_back(): pl.pallas_call(partial(backward_kernel, heads), out_shape=(jax.ShapeDtype...  4.68 us
    ppermute x3, starting transfers between devices, tp_swapped(): return lax.ppermute(block, 'tp', [(0, 1), (1, 0)])  4.14 us
    pallas_call x2, Pallas kernels, project(): pl.pallas_call(partial(project_kernel, tile, pieces), out_shape=tuple((ja...  3.62 us
    unnamed x14, local copies, waits for them, and re-layouts  3.39 us
  transfers between devices with their start and end apart: 20, of which 11 were waited for; matrix products, arithmetic and copies ran while one was open for 0% of the time, Pallas kernels for 22%

profile of v3, /device:TPU:0, one launch (start us, length us, event | category | flops | bytes accessed | tf_op | source)
XLA Modules:
  0.0 70.3 jit_solution(5145165112946950411)
XLA Ops:
  0.6 3.0 %collective-permute-start.11 = (bf16[256,2048]{1,0:T(8,128)(2,1)}, bf16[256,2048]{1,0:T(8,128)(2,1)S(1)}, u32[]{:S(2)}, u32[]{:S(2)}) collective-permute-start(bf16[256,2048]{1,0:T(8,128)(2,1)} %refs_0_.1), channel_id=1, source_target_pairs={{0,1},{1,0},{2,3},{3,2},{4,5},{5,4},{6,7},{7,6},{8,9},{9,8},{10,11... | collective-permute-start | bytes 3145736 | tf_op jit(solution)/shard_map/ppermute | solution.py:39
  3.6 0.8 %copy-done.4 = bf16[256,128]{1,0:T(8,128)(2,1)S(1)} copy-done((bf16[256,128]{1,0:T(8,128)(2,1)S(1)}, bf16[256,128]{1,0:T(8,128)(2,1)}, u32[]{:S(2)}) %copy-start.4) | copy-done | bytes 65560
  4.5 0.8 %copy-done.5 = bf16[256,128]{1,0:T(8,128)(2,1)S(1)} copy-done((bf16[256,128]{1,0:T(8,128)(2,1)S(1)}, bf16[256,128]{1,0:T(8,128)(2,1)}, u32[]{:S(2)}) %copy-start.5) | copy-done | bytes 65560
  5.4 3.5 %collective-permute-start.7 = (bf16[2,256,128]{2,1,0:T(8,128)(2,1)S(1)}, bf16[2,256,128]{2,1,0:T(8,128)(2,1)S(1)}, u32[]{:S(2)}, u32[]{:S(2)}) collective-permute-start(bf16[2,256,128]{2,1,0:T(8,128)(2,1)S(1)} %pair_up.1.rest_0_), channel_id=1, source_target_pairs={{0,8},{2,10},{4,12},{6,14},{8,16},{10,18},{12,20},{14,22},{16,24},... | collective-permute-start | bytes 393224 | tf_op jit(solution)/shard_map/ppermute | solution.py:26
  8.9 4.5 %collective-permute-start = (bf16[2,256,128]{2,1,0:T(8,128)(2,1)S(1)}, bf16[2,256,128]{2,1,0:T(8,128)(2,1)S(1)}, u32[]{:S(2)}, u32[]{:S(2)}) collective-permute-start(bf16[2,256,128]{2,1,0:T(8,128)(2,1)S(1)} %pair_up.1.rest_0_), channel_id=1, source_target_pairs={{0,16},{2,18},{4,20},{6,22},{8,24},{10,26},{12,28},{14,30},{1,17},... | collective-permute-start | bytes 393224 | tf_op jit(solution)/shard_map/ppermute | solution.py:26
  13.4 1.6 %collective-permute-start.5 = (bf16[2,256,128]{2,1,0:T(8,128)(2,1)S(1)}, bf16[2,256,128]{2,1,0:T(8,128)(2,1)S(1)}, u32[]{:S(2)}, u32[]{:S(2)}) collective-permute-start(bf16[2,256,128]{2,1,0:T(8,128)(2,1)S(1)} %pair_up.1.rest_0_), channel_id=1, source_target_pairs={{0,4},{2,6},{4,0},{6,2},{8,12},{10,14},{12,8},{14,10},{16,20},{18,... | collective-permute-start | bytes 393224 | tf_op jit(solution)/shard_map/ppermute | solution.py:35
  15.5 1.0 %copy-done.2 = bf16[256,1024]{1,0:T(8,128)(2,1)S(1)} copy-done((bf16[256,1024]{1,0:T(8,128)(2,1)S(1)}, bf16[256,1024]{1,0:T(8,128)(2,1)}, u32[]{:S(2)}) %copy-start.2) | copy-done | bytes 524312
  16.5 0.7 copy-done.6
  17.2 1.2 %prepare.1 = (bf16[8,128,256]{2,1,0:T(8,128)(2,1)S(1)}, s32[8,256]{1,0:T(8,128)S(1)}, s32[2]{0:T(128)S(1)}) custom-call(s32[8]{0:T(128)S(1)} %copy-done.6, bf16[256,1024]{1,0:T(8,128)(2,1)S(1)} %copy-done.2), custom_call_target="tpu_custom_call" | custom-call | tf_op jit(solution)/shard_map/prepare/pallas_call | solution.py:371
  19.3 1.9 %collective-permute-done.9.rest_6_ = bf16[2,256,128]{2,1,0:T(8,128)(2,1)S(1)} collective-permute-done((bf16[2,256,128]{2,1,0:T(8,128)(2,1)S(1)}, bf16[2,256,128]{2,1,0:T(8,128)(2,1)S(1)}, u32[]{:S(2)}, u32[]{:S(2)}) %collective-permute-start.9) | collective-permute-done | bytes 131104 | tf_op jit(solution)/shard_map/ppermute | solution.py:35
  21.3 1.5 %collective-permute-start.2 = (bf16[2,256,128]{2,1,0:T(8,128)(2,1)S(1)}, bf16[2,256,128]{2,1,0:T(8,128)(2,1)S(1)}, u32[]{:S(2)}, u32[]{:S(2)}) collective-permute-start(bf16[2,256,128]{2,1,0:T(8,128)(2,1)S(1)} %collective-permute-done.rest_0_), channel_id=1, source_target_pairs={{0,4},{2,6},{4,0},{6,2},{8,12},{10,14},{12,8},{14,10},{16,20},{18,... | collective-permute-start | bytes 393224 | tf_op jit(solution)/shard_map/ppermute | solution.py:35
  23.4 1.7 %attend.2 = (f32[8,144,256]{2,1,0:T(8,128)S(1)}, f32[8,256]{1,0:T(8,128)S(1)}, bf16[12,2,256,128]{3,2,1,0:T(8,128)(2,1)S(1)}) custom-call(s32[2]{0:T(128)S(1)} %get-tuple-element.33.begin_ref, s32[8,256]{1,0:T(8,128)S(1)} %get-tuple-element.34.starts_ref, bf16[8,128,256]{2,1,0:T(8,128)(2,1)S(1)} %get-tuple-element.35.qt_ref, ...), custom_call_target="tpu_custom_call" | custom-call | flops 2147483648 | bytes 4194304 | tf_op jit(solution)/shard_map/attend/pallas_call | solution.py:345
  25.0 2.6 %collective-permute-done.2.rest_2_ = bf16[2,256,128]{2,1,0:T(8,128)(2,1)S(1)} collective-permute-done((bf16[2,256,128]{2,1,0:T(8,128)(2,1)S(1)}, bf16[2,256,128]{2,1,0:T(8,128)(2,1)S(1)}, u32[]{:S(2)}, u32[]{:S(2)}) %collective-permute-start.2) | collective-permute-done | bytes 131104 | tf_op jit(solution)/shard_map/ppermute | solution.py:35
  27.6 2.4 %collective-permute-done.3.rest_3_ = bf16[2,256,128]{2,1,0:T(8,128)(2,1)S(1)} collective-permute-done((bf16[2,256,128]{2,1,0:T(8,128)(2,1)S(1)}, bf16[2,256,128]{2,1,0:T(8,128)(2,1)S(1)}, u32[]{:S(2)}, u32[]{:S(2)}) %collective-permute-start.3) | collective-permute-done | bytes 131104 | tf_op jit(solution)/shard_map/ppermute | solution.py:35
  30.0 1.3 %attend.3 = (bf16[256,1024]{1,0:T(8,128)(2,1)S(1)}, f32[8,256]{1,0:T(8,128)S(1)}, bf16[12,2,256,128]{3,2,1,0:T(8,128)(2,1)S(1)}) custom-call(s32[2]{0:T(128)S(1)} %get-tuple-element.33.begin_ref, s32[8,256]{1,0:T(8,128)S(1)} %get-tuple-element.34.starts_ref, bf16[8,128,256]{2,1,0:T(8,128)(2,1)S(1)} %get-tuple-element.35.qt_ref, ...), custom_call_target="tpu_custom_call" | custom-call | flops 1073741824 | bytes 4194304 | tf_op jit(solution)/shard_map/attend/pallas_call | solution.py:345
  31.4 1.3 %project.2 = (bf16[256,1280]{1,0:T(8,128)(2,1)S(1)}, bf16[256,768]{1,0:T(8,128)(2,1)S(1)}) custom-call(s32[1]{0:T(128)S(6)} %sub.3.half_ref, bf16[256,1024]{1,0:T(8,128)(2,1)S(1)} %get-tuple-element.40.att_ref, bf16[1024,4096]{1,0:T(8,128)(2,1)S(1)} %copy-done), custom_call_target="tpu_custom_call" | custom-call | flops 1073741824 | bytes 4194304 | tf_op jit(solution)/shard_map/project/pallas_call | solution.py:488
  32.7 0.6 collective-permute-start.12
  33.3 3.1 %attention_grad.1 = (bf16[256,1024]{1,0:T(8,128)(2,1)S(1)}, bf16[8,128,256]{2,1,0:T(8,128)(2,1)S(1)}) custom-call(s32[2]{0:T(128)S(1)} %pad_add_fusion.order_ref, bf16[256,2048]{1,0:T(8,128)(2,1)S(1)} %copy-done.1, bf16[256,2048]{1,0:T(8,128)(2,1)S(1)} %collective-permute-done.11.refs_1_, bf16[1024,4096]{1,0:T(8,128)(2,1)S(1)} %copy-done), custom_call_target="tpu_custom_call" | custom-call | flops 2147483648 | bytes 8388608 | tf_op jit(solution)/shard_map/attention_grad/pallas_call | solution.py:523
  36.4 4.7 %attend_back.1 = (bf16[256,1024]{1,0:T(8,128)(2,1)}, f32[6,2,128,256]{3,2,1,0:T(8,128)S(1)}, bf16[6,2,128,256]{3,2,1,0:T(8,128)(2,1)S(1)}) custom-call(s32[2]{0:T(128)S(1)} %get-tuple-element.33.begin_ref, s32[8,256]{1,0:T(8,128)S(1)} %get-tuple-element.34.starts_ref, bf16[256,1024]{1,0:T(8,128)(2,1)S(1)} %copy-done.3, ...), custom_call_target="tpu_custom_call" | custom-call | flops 6039797760 | bytes 8388608 | tf_op jit(solution)/shard_map/attend_back/pallas_call | solution.py:391
  41.0 8.1 %collective-permute-done.12.rest_0_ = bf16[256,1280]{1,0:T(8,128)(2,1)S(1)} collective-permute-done((bf16[256,1280]{1,0:T(8,128)(2,1)S(1)}, bf16[256,1280]{1,0:T(8,128)(2,1)S(1)}, u32[]{:S(2)}, u32[]{:S(2)}) %collective-permute-start.12) | collective-permute-done | bytes 655392 | tf_op jit(solution)/shard_map/ppermute | solution.py:39
  49.1 2.3 %collective-permute-done.14.received_ref = bf16[6,2,128,256]{3,2,1,0:T(8,128)(2,1)S(1)} collective-permute-done((bf16[6,2,128,256]{3,2,1,0:T(8,128)(2,1)S(1)}, bf16[6,2,128,256]{3,2,1,0:T(8,128)(2,1)S(1)}, u32[]{:S(2)}, u32[]{:S(2)}) %collective-permute-start.14) | collective-permute-done | bytes 786464 | tf_op jit(solution)/shard_map/ppermute | solution.py:35
  51.5 1.6 %collective-permute-start.18 = (bf16[2,128,256]{2,1,0:T(8,128)(2,1)S(1)}, bf16[2,128,256]{2,1,0:T(8,128)(2,1)S(1)}, u32[]{:S(2)}, u32[]{:S(2)}) collective-permute-start(bf16[2,128,256]{2,1,0:T(8,128)(2,1)S(1)} %get-tuple-element.58), channel_id=1, source_target_pairs={{0,4},{2,6},{4,0},{6,2},{8,12},{10,14},{12,8},{14,10},{16,20},{18,... | collective-permute-start | bytes 393224 | tf_op jit(solution)/shard_map/ppermute | solution.py:35
  53.6 0.5 collective-permute-start.13
  54.1 1.5 %collective-permute-start.15 = (bf16[2,128,256]{2,1,0:T(8,128)(2,1)S(1)}, bf16[2,128,256]{2,1,0:T(8,128)(2,1)S(1)}, u32[]{:S(2)}, u32[]{:S(2)}) collective-permute-start(bf16[2,128,256]{2,1,0:T(8,128)(2,1)S(1)} %get-tuple-element.60), channel_id=1, source_target_pairs={{0,4},{2,6},{4,0},{6,2},{8,12},{10,14},{12,8},{14,10},{16,20},{18,... | collective-permute-start | bytes 393224 | tf_op jit(solution)/shard_map/ppermute | solution.py:35
  55.6 2.2 %collective-permute-done.18 = bf16[2,128,256]{2,1,0:T(8,128)(2,1)S(1)} collective-permute-done((bf16[2,128,256]{2,1,0:T(8,128)(2,1)S(1)}, bf16[2,128,256]{2,1,0:T(8,128)(2,1)S(1)}, u32[]{:S(2)}, u32[]{:S(2)}) %collective-permute-start.18) | collective-permute-done | bytes 131104 | tf_op jit(solution)/shard_map/ppermute | solution.py:35
  57.9 2.8 %collective-permute-done.16 = bf16[2,128,256]{2,1,0:T(8,128)(2,1)S(1)} collective-permute-done((bf16[2,128,256]{2,1,0:T(8,128)(2,1)S(1)}, bf16[2,128,256]{2,1,0:T(8,128)(2,1)S(1)}, u32[]{:S(2)}, u32[]{:S(2)}) %collective-permute-start.16) | collective-permute-done | bytes 131104 | tf_op jit(solution)/shard_map/ppermute | solution.py:35
  60.8 2.8 %collective-permute-start.19 = (bf16[2,128,256]{2,1,0:T(8,128)(2,1)S(1)}, bf16[2,128,256]{2,1,0:T(8,128)(2,1)S(1)}, u32[]{:S(2)}, u32[]{:S(2)}) collective-permute-start(bf16[2,128,256]{2,1,0:T(8,128)(2,1)S(1)} %get-tuple-element.56), channel_id=1, source_target_pairs={{0,16},{2,18},{4,20},{6,22},{8,24},{10,26},{12,28},{14,30},{16,0},... | collective-permute-start | bytes 393224 | tf_op jit(solution)/shard_map/ppermute | solution.py:31
  63.6 0.6 collective-permute-done.13.rest_1_
  64.2 2.3 %project.3 = bf16[256,2048]{1,0:T(8,128)(2,1)} custom-call(s32[1]{0:T(128)} %bitcast.half_ref, bf16[256,1024]{1,0:T(8,128)(2,1)S(1)} %get-tuple-element.40.att_ref, bf16[1024,4096]{1,0:T(8,128)(2,1)S(1)} %copy-done, bf16[256,1280]{1,0:T(8,128)(2,1)S(1)} %collective-permute-done.12.rest_0_, bf16[256,768]{1,0:T(8,128)(2,1)S(1)} %collective-permute-done.13.rest_1_), custom_call_target="tpu_custom_call" | custom-call | flops 1073741824 | bytes 4194304 | tf_op jit(solution)/shard_map/project/pallas_call | solution.py:488
  66.5 2.3 %collective-permute-done.19.rest_2_ = bf16[2,128,256]{2,1,0:T(8,128)(2,1)S(1)} collective-permute-done((bf16[2,128,256]{2,1,0:T(8,128)(2,1)S(1)}, bf16[2,128,256]{2,1,0:T(8,128)(2,1)S(1)}, u32[]{:S(2)}, u32[]{:S(2)}) %collective-permute-start.19) | collective-permute-done | bytes 131104 | tf_op jit(solution)/shard_map/ppermute | solution.py:31
  68.8 0.7 collective-permute-done.17.rest_1_
  69.5 0.8 %finish.1 = (bf16[256,128]{1,0:T(8,128)(2,1)}, bf16[256,128]{1,0:T(8,128)(2,1)}) custom-call(f32[6,2,128,256]{3,2,1,0:T(8,128)S(1)} %get-tuple-element.52.keep_ref, bf16[6,2,128,256]{3,2,1,0:T(8,128)(2,1)S(1)} %collective-permute-done.14.received_ref, bf16[2,128,256]{2,1,0:T(8,128)(2,1)S(1)} %collective-permute-done.15.rest_0_, ...), custom_call_target="tpu_custom_call" | custom-call | tf_op jit(solution)/shard_map/finish/pallas_call | solution.py:453
  (34 shorter events, 2.8 us)
Async XLA Ops:
  0.6 32.6 %collective-permute-start.11 = (bf16[256,2048]{1,0:T(8,128)(2,1)}, bf16[256,2048]{1,0:T(8,128)(2,1)S(1)}, u32[]{:S(2)}, u32[]{:S(2)}) collective-permute-start(bf16[256,2048]{1,0:T(8,128)(2,1)} %refs_0_.1), channel_id=1, source_target_pairs={{0,1},{1,0},{2,3},{3,2},{4,5},{5,4},{6,7},{7,6},{8,9},{9,8},{10,11... | collective-permute-start | bytes 3145736 | tf_op jit(solution)/shard_map/ppermute | solution.py:39
  3.6 0.8 %copy-start.4 = (bf16[256,128]{1,0:T(8,128)(2,1)S(1)}, bf16[256,128]{1,0:T(8,128)(2,1)}, u32[]{:S(2)}) copy-start(bf16[256,128]{1,0:T(8,128)(2,1)} %keys_ref.1) | copy-start | bytes 196612
  4.5 0.8 %copy-start.5 = (bf16[256,128]{1,0:T(8,128)(2,1)S(1)}, bf16[256,128]{1,0:T(8,128)(2,1)}, u32[]{:S(2)}) copy-start(bf16[256,128]{1,0:T(8,128)(2,1)} %values_ref.1) | copy-start | bytes 196612
  5.4 9.6 %collective-permute-start.7 = (bf16[2,256,128]{2,1,0:T(8,128)(2,1)S(1)}, bf16[2,256,128]{2,1,0:T(8,128)(2,1)S(1)}, u32[]{:S(2)}, u32[]{:S(2)}) collective-permute-start(bf16[2,256,128]{2,1,0:T(8,128)(2,1)S(1)} %pair_up.1.rest_0_), channel_id=1, source_target_pairs={{0,8},{2,10},{4,12},{6,14},{8,16},{10,18},{12,20},{14,22},{16,24},... | collective-permute-start | bytes 393224 | tf_op jit(solution)/shard_map/ppermute | solution.py:26
  8.9 9.5 %collective-permute-start = (bf16[2,256,128]{2,1,0:T(8,128)(2,1)S(1)}, bf16[2,256,128]{2,1,0:T(8,128)(2,1)S(1)}, u32[]{:S(2)}, u32[]{:S(2)}) collective-permute-start(bf16[2,256,128]{2,1,0:T(8,128)(2,1)S(1)} %pair_up.1.rest_0_), channel_id=1, source_target_pairs={{0,16},{2,18},{4,20},{6,22},{8,24},{10,26},{12,28},{14,30},{1,17},... | collective-permute-start | bytes 393224 | tf_op jit(solution)/shard_map/ppermute | solution.py:26
  13.4 5.4 %collective-permute-start.5 = (bf16[2,256,128]{2,1,0:T(8,128)(2,1)S(1)}, bf16[2,256,128]{2,1,0:T(8,128)(2,1)S(1)}, u32[]{:S(2)}, u32[]{:S(2)}) collective-permute-start(bf16[2,256,128]{2,1,0:T(8,128)(2,1)S(1)} %pair_up.1.rest_0_), channel_id=1, source_target_pairs={{0,4},{2,6},{4,0},{6,2},{8,12},{10,14},{12,8},{14,10},{16,20},{18,... | collective-permute-start | bytes 393224 | tf_op jit(solution)/shard_map/ppermute | solution.py:35
  15.0 4.0 %collective-permute-start.4 = (bf16[2,256,128]{2,1,0:T(8,128)(2,1)S(1)}, bf16[2,256,128]{2,1,0:T(8,128)(2,1)S(1)}, u32[]{:S(2)}, u32[]{:S(2)}) collective-permute-start(bf16[2,256,128]{2,1,0:T(8,128)(2,1)S(1)} %pair_up.1.rest_0_), channel_id=1, source_target_pairs={{0,2},{2,0},{4,6},{6,4},{8,10},{10,8},{12,14},{14,12},{16,18},{18,... | collective-permute-start | bytes 393224 | tf_op jit(solution)/shard_map/ppermute | solution.py:35
  15.0 6.3 %collective-permute-start.9 = (bf16[2,256,128]{2,1,0:T(8,128)(2,1)S(1)}, bf16[2,256,128]{2,1,0:T(8,128)(2,1)S(1)}, u32[]{:S(2)}, u32[]{:S(2)}) collective-permute-start(bf16[2,256,128]{2,1,0:T(8,128)(2,1)S(1)} %collective-permute-done.7.rest_4_), channel_id=1, source_target_pairs={{0,4},{2,6},{4,0},{6,2},{8,12},{10,14},{12,8},{14,10},{16,20},{18,... | collective-permute-start | bytes 393224 | tf_op jit(solution)/shard_map/ppermute | solution.py:35
  15.5 1.0 %copy-start.2 = (bf16[256,1024]{1,0:T(8,128)(2,1)S(1)}, bf16[256,1024]{1,0:T(8,128)(2,1)}, u32[]{:S(2)}) copy-start(bf16[256,1024]{1,0:T(8,128)(2,1)} %q_ref.1) | copy-start | bytes 1572868
  16.5 0.7 copy-start.6
  18.4 2.9 %collective-permute-start.8 = (bf16[2,256,128]{2,1,0:T(8,128)(2,1)S(1)}, bf16[2,256,128]{2,1,0:T(8,128)(2,1)S(1)}, u32[]{:S(2)}, u32[]{:S(2)}) collective-permute-start(bf16[2,256,128]{2,1,0:T(8,128)(2,1)S(1)} %collective-permute-done.7.rest_4_), channel_id=1, source_target_pairs={{0,2},{2,0},{4,6},{6,4},{8,10},{10,8},{12,14},{14,12},{16,18},{18,... | collective-permute-start | bytes 393224 | tf_op jit(solution)/shard_map/ppermute | solution.py:35
  18.8 4.0 %collective-permute-start.1 = (bf16[2,256,128]{2,1,0:T(8,128)(2,1)S(1)}, bf16[2,256,128]{2,1,0:T(8,128)(2,1)S(1)}, u32[]{:S(2)}, u32[]{:S(2)}) collective-permute-start(bf16[2,256,128]{2,1,0:T(8,128)(2,1)S(1)} %collective-permute-done.rest_0_), channel_id=1, source_target_pairs={{0,2},{2,0},{4,6},{6,4},{8,10},{10,8},{12,14},{14,12},{16,18},{18,... | collective-permute-start | bytes 393224 | tf_op jit(solution)/shard_map/ppermute | solution.py:35
  19.0 4.3 %collective-permute-start.6 = (bf16[2,256,128]{2,1,0:T(8,128)(2,1)S(1)}, bf16[2,256,128]{2,1,0:T(8,128)(2,1)S(1)}, u32[]{:S(2)}, u32[]{:S(2)}) collective-permute-start(bf16[2,256,128]{2,1,0:T(8,128)(2,1)S(1)} %collective-permute-done.5.rest_2_), channel_id=1, source_target_pairs={{0,2},{2,0},{4,6},{6,4},{8,10},{10,8},{12,14},{14,12},{16,18},{18,... | collective-permute-start | bytes 393224 | tf_op jit(solution)/shard_map/ppermute | solution.py:35
  21.2 2.1 %collective-permute-start.10 = (bf16[2,256,128]{2,1,0:T(8,128)(2,1)S(1)}, bf16[2,256,128]{2,1,0:T(8,128)(2,1)S(1)}, u32[]{:S(2)}, u32[]{:S(2)}) collective-permute-start(bf16[2,256,128]{2,1,0:T(8,128)(2,1)S(1)} %collective-permute-done.9.rest_6_), channel_id=1, source_target_pairs={{0,2},{2,0},{4,6},{6,4},{8,10},{10,8},{12,14},{14,12},{16,18},{18,... | collective-permute-start | bytes 393224 | tf_op jit(solution)/shard_map/ppermute | solution.py:35
  21.3 6.3 %collective-permute-start.2 = (bf16[2,256,128]{2,1,0:T(8,128)(2,1)S(1)}, bf16[2,256,128]{2,1,0:T(8,128)(2,1)S(1)}, u32[]{:S(2)}, u32[]{:S(2)}) collective-permute-start(bf16[2,256,128]{2,1,0:T(8,128)(2,1)S(1)} %collective-permute-done.rest_0_), channel_id=1, source_target_pairs={{0,4},{2,6},{4,0},{6,2},{8,12},{10,14},{12,8},{14,10},{16,20},{18,... | collective-permute-start | bytes 393224 | tf_op jit(solution)/shard_map/ppermute | solution.py:35
  22.8 7.2 %collective-permute-start.3 = (bf16[2,256,128]{2,1,0:T(8,128)(2,1)S(1)}, bf16[2,256,128]{2,1,0:T(8,128)(2,1)S(1)}, u32[]{:S(2)}, u32[]{:S(2)}) collective-permute-start(bf16[2,256,128]{2,1,0:T(8,128)(2,1)S(1)} %collective-permute-done.1.rest_1_), channel_id=1, source_target_pairs={{0,4},{2,6},{4,0},{6,2},{8,12},{10,14},{12,8},{14,10},{16,20},{18,... | collective-permute-start | bytes 393224 | tf_op jit(solution)/shard_map/ppermute | solution.py:35
  23.4 8.0 %copy-start = (bf16[1024,4096]{1,0:T(8,128)(2,1)S(1)}, bf16[1024,4096]{1,0:T(8,128)(2,1)}, u32[]{:S(2)}) copy-start(bf16[1024,4096]{1,0:T(8,128)(2,1)} %weight_ref.3) | copy-start | bytes 25165828
  31.3 1.9 %copy-start.1 = (bf16[256,2048]{1,0:T(8,128)(2,1)S(1)}, bf16[256,2048]{1,0:T(8,128)(2,1)}, u32[]{:S(2)}) copy-start(bf16[256,2048]{1,0:T(8,128)(2,1)} %refs_0_.1) | copy-start | bytes 3145732
  32.7 16.4 %collective-permute-start.12 = (bf16[256,1280]{1,0:T(8,128)(2,1)S(1)}, bf16[256,1280]{1,0:T(8,128)(2,1)S(1)}, u32[]{:S(2)}, u32[]{:S(2)}) collective-permute-start(bf16[256,1280]{1,0:T(8,128)(2,1)S(1)} %get-tuple-element.42), channel_id=1, source_target_pairs={{0,1},{1,0},{2,3},{3,2},{4,5},{5,4},{6,7},{7,6},{8,9},{9,8},{10,11... | collective-permute-start | bytes 1966088 | tf_op jit(solution)/shard_map/ppermute | solution.py:39
  33.3 3.1 %copy-start.3 = (bf16[256,1024]{1,0:T(8,128)(2,1)S(1)}, bf16[256,1024]{1,0:T(8,128)(2,1)}, u32[]{:S(2)}) copy-start(bf16[256,1024]{1,0:T(8,128)(2,1)} %q_ref.1) | copy-start | bytes 1572868
  49.1 2.3 %collective-permute-start.14 = (bf16[6,2,128,256]{3,2,1,0:T(8,128)(2,1)S(1)}, bf16[6,2,128,256]{3,2,1,0:T(8,128)(2,1)S(1)}, u32[]{:S(2)}, u32[]{:S(2)}) collective-permute-start(bf16[6,2,128,256]{3,2,1,0:T(8,128)(2,1)S(1)} %get-tuple-element.53), channel_id=1, source_target_pairs={{0,2},{2,0},{4,6},{6,4},{8,10},{10,8},{12,14},{14,12},{16,18},{18,... | collective-permute-start | bytes 2359304 | tf_op jit(solution)/shard_map/ppermute | solution.py:35
  51.5 6.4 %collective-permute-start.18 = (bf16[2,128,256]{2,1,0:T(8,128)(2,1)S(1)}, bf16[2,128,256]{2,1,0:T(8,128)(2,1)S(1)}, u32[]{:S(2)}, u32[]{:S(2)}) collective-permute-start(bf16[2,128,256]{2,1,0:T(8,128)(2,1)S(1)} %get-tuple-element.58), channel_id=1, source_target_pairs={{0,4},{2,6},{4,0},{6,2},{8,12},{10,14},{12,8},{14,10},{16,20},{18,... | collective-permute-start | bytes 393224 | tf_op jit(solution)/shard_map/ppermute | solution.py:35
  53.1 7.6 %collective-permute-start.16 = (bf16[2,128,256]{2,1,0:T(8,128)(2,1)S(1)}, bf16[2,128,256]{2,1,0:T(8,128)(2,1)S(1)}, u32[]{:S(2)}, u32[]{:S(2)}) collective-permute-start(bf16[2,128,256]{2,1,0:T(8,128)(2,1)S(1)} %get-tuple-element.59), channel_id=1, source_target_pairs={{0,4},{2,6},{4,0},{6,2},{8,12},{10,14},{12,8},{14,10},{16,20},{18,... | collective-permute-start | bytes 393224 | tf_op jit(solution)/shard_map/ppermute | solution.py:35
  53.6 10.6 %collective-permute-start.13 = (bf16[256,768]{1,0:T(8,128)(2,1)S(1)}, bf16[256,768]{1,0:T(8,128)(2,1)S(1)}, u32[]{:S(2)}, u32[]{:S(2)}) collective-permute-start(bf16[256,768]{1,0:T(8,128)(2,1)S(1)} %get-tuple-element.50), channel_id=1, source_target_pairs={{0,1},{1,0},{2,3},{3,2},{4,5},{5,4},{6,7},{7,6},{8,9},{9,8},{10,11... | collective-permute-start | bytes 1179656 | tf_op jit(solution)/shard_map/ppermute | solution.py:39
  54.1 12.4 %collective-permute-start.15 = (bf16[2,128,256]{2,1,0:T(8,128)(2,1)S(1)}, bf16[2,128,256]{2,1,0:T(8,128)(2,1)S(1)}, u32[]{:S(2)}, u32[]{:S(2)}) collective-permute-start(bf16[2,128,256]{2,1,0:T(8,128)(2,1)S(1)} %get-tuple-element.60), channel_id=1, source_target_pairs={{0,4},{2,6},{4,0},{6,2},{8,12},{10,14},{12,8},{14,10},{16,20},{18,... | collective-permute-start | bytes 393224 | tf_op jit(solution)/shard_map/ppermute | solution.py:35
  60.8 8.0 %collective-permute-start.19 = (bf16[2,128,256]{2,1,0:T(8,128)(2,1)S(1)}, bf16[2,128,256]{2,1,0:T(8,128)(2,1)S(1)}, u32[]{:S(2)}, u32[]{:S(2)}) collective-permute-start(bf16[2,128,256]{2,1,0:T(8,128)(2,1)S(1)} %get-tuple-element.56), channel_id=1, source_target_pairs={{0,16},{2,18},{4,20},{6,22},{8,24},{10,26},{12,28},{14,30},{16,0},... | collective-permute-start | bytes 393224 | tf_op jit(solution)/shard_map/ppermute | solution.py:31
  63.6 5.9 %collective-permute-start.17 = (bf16[2,128,256]{2,1,0:T(8,128)(2,1)S(1)}, bf16[2,128,256]{2,1,0:T(8,128)(2,1)S(1)}, u32[]{:S(2)}, u32[]{:S(2)}) collective-permute-start(bf16[2,128,256]{2,1,0:T(8,128)(2,1)S(1)} %get-tuple-element.57), channel_id=1, source_target_pairs={{0,24},{2,26},{4,28},{6,30},{8,0},{10,2},{12,4},{14,6},{16,8},{18,... | collective-permute-start | bytes 393224 | tf_op jit(solution)/shard_map/ppermute | solution.py:31

commit v4 on v3

--- a/solution.py
+++ b/solution.py
@@ -572,9 +572,10 @@
     def core_sum(slots):
         return keep[slots] + received[slots].astype(jnp.float32)
 
-    crossed = {}
-    for plane in reversed(range(PLANES)):
-        crossed[plane] = swapped(core_sum(PLANES + plane).astype(jnp.bfloat16), 2)
+    crossing = [core_sum(PLANES + plane).astype(jnp.bfloat16) for plane in range(PLANES)]
+    crossed = [None] + [swapped(block, 2) for block in crossing[1:]]
+    crossed[1], crossing[0] = lax.optimization_barrier((crossed[1], crossing[0]))
+    crossed[0] = swapped(crossing[0], 2)
     arrived = []
     for plane in range(1, PLANES):
         half_sum = core_sum(plane) + crossed[plane].astype(jnp.float32)

time: 70.2 us -> 70.4 us (level)
  starting transfers between devices: 23.5 us -> 22.5 us
    ppermute x13, starting transfers between devices: 8.56 us -> 7.42 us  [swapped(): lax.ppermute(block, 'ctx', [(i, i ^ bit) for i in range(lax.axis_size('ct...]
    ppermute x13, waiting for transfers between devices: 14.3 us -> 15.1 us  [swapped(): lax.ppermute(block, 'ctx', [(i, i ^ bit) for i in range(lax.axis_size('ct...]
  transfers between devices with their start and end apart: 20 -> 20, of which waited for: 11 -> 10; matrix products, arithmetic and copies ran while one was open for 0% -> 0% of each run, Pallas kernels for 22% -> 22%
where the time goes in v4:
time: 70.4 us; the launch traced here: 69.8 us
  waiting for transfers between devices  26.5 us (38%)
  starting transfers between devices  22.5 us (32%)
  Pallas kernels  16.4 us (23%)
  local copies, waits for them, and re-layouts  3.39 us (5%)
  between operations  0.76 us (1%)
    ppermute x13, waiting for transfers between devices, swapped(): lax.ppermute(block, 'ctx', [(i, i ^ bit) for i in range(lax.axis_size('ct...  15.1 us
    ppermute x3, waiting for transfers between devices, tp_swapped(): return lax.ppermute(block, 'tp', [(0, 1), (1, 0)])  8.91 us
    ppermute x2, starting transfers between devices, sent_on(): lax.ppermute(block, 'ctx', [(i, i + distance) for i in range(size - dista...  7.99 us
    ppermute x13, starting transfers between devices, swapped(): lax.ppermute(block, 'ctx', [(i, i ^ bit) for i in range(lax.axis_size('ct...  7.42 us
    pallas_call x1, Pallas kernels, attend_back(): pl.pallas_call(partial(backward_kernel, heads), out_shape=(jax.ShapeDtype...  4.68 us
    ppermute x3, starting transfers between devices, tp_swapped(): return lax.ppermute(block, 'tp', [(0, 1), (1, 0)])  4.14 us
    pallas_call x2, Pallas kernels, project(): pl.pallas_call(partial(project_kernel, tile, pieces), out_shape=tuple((ja...  3.62 us
    unnamed x14, local copies, waits for them, and re-layouts  3.39 us
  transfers between devices with their start and end apart: 20, of which 10 were waited for; matrix products, arithmetic and copies ran while one was open for 0% of the time, Pallas kernels for 22%

profile of v4, /device:TPU:0, one launch (start us, length us, event | category | flops | bytes accessed | tf_op | source)
XLA Modules:
  0.0 69.8 jit_solution(6768046415003168254)
XLA Ops:
  0.6 3.0 %collective-permute-start.11 = (bf16[256,2048]{1,0:T(8,128)(2,1)}, bf16[256,2048]{1,0:T(8,128)(2,1)S(1)}, u32[]{:S(2)}, u32[]{:S(2)}) collective-permute-start(bf16[256,2048]{1,0:T(8,128)(2,1)} %refs_0_.1), channel_id=1, source_target_pairs={{0,1},{1,0},{2,3},{3,2},{4,5},{5,4},{6,7},{7,6},{8,9},{9,8},{10,11... | collective-permute-start | bytes 3145736 | tf_op jit(solution)/shard_map/ppermute | solution.py:39
  3.6 0.8 %copy-done.4 = bf16[256,128]{1,0:T(8,128)(2,1)S(1)} copy-done((bf16[256,128]{1,0:T(8,128)(2,1)S(1)}, bf16[256,128]{1,0:T(8,128)(2,1)}, u32[]{:S(2)}) %copy-start.4) | copy-done | bytes 65560
  4.5 0.8 %copy-done.5 = bf16[256,128]{1,0:T(8,128)(2,1)S(1)} copy-done((bf16[256,128]{1,0:T(8,128)(2,1)S(1)}, bf16[256,128]{1,0:T(8,128)(2,1)}, u32[]{:S(2)}) %copy-start.5) | copy-done | bytes 65560
  5.4 3.5 %collective-permute-start.7 = (bf16[2,256,128]{2,1,0:T(8,128)(2,1)S(1)}, bf16[2,256,128]{2,1,0:T(8,128)(2,1)S(1)}, u32[]{:S(2)}, u32[]{:S(2)}) collective-permute-start(bf16[2,256,128]{2,1,0:T(8,128)(2,1)S(1)} %pair_up.1.rest_0_), channel_id=1, source_target_pairs={{0,8},{2,10},{4,12},{6,14},{8,16},{10,18},{12,20},{14,22},{16,24},... | collective-permute-start | bytes 393224 | tf_op jit(solution)/shard_map/ppermute | solution.py:26
  8.9 4.5 %collective-permute-start = (bf16[2,256,128]{2,1,0:T(8,128)(2,1)S(1)}, bf16[2,256,128]{2,1,0:T(8,128)(2,1)S(1)}, u32[]{:S(2)}, u32[]{:S(2)}) collective-permute-start(bf16[2,256,128]{2,1,0:T(8,128)(2,1)S(1)} %pair_up.1.rest_0_), channel_id=1, source_target_pairs={{0,16},{2,18},{4,20},{6,22},{8,24},{10,26},{12,28},{14,30},{1,17},... | collective-permute-start | bytes 393224 | tf_op jit(solution)/shard_map/ppermute | solution.py:26
  13.4 1.6 %collective-permute-start.5 = (bf16[2,256,128]{2,1,0:T(8,128)(2,1)S(1)}, bf16[2,256,128]{2,1,0:T(8,128)(2,1)S(1)}, u32[]{:S(2)}, u32[]{:S(2)}) collective-permute-start(bf16[2,256,128]{2,1,0:T(8,128)(2,1)S(1)} %pair_up.1.rest_0_), channel_id=1, source_target_pairs={{0,4},{2,6},{4,0},{6,2},{8,12},{10,14},{12,8},{14,10},{16,20},{18,... | collective-permute-start | bytes 393224 | tf_op jit(solution)/shard_map/ppermute | solution.py:35
  15.0 0.5 collective-permute-start.9
  15.5 1.0 %copy-done.2 = bf16[256,1024]{1,0:T(8,128)(2,1)S(1)} copy-done((bf16[256,1024]{1,0:T(8,128)(2,1)S(1)}, bf16[256,1024]{1,0:T(8,128)(2,1)}, u32[]{:S(2)}) %copy-start.2) | copy-done | bytes 524312
  16.5 0.7 copy-done.6
  17.2 1.2 %prepare.1 = (bf16[8,128,256]{2,1,0:T(8,128)(2,1)S(1)}, s32[8,256]{1,0:T(8,128)S(1)}, s32[2]{0:T(128)S(1)}) custom-call(s32[8]{0:T(128)S(1)} %copy-done.6, bf16[256,1024]{1,0:T(8,128)(2,1)S(1)} %copy-done.2), custom_call_target="tpu_custom_call" | custom-call | tf_op jit(solution)/shard_map/prepare/pallas_call | solution.py:371
  19.3 1.9 %collective-permute-done.9.rest_6_ = bf16[2,256,128]{2,1,0:T(8,128)(2,1)S(1)} collective-permute-done((bf16[2,256,128]{2,1,0:T(8,128)(2,1)S(1)}, bf16[2,256,128]{2,1,0:T(8,128)(2,1)S(1)}, u32[]{:S(2)}, u32[]{:S(2)}) %collective-permute-start.9) | collective-permute-done | bytes 131104 | tf_op jit(solution)/shard_map/ppermute | solution.py:35
  21.3 1.5 %collective-permute-start.2 = (bf16[2,256,128]{2,1,0:T(8,128)(2,1)S(1)}, bf16[2,256,128]{2,1,0:T(8,128)(2,1)S(1)}, u32[]{:S(2)}, u32[]{:S(2)}) collective-permute-start(bf16[2,256,128]{2,1,0:T(8,128)(2,1)S(1)} %collective-permute-done.rest_0_), channel_id=1, source_target_pairs={{0,4},{2,6},{4,0},{6,2},{8,12},{10,14},{12,8},{14,10},{16,20},{18,... | collective-permute-start | bytes 393224 | tf_op jit(solution)/shard_map/ppermute | solution.py:35
  22.8 0.5 collective-permute-start.3
  23.4 1.7 %attend.2 = (f32[8,144,256]{2,1,0:T(8,128)S(1)}, f32[8,256]{1,0:T(8,128)S(1)}, bf16[12,2,256,128]{3,2,1,0:T(8,128)(2,1)S(1)}) custom-call(s32[2]{0:T(128)S(1)} %get-tuple-element.35.begin_ref, s32[8,256]{1,0:T(8,128)S(1)} %get-tuple-element.36.starts_ref, bf16[8,128,256]{2,1,0:T(8,128)(2,1)S(1)} %get-tuple-element.37.qt_ref, ...), custom_call_target="tpu_custom_call" | custom-call | flops 2147483648 | bytes 4194304 | tf_op jit(solution)/shard_map/attend/pallas_call | solution.py:345
  25.0 2.6 %collective-permute-done.2.rest_2_ = bf16[2,256,128]{2,1,0:T(8,128)(2,1)S(1)} collective-permute-done((bf16[2,256,128]{2,1,0:T(8,128)(2,1)S(1)}, bf16[2,256,128]{2,1,0:T(8,128)(2,1)S(1)}, u32[]{:S(2)}, u32[]{:S(2)}) %collective-permute-start.2) | collective-permute-done | bytes 131104 | tf_op jit(solution)/shard_map/ppermute | solution.py:35
  27.6 2.4 %collective-permute-done.3.rest_3_ = bf16[2,256,128]{2,1,0:T(8,128)(2,1)S(1)} collective-permute-done((bf16[2,256,128]{2,1,0:T(8,128)(2,1)S(1)}, bf16[2,256,128]{2,1,0:T(8,128)(2,1)S(1)}, u32[]{:S(2)}, u32[]{:S(2)}) %collective-permute-start.3) | collective-permute-done | bytes 131104 | tf_op jit(solution)/shard_map/ppermute | solution.py:35
  30.0 1.3 %attend.3 = (bf16[256,1024]{1,0:T(8,128)(2,1)S(1)}, f32[8,256]{1,0:T(8,128)S(1)}, bf16[12,2,256,128]{3,2,1,0:T(8,128)(2,1)S(1)}) custom-call(s32[2]{0:T(128)S(1)} %get-tuple-element.35.begin_ref, s32[8,256]{1,0:T(8,128)S(1)} %get-tuple-element.36.starts_ref, bf16[8,128,256]{2,1,0:T(8,128)(2,1)S(1)} %get-tuple-element.37.qt_ref, ...), custom_call_target="tpu_custom_call" | custom-call | flops 1073741824 | bytes 4194304 | tf_op jit(solution)/shard_map/attend/pallas_call | solution.py:345
  31.4 1.3 %project.2 = (bf16[256,1280]{1,0:T(8,128)(2,1)S(1)}, bf16[256,768]{1,0:T(8,128)(2,1)S(1)}) custom-call(s32[1]{0:T(128)S(6)} %sub.3.half_ref, bf16[256,1024]{1,0:T(8,128)(2,1)S(1)} %get-tuple-element.42.att_ref, bf16[1024,4096]{1,0:T(8,128)(2,1)S(1)} %copy-done), custom_call_target="tpu_custom_call" | custom-call | flops 1073741824 | bytes 4194304 | tf_op jit(solution)/shard_map/project/pallas_call | solution.py:488
  32.7 0.6 collective-permute-start.12
  33.3 3.1 %attention_grad.1 = (bf16[256,1024]{1,0:T(8,128)(2,1)S(1)}, bf16[8,128,256]{2,1,0:T(8,128)(2,1)S(1)}) custom-call(s32[2]{0:T(128)S(1)} %pad_add_fusion.order_ref, bf16[256,2048]{1,0:T(8,128)(2,1)S(1)} %copy-done.1, bf16[256,2048]{1,0:T(8,128)(2,1)S(1)} %collective-permute-done.11.refs_1_, bf16[1024,4096]{1,0:T(8,128)(2,1)S(1)} %copy-done), custom_call_target="tpu_custom_call" | custom-call | flops 2147483648 | bytes 8388608 | tf_op jit(solution)/shard_map/attention_grad/pallas_call | solution.py:523
  36.4 4.7 %attend_back.1 = (bf16[256,1024]{1,0:T(8,128)(2,1)}, f32[6,2,128,256]{3,2,1,0:T(8,128)S(1)}, bf16[6,2,128,256]{3,2,1,0:T(8,128)(2,1)S(1)}) custom-call(s32[2]{0:T(128)S(1)} %get-tuple-element.35.begin_ref, s32[8,256]{1,0:T(8,128)S(1)} %get-tuple-element.36.starts_ref, bf16[256,1024]{1,0:T(8,128)(2,1)S(1)} %copy-done.3, ...), custom_call_target="tpu_custom_call" | custom-call | flops 6039797760 | bytes 8388608 | tf_op jit(solution)/shard_map/attend_back/pallas_call | solution.py:391
  41.0 8.1 %collective-permute-done.12.rest_0_ = bf16[256,1280]{1,0:T(8,128)(2,1)S(1)} collective-permute-done((bf16[256,1280]{1,0:T(8,128)(2,1)S(1)}, bf16[256,1280]{1,0:T(8,128)(2,1)S(1)}, u32[]{:S(2)}, u32[]{:S(2)}) %collective-permute-start.12) | collective-permute-done | bytes 655392 | tf_op jit(solution)/shard_map/ppermute | solution.py:39
  49.1 2.3 %collective-permute-done.14.received_ref = bf16[6,2,128,256]{3,2,1,0:T(8,128)(2,1)S(1)} collective-permute-done((bf16[6,2,128,256]{3,2,1,0:T(8,128)(2,1)S(1)}, bf16[6,2,128,256]{3,2,1,0:T(8,128)(2,1)S(1)}, u32[]{:S(2)}, u32[]{:S(2)}) %collective-permute-start.14) | collective-permute-done | bytes 786464 | tf_op jit(solution)/shard_map/ppermute | solution.py:35
  51.5 1.6 %collective-permute-start.15 = (bf16[2,128,256]{2,1,0:T(8,128)(2,1)S(1)}, bf16[2,128,256]{2,1,0:T(8,128)(2,1)S(1)}, u32[]{:S(2)}, u32[]{:S(2)}) collective-permute-start(bf16[2,128,256]{2,1,0:T(8,128)(2,1)S(1)} %get-tuple-element.64), channel_id=1, source_target_pairs={{0,4},{2,6},{4,0},{6,2},{8,12},{10,14},{12,8},{14,10},{16,20},{18,... | collective-permute-start | bytes 393224 | tf_op jit(solution)/shard_map/ppermute | solution.py:35
  53.6 0.5 collective-permute-start.13
  54.1 3.8 %collective-permute-done.15 = bf16[2,128,256]{2,1,0:T(8,128)(2,1)S(1)} collective-permute-done((bf16[2,128,256]{2,1,0:T(8,128)(2,1)S(1)}, bf16[2,128,256]{2,1,0:T(8,128)(2,1)S(1)}, u32[]{:S(2)}, u32[]{:S(2)}) %collective-permute-start.15) | collective-permute-done | bytes 131104 | tf_op jit(solution)/shard_map/ppermute | solution.py:35
  57.9 2.0 %collective-permute-done.18 = bf16[2,128,256]{2,1,0:T(8,128)(2,1)S(1)} collective-permute-done((bf16[2,128,256]{2,1,0:T(8,128)(2,1)S(1)}, bf16[2,128,256]{2,1,0:T(8,128)(2,1)S(1)}, u32[]{:S(2)}, u32[]{:S(2)}) %collective-permute-start.18) | collective-permute-done | bytes 131104 | tf_op jit(solution)/shard_map/ppermute | solution.py:35
  60.1 2.9 %collective-permute-start.17 = (bf16[2,128,256]{2,1,0:T(8,128)(2,1)S(1)}, bf16[2,128,256]{2,1,0:T(8,128)(2,1)S(1)}, u32[]{:S(2)}, u32[]{:S(2)}) collective-permute-start(bf16[2,128,256]{2,1,0:T(8,128)(2,1)S(1)} %get-tuple-element.61), channel_id=1, source_target_pairs={{0,24},{2,26},{4,28},{6,30},{8,0},{10,2},{12,4},{14,6},{16,8},{18,... | collective-permute-start | bytes 393224 | tf_op jit(solution)/shard_map/ppermute | solution.py:31
  63.3 0.9 %collective-permute-done.13.rest_1_ = bf16[256,768]{1,0:T(8,128)(2,1)S(1)} collective-permute-done((bf16[256,768]{1,0:T(8,128)(2,1)S(1)}, bf16[256,768]{1,0:T(8,128)(2,1)S(1)}, u32[]{:S(2)}, u32[]{:S(2)}) %collective-permute-start.13) | collective-permute-done | bytes 393248 | tf_op jit(solution)/shard_map/ppermute | solution.py:39
  64.2 2.3 %project.3 = bf16[256,2048]{1,0:T(8,128)(2,1)} custom-call(s32[1]{0:T(128)} %bitcast.half_ref, bf16[256,1024]{1,0:T(8,128)(2,1)S(1)} %get-tuple-element.42.att_ref, bf16[1024,4096]{1,0:T(8,128)(2,1)S(1)} %copy-done, bf16[256,1280]{1,0:T(8,128)(2,1)S(1)} %collective-permute-done.12.rest_0_, bf16[256,768]{1,0:T(8,128)(2,1)S(1)} %collective-permute-done.13.rest_1_), custom_call_target="tpu_custom_call" | custom-call | flops 1073741824 | bytes 4194304 | tf_op jit(solution)/shard_map/project/pallas_call | solution.py:488
  66.5 2.5 %collective-permute-done.19.rest_2_ = bf16[2,128,256]{2,1,0:T(8,128)(2,1)S(1)} collective-permute-done((bf16[2,128,256]{2,1,0:T(8,128)(2,1)S(1)}, bf16[2,128,256]{2,1,0:T(8,128)(2,1)S(1)}, u32[]{:S(2)}, u32[]{:S(2)}) %collective-permute-start.19) | collective-permute-done | bytes 131104 | tf_op jit(solution)/shard_map/ppermute | solution.py:31
  69.0 0.8 %finish.1 = (bf16[256,128]{1,0:T(8,128)(2,1)}, bf16[256,128]{1,0:T(8,128)(2,1)}) custom-call(f32[6,2,128,256]{3,2,1,0:T(8,128)S(1)} %get-tuple-element.54.keep_ref, bf16[6,2,128,256]{3,2,1,0:T(8,128)(2,1)S(1)} %collective-permute-done.14.received_ref, bf16[2,128,256]{2,1,0:T(8,128)(2,1)S(1)} %collective-permute-done.16.rest_0_, ...), custom_call_target="tpu_custom_call" | custom-call | tf_op jit(solution)/shard_map/finish/pallas_call | solution.py:453
  (34 shorter events, 2.2 us)
Async XLA Ops:
  0.6 32.6 %collective-permute-start.11 = (bf16[256,2048]{1,0:T(8,128)(2,1)}, bf16[256,2048]{1,0:T(8,128)(2,1)S(1)}, u32[]{:S(2)}, u32[]{:S(2)}) collective-permute-start(bf16[256,2048]{1,0:T(8,128)(2,1)} %refs_0_.1), channel_id=1, source_target_pairs={{0,1},{1,0},{2,3},{3,2},{4,5},{5,4},{6,7},{7,6},{8,9},{9,8},{10,11... | collective-permute-start | bytes 3145736 | tf_op jit(solution)/shard_map/ppermute | solution.py:39
  3.6 0.8 %copy-start.4 = (bf16[256,128]{1,0:T(8,128)(2,1)S(1)}, bf16[256,128]{1,0:T(8,128)(2,1)}, u32[]{:S(2)}) copy-start(bf16[256,128]{1,0:T(8,128)(2,1)} %keys_ref.1) | copy-start | bytes 196612
  4.5 0.8 %copy-start.5 = (bf16[256,128]{1,0:T(8,128)(2,1)S(1)}, bf16[256,128]{1,0:T(8,128)(2,1)}, u32[]{:S(2)}) copy-start(bf16[256,128]{1,0:T(8,128)(2,1)} %values_ref.1) | copy-start | bytes 196612
  5.4 9.6 %collective-permute-start.7 = (bf16[2,256,128]{2,1,0:T(8,128)(2,1)S(1)}, bf16[2,256,128]{2,1,0:T(8,128)(2,1)S(1)}, u32[]{:S(2)}, u32[]{:S(2)}) collective-permute-start(bf16[2,256,128]{2,1,0:T(8,128)(2,1)S(1)} %pair_up.1.rest_0_), channel_id=1, source_target_pairs={{0,8},{2,10},{4,12},{6,14},{8,16},{10,18},{12,20},{14,22},{16,24},... | collective-permute-start | bytes 393224 | tf_op jit(solution)/shard_map/ppermute | solution.py:26
  8.9 9.5 %collective-permute-start = (bf16[2,256,128]{2,1,0:T(8,128)(2,1)S(1)}, bf16[2,256,128]{2,1,0:T(8,128)(2,1)S(1)}, u32[]{:S(2)}, u32[]{:S(2)}) collective-permute-start(bf16[2,256,128]{2,1,0:T(8,128)(2,1)S(1)} %pair_up.1.rest_0_), channel_id=1, source_target_pairs={{0,16},{2,18},{4,20},{6,22},{8,24},{10,26},{12,28},{14,30},{1,17},... | collective-permute-start | bytes 393224 | tf_op jit(solution)/shard_map/ppermute | solution.py:26
  13.4 5.4 %collective-permute-start.5 = (bf16[2,256,128]{2,1,0:T(8,128)(2,1)S(1)}, bf16[2,256,128]{2,1,0:T(8,128)(2,1)S(1)}, u32[]{:S(2)}, u32[]{:S(2)}) collective-permute-start(bf16[2,256,128]{2,1,0:T(8,128)(2,1)S(1)} %pair_up.1.rest_0_), channel_id=1, source_target_pairs={{0,4},{2,6},{4,0},{6,2},{8,12},{10,14},{12,8},{14,10},{16,20},{18,... | collective-permute-start | bytes 393224 | tf_op jit(solution)/shard_map/ppermute | solution.py:35
  15.0 4.0 %collective-permute-start.4 = (bf16[2,256,128]{2,1,0:T(8,128)(2,1)S(1)}, bf16[2,256,128]{2,1,0:T(8,128)(2,1)S(1)}, u32[]{:S(2)}, u32[]{:S(2)}) collective-permute-start(bf16[2,256,128]{2,1,0:T(8,128)(2,1)S(1)} %pair_up.1.rest_0_), channel_id=1, source_target_pairs={{0,2},{2,0},{4,6},{6,4},{8,10},{10,8},{12,14},{14,12},{16,18},{18,... | collective-permute-start | bytes 393224 | tf_op jit(solution)/shard_map/ppermute | solution.py:35
  15.0 6.3 %collective-permute-start.9 = (bf16[2,256,128]{2,1,0:T(8,128)(2,1)S(1)}, bf16[2,256,128]{2,1,0:T(8,128)(2,1)S(1)}, u32[]{:S(2)}, u32[]{:S(2)}) collective-permute-start(bf16[2,256,128]{2,1,0:T(8,128)(2,1)S(1)} %collective-permute-done.7.rest_4_), channel_id=1, source_target_pairs={{0,4},{2,6},{4,0},{6,2},{8,12},{10,14},{12,8},{14,10},{16,20},{18,... | collective-permute-start | bytes 393224 | tf_op jit(solution)/shard_map/ppermute | solution.py:35
  15.5 1.0 %copy-start.2 = (bf16[256,1024]{1,0:T(8,128)(2,1)S(1)}, bf16[256,1024]{1,0:T(8,128)(2,1)}, u32[]{:S(2)}) copy-start(bf16[256,1024]{1,0:T(8,128)(2,1)} %q_ref.1) | copy-start | bytes 1572868
  16.5 0.7 copy-start.6
  18.4 2.9 %collective-permute-start.8 = (bf16[2,256,128]{2,1,0:T(8,128)(2,1)S(1)}, bf16[2,256,128]{2,1,0:T(8,128)(2,1)S(1)}, u32[]{:S(2)}, u32[]{:S(2)}) collective-permute-start(bf16[2,256,128]{2,1,0:T(8,128)(2,1)S(1)} %collective-permute-done.7.rest_4_), channel_id=1, source_target_pairs={{0,2},{2,0},{4,6},{6,4},{8,10},{10,8},{12,14},{14,12},{16,18},{18,... | collective-permute-start | bytes 393224 | tf_op jit(solution)/shard_map/ppermute | solution.py:35
  18.8 4.0 %collective-permute-start.1 = (bf16[2,256,128]{2,1,0:T(8,128)(2,1)S(1)}, bf16[2,256,128]{2,1,0:T(8,128)(2,1)S(1)}, u32[]{:S(2)}, u32[]{:S(2)}) collective-permute-start(bf16[2,256,128]{2,1,0:T(8,128)(2,1)S(1)} %collective-permute-done.rest_0_), channel_id=1, source_target_pairs={{0,2},{2,0},{4,6},{6,4},{8,10},{10,8},{12,14},{14,12},{16,18},{18,... | collective-permute-start | bytes 393224 | tf_op jit(solution)/shard_map/ppermute | solution.py:35
  19.0 4.3 %collective-permute-start.6 = (bf16[2,256,128]{2,1,0:T(8,128)(2,1)S(1)}, bf16[2,256,128]{2,1,0:T(8,128)(2,1)S(1)}, u32[]{:S(2)}, u32[]{:S(2)}) collective-permute-start(bf16[2,256,128]{2,1,0:T(8,128)(2,1)S(1)} %collective-permute-done.5.rest_2_), channel_id=1, source_target_pairs={{0,2},{2,0},{4,6},{6,4},{8,10},{10,8},{12,14},{14,12},{16,18},{18,... | collective-permute-start | bytes 393224 | tf_op jit(solution)/shard_map/ppermute | solution.py:35
  21.2 2.1 %collective-permute-start.10 = (bf16[2,256,128]{2,1,0:T(8,128)(2,1)S(1)}, bf16[2,256,128]{2,1,0:T(8,128)(2,1)S(1)}, u32[]{:S(2)}, u32[]{:S(2)}) collective-permute-start(bf16[2,256,128]{2,1,0:T(8,128)(2,1)S(1)} %collective-permute-done.9.rest_6_), channel_id=1, source_target_pairs={{0,2},{2,0},{4,6},{6,4},{8,10},{10,8},{12,14},{14,12},{16,18},{18,... | collective-permute-start | bytes 393224 | tf_op jit(solution)/shard_map/ppermute | solution.py:35
  21.3 6.3 %collective-permute-start.2 = (bf16[2,256,128]{2,1,0:T(8,128)(2,1)S(1)}, bf16[2,256,128]{2,1,0:T(8,128)(2,1)S(1)}, u32[]{:S(2)}, u32[]{:S(2)}) collective-permute-start(bf16[2,256,128]{2,1,0:T(8,128)(2,1)S(1)} %collective-permute-done.rest_0_), channel_id=1, source_target_pairs={{0,4},{2,6},{4,0},{6,2},{8,12},{10,14},{12,8},{14,10},{16,20},{18,... | collective-permute-start | bytes 393224 | tf_op jit(solution)/shard_map/ppermute | solution.py:35
  22.8 7.2 %collective-permute-start.3 = (bf16[2,256,128]{2,1,0:T(8,128)(2,1)S(1)}, bf16[2,256,128]{2,1,0:T(8,128)(2,1)S(1)}, u32[]{:S(2)}, u32[]{:S(2)}) collective-permute-start(bf16[2,256,128]{2,1,0:T(8,128)(2,1)S(1)} %collective-permute-done.1.rest_1_), channel_id=1, source_target_pairs={{0,4},{2,6},{4,0},{6,2},{8,12},{10,14},{12,8},{14,10},{16,20},{18,... | collective-permute-start | bytes 393224 | tf_op jit(solution)/shard_map/ppermute | solution.py:35
  23.4 8.0 %copy-start = (bf16[1024,4096]{1,0:T(8,128)(2,1)S(1)}, bf16[1024,4096]{1,0:T(8,128)(2,1)}, u32[]{:S(2)}) copy-start(bf16[1024,4096]{1,0:T(8,128)(2,1)} %weight_ref.3) | copy-start | bytes 25165828
  31.3 1.9 %copy-start.1 = (bf16[256,2048]{1,0:T(8,128)(2,1)S(1)}, bf16[256,2048]{1,0:T(8,128)(2,1)}, u32[]{:S(2)}) copy-start(bf16[256,2048]{1,0:T(8,128)(2,1)} %refs_0_.1) | copy-start | bytes 3145732
  32.7 16.4 %collective-permute-start.12 = (bf16[256,1280]{1,0:T(8,128)(2,1)S(1)}, bf16[256,1280]{1,0:T(8,128)(2,1)S(1)}, u32[]{:S(2)}, u32[]{:S(2)}) collective-permute-start(bf16[256,1280]{1,0:T(8,128)(2,1)S(1)} %get-tuple-element.44), channel_id=1, source_target_pairs={{0,1},{1,0},{2,3},{3,2},{4,5},{5,4},{6,7},{7,6},{8,9},{9,8},{10,11... | collective-permute-start | bytes 1966088 | tf_op jit(solution)/shard_map/ppermute | solution.py:39
  33.3 3.1 %copy-start.3 = (bf16[256,1024]{1,0:T(8,128)(2,1)S(1)}, bf16[256,1024]{1,0:T(8,128)(2,1)}, u32[]{:S(2)}) copy-start(bf16[256,1024]{1,0:T(8,128)(2,1)} %q_ref.1) | copy-start | bytes 1572868
  49.1 2.3 %collective-permute-start.14 = (bf16[6,2,128,256]{3,2,1,0:T(8,128)(2,1)S(1)}, bf16[6,2,128,256]{3,2,1,0:T(8,128)(2,1)S(1)}, u32[]{:S(2)}, u32[]{:S(2)}) collective-permute-start(bf16[6,2,128,256]{3,2,1,0:T(8,128)(2,1)S(1)} %get-tuple-element.55), channel_id=1, source_target_pairs={{0,2},{2,0},{4,6},{6,4},{8,10},{10,8},{12,14},{14,12},{16,18},{18,... | collective-permute-start | bytes 2359304 | tf_op jit(solution)/shard_map/ppermute | solution.py:35
  51.5 6.4 %collective-permute-start.15 = (bf16[2,128,256]{2,1,0:T(8,128)(2,1)S(1)}, bf16[2,128,256]{2,1,0:T(8,128)(2,1)S(1)}, u32[]{:S(2)}, u32[]{:S(2)}) collective-permute-start(bf16[2,128,256]{2,1,0:T(8,128)(2,1)S(1)} %get-tuple-element.64), channel_id=1, source_target_pairs={{0,4},{2,6},{4,0},{6,2},{8,12},{10,14},{12,8},{14,10},{16,20},{18,... | collective-permute-start | bytes 393224 | tf_op jit(solution)/shard_map/ppermute | solution.py:35
  53.1 6.8 %collective-permute-start.18 = (bf16[2,128,256]{2,1,0:T(8,128)(2,1)S(1)}, bf16[2,128,256]{2,1,0:T(8,128)(2,1)S(1)}, u32[]{:S(2)}, u32[]{:S(2)}) collective-permute-start(bf16[2,128,256]{2,1,0:T(8,128)(2,1)S(1)} %get-tuple-element.62), channel_id=1, source_target_pairs={{0,4},{2,6},{4,0},{6,2},{8,12},{10,14},{12,8},{14,10},{16,20},{18,... | collective-permute-start | bytes 393224 | tf_op jit(solution)/shard_map/ppermute | solution.py:35
  53.6 10.6 %collective-permute-start.13 = (bf16[256,768]{1,0:T(8,128)(2,1)S(1)}, bf16[256,768]{1,0:T(8,128)(2,1)S(1)}, u32[]{:S(2)}, u32[]{:S(2)}) collective-permute-start(bf16[256,768]{1,0:T(8,128)(2,1)S(1)} %get-tuple-element.52), channel_id=1, source_target_pairs={{0,1},{1,0},{2,3},{3,2},{4,5},{5,4},{6,7},{7,6},{8,9},{9,8},{10,11... | collective-permute-start | bytes 1179656 | tf_op jit(solution)/shard_map/ppermute | solution.py:39
  60.0 9.0 %collective-permute-start.19 = (bf16[2,128,256]{2,1,0:T(8,128)(2,1)S(1)}, bf16[2,128,256]{2,1,0:T(8,128)(2,1)S(1)}, u32[]{:S(2)}, u32[]{:S(2)}) collective-permute-start(bf16[2,128,256]{2,1,0:T(8,128)(2,1)S(1)} %get-tuple-element.60), channel_id=1, source_target_pairs={{0,16},{2,18},{4,20},{6,22},{8,24},{10,26},{12,28},{14,30},{16,0},... | collective-permute-start | bytes 393224 | tf_op jit(solution)/shard_map/ppermute | solution.py:31
  60.1 9.0 %collective-permute-start.17 = (bf16[2,128,256]{2,1,0:T(8,128)(2,1)S(1)}, bf16[2,128,256]{2,1,0:T(8,128)(2,1)S(1)}, u32[]{:S(2)}, u32[]{:S(2)}) collective-permute-start(bf16[2,128,256]{2,1,0:T(8,128)(2,1)S(1)} %get-tuple-element.61), channel_id=1, source_target_pairs={{0,24},{2,26},{4,28},{6,30},{8,0},{10,2},{12,4},{14,6},{16,8},{18,... | collective-permute-start | bytes 393224 | tf_op jit(solution)/shard_map/ppermute | solution.py:31
  62.9 6.1 %collective-permute-start.16 = (bf16[2,128,256]{2,1,0:T(8,128)(2,1)S(1)}, bf16[2,128,256]{2,1,0:T(8,128)(2,1)S(1)}, u32[]{:S(2)}, u32[]{:S(2)}) collective-permute-start(bf16[2,128,256]{2,1,0:T(8,128)(2,1)S(1)} %get-tuple-element.56), channel_id=1, source_target_pairs={{0,4},{2,6},{4,0},{6,2},{8,12},{10,14},{12,8},{14,10},{16,20},{18,... | collective-permute-start | bytes 393224 | tf_op jit(solution)/shard_map/ppermute | solution.py:35
